TPU v7x, 32 devices: a whole 2x2x4 slice. The times are simulated.
32 devices in a mesh: wide: 16 (over z, y, x), narrow: 2 (over core).
Axes of the slice: x: 2, y: 2, z: 4, core: 2. Of those that a mesh axis runs over, the one named last changes fastest.
Arguments:
- patches: bfloat16 [384, 4096], P('wide', 'narrow'), may hold values from -6 to 6
- patch_index: int32 [384], P('wide'), may hold values from 0 to 255, as said below
- pos_table: bfloat16 [256, 4096], P(None, 'narrow'), may hold values from -4 to 4
- ln_gain: float32 [4096], P('narrow'), may hold values from 0.1 to 1.9
- ln_bias: float32 [4096], P('narrow'), may hold values from -0.6 to 0.6
- w_up: bfloat16 [4096, 16384], P('narrow', 'wide'), may hold values from -0.09375 to 0.09375
- up_bias: float32 [16384], P('wide'), may hold values from -3 to 3
- w_down: bfloat16 [16384, 4096], P('wide', 'narrow'), may hold values from -0.046875 to 0.046875
- d_out: bfloat16 [384, 4096], P('wide', 'narrow'), may hold values from -6 to 6
Outputs:
- d_patches: bfloat16 [384, 4096], P('wide', 'narrow')
- d_pos: float32 [256, 4096], P(None, 'narrow')
- d_gain: float32 [4096], P('narrow')
- d_lnbias: float32 [4096], P('narrow')
- d_up: bfloat16 [4096, 16384], P('narrow', 'wide')
- d_upbias: float32 [16384], P('wide')
- d_down: bfloat16 [16384, 4096], P('wide', 'narrow')
- d_downbias: float32 [4096], P('narrow')
Inputs may be any that keep to these rules, and one draw needn't show every extreme that they name: `patch_index`: each aligned block of 64 tokens is one image: its patch positions are distinct, a random choice of 64 of the 256.
All inputs are finite; a program needn't handle non-finite values.
Results may differ from a plain program's by a relative error of at most 0.0062.
Values may be sent and summed in bfloat16 or wider, within the bound.
No kernel may reach another device: no remote copies, remote signals or barrier semaphores. Data moves between devices by JAX's collectives and lax.ppermute only.
A program may use at most 128 MiB of HBM per device.

v0:
```python
import jax
import jax.numpy as jnp
from jax import lax
from jax.sharding import PartitionSpec as P

D = 4096


EPS = 1e-06
INV_ROOT_TWO = 0.7071067811865476
INV_ROOT_TWO_PI = 0.3989422804014327


def gelu_parts(values):
    normal_cdf = 0.5 * (1.0 + jax.scipy.special.erf(values * INV_ROOT_TWO))
    normal_pdf = jnp.exp(-0.5 * values * values) * INV_ROOT_TWO_PI
    return (values * normal_cdf, normal_cdf + values * normal_pdf)


def hidden_grads(pre_part, back_part, up_bias):
    act_value, gelu_slope = gelu_parts(pre_part + up_bias)
    return (act_value.astype(jnp.bfloat16), (back_part * gelu_slope).astype(jnp.bfloat16))


def on_device(patches, patch_index, pos_table, ln_gain, ln_bias, w_up, up_bias, w_down, d_out):
    own_rows = patches.shape[0]
    table_rows = pos_table.shape[0]
    picked = lax.broadcasted_iota(jnp.int32, (own_rows, table_rows), 1) == patch_index[:, None]
    onehot = jnp.where(picked, 1.0, 0.0).astype(jnp.float32)
    pos_rows = jnp.dot(onehot.astype(jnp.bfloat16), pos_table, preferred_element_type=jnp.float32)
    layer_in = patches.astype(jnp.float32) + pos_rows
    first_sum, square_sum = lax.psum(
        (jnp.sum(layer_in, axis=1), jnp.sum(layer_in * layer_in, axis=1)), "narrow"
    )
    centre_mean = (first_sum / D)[:, None]
    variance = (square_sum / D)[:, None] - centre_mean * centre_mean
    inverse_std = lax.rsqrt(variance + EPS)
    normed = (layer_in - centre_mean) * inverse_std
    hidden_in = (normed * ln_gain + ln_bias).astype(jnp.bfloat16)
    hidden_panel, grad_panel = (
        lax.all_gather(hidden_in, "wide", axis=0, tiled=True),
        lax.all_gather(d_out, "wide", axis=0, tiled=True),
    )
    pre_part = jnp.dot(hidden_panel, w_up, preferred_element_type=jnp.float32)
    back_part = lax.dot_general(
        grad_panel, w_down, (((1,), (1,)), ((), ())), preferred_element_type=jnp.float32
    )
    pre_full, back_full = lax.psum((pre_part, back_part), "narrow")
    activation, d_hidden = hidden_grads(pre_full, back_full, up_bias)
    contract_rows = (((0,), (0,)), ((), ()))
    d_down = lax.dot_general(
        activation, grad_panel, contract_rows, preferred_element_type=jnp.float32
    ).astype(jnp.bfloat16)
    d_up = lax.dot_general(
        hidden_panel, d_hidden, contract_rows, preferred_element_type=jnp.float32
    ).astype(jnp.bfloat16)
    d_upbias = jnp.sum(d_hidden.astype(jnp.float32), axis=0)
    d_downbias = jnp.sum(grad_panel.astype(jnp.float32), axis=0)
    d_normout = lax.psum_scatter(
        lax.dot_general(
            d_hidden, w_up, (((1,), (1,)), ((), ())), preferred_element_type=jnp.float32
        ),
        "wide",
        scatter_dimension=0,
        tiled=True,
    )
    gain_term = jnp.sum(d_normout * normed, axis=0)
    bias_term = jnp.sum(d_normout, axis=0)
    scaled = d_normout * ln_gain
    scaled_sum, cross_sum = lax.psum(
        (jnp.sum(scaled, axis=1), jnp.sum(scaled * normed, axis=1)), "narrow"
    )
    d_layer = inverse_std * (scaled - (scaled_sum / D)[:, None] - normed * (cross_sum / D)[:, None])
    summed_grad = d_out.astype(jnp.float32) + d_layer
    d_patches = summed_grad.astype(jnp.bfloat16)
    pos_term = lax.dot_general(
        onehot,
        summed_grad,
        contract_rows,
        precision=lax.Precision.HIGHEST,
        preferred_element_type=jnp.float32,
    )
    d_pos, d_gain, d_lnbias = lax.psum((pos_term, gain_term, bias_term), "wide")
    return (d_patches, d_pos, d_gain, d_lnbias, d_up, d_upbias, d_down, d_downbias)


def solution(mesh):
    in_specs = (
        P("wide", "narrow"),
        P("wide"),
        P(None, "narrow"),
        P("narrow"),
        P("narrow"),
        P("narrow", "wide"),
        P("wide"),
        P("wide", "narrow"),
        P("wide", "narrow"),
    )
    out_specs = (
        P("wide", "narrow"),
        P(None, "narrow"),
        P("narrow"),
        P("narrow"),
        P("narrow", "wide"),
        P("wide"),
        P("wide", "narrow"),
        P("narrow"),
    )
    return jax.shard_map(
        on_device, mesh=mesh, in_specs=in_specs, out_specs=out_specs, check_vma=False
    )
```

profile of v0, /device:TPU:0, one launch (start us, length us, event | category | flops | bytes accessed | tf_op | source)
XLA Modules:
  0.0 447.2 jit_solution(456520345250579881)
XLA Ops:
  7.2 0.0 copy-start
  7.2 0.0 all-gather.5.cloned.1.call-start
  7.2 1.2 copy-done
  8.4 1.3 multiply_reduce_fusion.2
  9.7 2.6 all-reduce.2
  12.3 1.5 add_convert_fusion
  13.8 0.0 all-gather.5.cloned.1.call-update
  13.8 0.0 all-gather.3.cloned.1.call-start
  13.8 0.7 all-gather.3.cloned.1.call-update
  14.5 0.0 all-reduce.9.cloned.1.call-start
  14.6 59.8 %all-gather.5.cloned.1.call-done = bf16[384,2048]{1,0:T(8,128)(2,1)} async-done(((bf16[24,2048]{1,0:T(8,128)(2,1)}), bf16[384,2048]{1,0:T(8,128)(2,1)}) %all-gather.5.cloned.1.call-update) | async-done | bytes 1572880 | tf_op jit(solution)/shard_map/all_gather | solution.py:41
  74.4 5.6 %fusion.22 = f32[384,1024]{1,0:T(8,128)} fusion(bf16[384,2048]{1,0:T(8,128)(2,1)} %all-gather.5.cloned.1.call-done, bf16[2048,1024]{1,0:T(8,128)(2,1)} %param.14), kind=kOutput, calls=%fused_computation.42 | convolution fusion | flops 1610612736 | bytes 7340032 | tf_op jit(solution)/shard_map/dot_general | solution.py:44
  80.0 53.8 %all-gather.3.cloned.1.call-done = bf16[384,2048]{1,0:T(8,128)(2,1)} async-done(((bf16[24,2048]{1,0:T(8,128)(2,1)}), bf16[384,2048]{1,0:T(8,128)(2,1)}) %all-gather.3.cloned.1.call-update) | async-done | bytes 1572880 | tf_op jit(solution)/shard_map/all_gather | solution.py:42
  133.8 5.6 %fusion.21 = f32[384,1024]{1,0:T(8,128)} fusion(bf16[384,2048]{1,0:T(8,128)(2,1)} %all-gather.3.cloned.1.call-done, bf16[1024,2048]{1,0:T(8,128)(2,1)} %param.16), kind=kOutput, calls=%fused_computation.41 | convolution fusion | flops 1610612736 | bytes 7340032 | tf_op jit(solution)/shard_map/dot_general | solution.py:45
  139.4 0.0 copy-start.7
  139.4 0.0 all-reduce.9.cloned.1.call-update
  139.4 0.0 reduce-scatter.2.cloned.1.call-start
  139.5 22.1 %all-reduce.9.cloned.1.call-done = (f32[384,1024]{1,0:T(8,128)}, f32[384,1024]{1,0:T(8,128)}) async-done(((f32[384,1024]{1,0:T(8,128)}, f32[384,1024]{1,0:T(8,128)}), (f32[384,1024]{1,0:T(8,128)}, f32[384,1024]{1,0:T(8,128)})) %all-reduce.9.cloned.1.call-update) | async-done | bytes 3145744 | tf_op jit(solution)/shard_map/psum | solution.py:48
  161.6 0.0 copy-done.7
  161.6 3.2 convert_reduce_fusion.1
  164.8 0.0 copy-start.3
  164.8 0.9 copy-done.3
  165.7 5.7 %fusion.23 = f32[384,2048]{1,0:T(8,128)} fusion(bf16[384,1024]{1,0:T(8,128)(2,1)S(1)} %get-tuple-element.23, bf16[2048,1024]{1,0:T(8,128)(2,1)} %param.14), kind=kOutput, calls=%fused_computation.43 | convolution fusion | flops 1610612736 | bytes 8126464 | tf_op jit(solution)/shard_map/dot_general | solution.py:60
  171.4 0.0 copy-start.6
  171.4 0.0 copy-start.5
  171.4 0.0 copy-start.8
  171.4 0.0 reduce-scatter.2.cloned.1.call-update
  171.4 0.0 all-reduce.7.cloned.1.call-start
  171.5 131.8 %reduce-scatter.2.cloned.1.call-done = f32[24,2048]{1,0:T(8,128)} async-done(((f32[384,2048]{1,0:T(8,128)}), f32[24,2048]{1,0:T(8,128)}) %reduce-scatter.2.cloned.1.call-update) | async-done | bytes 196624 | tf_op jit(solution)/shard_map/reduce_scatter | solution.py:59
  303.3 0.0 copy-done.6
  303.3 1.2 multiply_reduce_fusion
  304.4 2.7 all-reduce.1
  307.1 0.0 copy-done.5
  307.1 1.7 fusion.20
  308.8 0.0 copy-done.8
  308.8 3.2 fusion.7
  312.0 0.0 copy-start.1
  312.0 0.0 all-reduce.7.cloned.1.call-update
  312.0 1.4 copy-done.1
  313.4 0.0 copy-start.4
  313.4 0.9 convert_reduce_fusion
  314.3 0.3 copy-done.4
  314.6 5.9 %convolution_convert_fusion.1 = bf16[2048,1024]{1,0:T(8,128)(2,1)} fusion(bf16[384,2048]{1,0:T(8,128)(2,1)} %all-gather.5.cloned.1.call-done, bf16[384,1024]{1,0:T(8,128)(2,1)S(1)} %copy-done.4), kind=kOutput, calls=%fused_computation.1 | convolution fusion | flops 1612709888 | bytes 6553600 | tf_op jit(solution)/shard_map/dot_general | solution.py:54
  320.5 0.0 copy-done.2
  320.5 4.5 convolution_convert_fusion
  324.9 75.5 %all-reduce = (f32[2048]{0:T(1024)}, f32[2048]{0:T(1024)}) all-reduce(f32[2048]{0:T(1024)S(1)} %get-tuple-element.8, f32[2048]{0:T(1024)S(1)} %get-tuple-element.11), channel_id=1, replica_groups=mesh['wide'=16,'narrow'=2] {'wide'}, use_global_device_ids=true, to_apply=%region_13.14 | all-reduce | flops 4096 | bytes 32768 | tf_op jit(solution)/shard_map/psum | solution.py:83
  400.5 37.1 %all-reduce.7.cloned.1.call-done = f32[256,2048]{1,0:T(8,128)} async-done(((f32[256,2048]{1,0:T(8,128)}), f32[256,2048]{1,0:T(8,128)}) %all-reduce.7.cloned.1.call-update) | async-done | bytes 2097168 | tf_op jit(solution)/shard_map/psum | solution.py:83
  437.5 3.1 copy.20
  (3 shorter events, 0.0 us)
Async XLA Ops:
  7.2 1.2 copy-start
  7.2 67.2 %all-gather.5.cloned.1.call-start = ((), (), s32[]{:S(2)}) async-start(), calls=%async_computation.2 | async-start | bytes 1671168 | tf_op jit(solution)/shard_map/all_gather | solution.py:41
  13.8 120.0 %all-gather.3.cloned.1.call-start = ((), (), s32[]{:S(2)}) async-start(), calls=%async_computation.1 | async-start | bytes 1671168 | tf_op jit(solution)/shard_map/all_gather | solution.py:42
  14.5 147.1 %all-reduce.9.cloned.1.call-start = ((), (), s32[]{:S(2)}) async-start(), calls=%async_computation.5 | async-start | bytes 6291456 | tf_op jit(solution)/shard_map/psum | solution.py:48
  139.4 22.2 %copy-start.7 = (f32[1024]{0:T(1024)S(1)}, f32[1024]{0:T(1024)}, u32[]{:S(2)}) copy-start(f32[1024]{0:T(1024)} %param.15) | copy-start | bytes 12292
  139.4 163.8 %reduce-scatter.2.cloned.1.call-start = ((), (), s32[]{:S(2)}) async-start(), calls=%async_computation.3 | async-start | bytes 3342336 | tf_op jit(solution)/shard_map/reduce_scatter | solution.py:59
  164.8 0.9 copy-start.3
  171.4 131.9 %copy-start.6 = (f32[2048]{0:T(1024)S(1)}, f32[2048]{0:T(1024)}, u32[]{:S(2)}) copy-start(f32[2048]{0:T(1024)} %param.12) | copy-start | bytes 24580
  171.4 135.7 %copy-start.5 = (bf16[24,2048]{1,0:T(8,128)(2,1)S(1)}, bf16[24,2048]{1,0:T(8,128)(2,1)}, u32[]{:S(2)}) copy-start(bf16[24,2048]{1,0:T(8,128)(2,1)} %param.17) | copy-start | bytes 294916
  171.4 137.4 %copy-start.8 = (s32[24]{0:T(128)S(1)}, s32[24]{0:T(128)}, u32[]{:S(2)}) copy-start(s32[24]{0:T(128)} %param.10) | copy-start | bytes 292
  171.4 266.1 %all-reduce.7.cloned.1.call-start = ((), (), s32[]{:S(2)}) async-start(), calls=%async_computation.4 | async-start | bytes 4194304 | tf_op jit(solution)/shard_map/psum | solution.py:83
  312.0 1.4 copy-start.1
  313.4 1.1 copy-start.4
  314.6 5.9 %copy-start.2 = (f32[384,1024]{1,0:T(8,128)S(1)}, f32[384,1024]{1,0:T(8,128)}, u32[]{:S(2)}) copy-start(f32[384,1024]{1,0:T(8,128)} %get-tuple-element.21) | copy-start | bytes 4718596
Sparse Core Ops, SparseCore 0:
  13.9 60.4 all-gather.4
  77.2 56.5 all-gather.2
  139.6 21.9 all-reduce.8
  171.5 131.6 reduce-scatter.1
  312.2 125.3 all-reduce.6
where the time goes:
time: 448 us; the launch traced here: 447 us
  waiting for transfers between devices  305 us (68%)
  blocking collectives  80.8 us (18%)
  matrix products  31.8 us (7%)
  between operations  13.8 us (3%)
  other arithmetic  8.41 us (2%)
  local copies, waits for them, and re-layouts  6.87 us (2%)
    reduce_scatter x1, waiting for transfers between devices, on_device(): lax.psum_scatter(lax.dot_general(d_hidden, w_up, (((1,), (1,)), ((), ()))...  132 us
    psum x1, blocking collectives, on_device(): d_pos, d_gain, d_lnbias = lax.psum((pos_term, gain_term, bias_term), 'wide')  75.5 us
    all_gather x1, waiting for transfers between devices, on_device(): lax.all_gather(hidden_in, 'wide', axis=0, tiled=True)  59.8 us
    all_gather x1, waiting for transfers between devices, on_device(): lax.all_gather(d_out, 'wide', axis=0, tiled=True)  53.8 us
    psum x1, waiting for transfers between devices, on_device(): d_pos, d_gain, d_lnbias = lax.psum((pos_term, gain_term, bias_term), 'wide')  37.1 us
    psum x1, waiting for transfers between devices, on_device(): pre_full, back_full = lax.psum((pre_part, back_part), 'narrow')  22.1 us
  transfers between devices with their start and end apart: 5, of which 5 were waited for; matrix products, arithmetic and copies ran while one was open for 4% of the time, Pallas kernels for 0%

commit v1 on v0

v1 whole, which is shorter than its diff:
```python
import jax
import jax.numpy as jnp
from jax import lax
from jax.sharding import PartitionSpec as P

D = 4096

EPS = 1e-06
INV_ROOT_TWO = 0.7071067811865476
INV_ROOT_TWO_PI = 0.3989422804014327
BF16 = jnp.bfloat16
F32 = jnp.float32


def gelu_parts(values):
    normal_cdf = 0.5 * (1.0 + jax.scipy.special.erf(values * INV_ROOT_TWO))
    normal_pdf = jnp.exp(-0.5 * values * values) * INV_ROOT_TWO_PI
    return (values * normal_cdf, normal_cdf + values * normal_pdf)


def program(wide, narrow):
    outer = wide // 4
    near = outer // 2

    def flip(x, bit):
        return lax.ppermute(x, "wide", [(i, i ^ bit) for i in range(wide)])

    def along_x(x):
        return flip(x, 1)

    def along_y(x):
        return flip(x, 2)

    def shift(x, k):
        return lax.ppermute(x, "wide", [(i, (i + 4 * k) % wide) for i in range(wide)])

    def other_core(x):
        return lax.ppermute(x, "narrow", [(0, 1), (1, 0)])

    def narrow_sum(x):
        if narrow == 2:
            return x.astype(F32) + other_core(x).astype(F32)
        return lax.psum(x.astype(F32), "narrow")

    def gather_outer(x):
        return [x] + [shift(x, k) for k in range(1, outer)]

    def gather_plane(blocks):
        low = jnp.concatenate(blocks[:near], axis=0)
        high = jnp.concatenate(blocks[near:], axis=0)
        low_x = along_x(low)
        high_y = along_y(high)
        low_y = along_y(low)
        high_x = along_x(high)
        low_xy = along_y(low_x)
        high_xy = along_x(high_y)
        return [low, high, low_x, high_x, low_y, high_y, low_xy, high_xy]

    def scatter_plane(low, high):
        low_far = along_y(low[3])
        high_far = along_x(high[3])
        low_y = along_y(low[2])
        high_x = along_x(high[1])
        low_x = along_x((low[1].astype(F32) + low_far.astype(F32)).astype(BF16))
        high_y = along_y((high[2].astype(F32) + high_far.astype(F32)).astype(BF16))
        low_sum = low[0].astype(F32) + low_y.astype(F32) + low_x.astype(F32)
        high_sum = high[0].astype(F32) + high_x.astype(F32) + high_y.astype(F32)
        return low_sum, high_sum

    def pair_sum(terms):
        while len(terms) > 1:
            half = len(terms) // 2
            terms = [terms[i] + terms[i + half] for i in range(half)]
        return terms[0]

    def on_device(patches, patch_index, pos_table, ln_gain, ln_bias, w_up, up_bias, w_down, d_out):
        rows, cols = patches.shape
        table_rows = pos_table.shape[0]
        grad_blocks = gather_outer(d_out)
        picked = lax.broadcasted_iota(jnp.int32, (rows, table_rows), 1) == patch_index[:, None]
        onehot = jnp.where(picked, 1.0, 0.0).astype(BF16)
        pos_rows = jnp.dot(onehot, pos_table, preferred_element_type=F32)
        layer_in = patches.astype(F32) + pos_rows
        sums = jnp.stack([jnp.sum(layer_in, axis=1), jnp.sum(layer_in * layer_in, axis=1)])
        first_sum, square_sum = narrow_sum(sums)
        centre_mean = (first_sum / D)[:, None]
        variance = (square_sum / D)[:, None] - centre_mean * centre_mean
        inverse_std = lax.rsqrt(variance + EPS)
        normed = (layer_in - centre_mean) * inverse_std
        hidden_in = (normed * ln_gain + ln_bias).astype(BF16)
        hidden_blocks = gather_outer(hidden_in)
        grad_panel = jnp.concatenate(gather_plane(grad_blocks), axis=0)
        hidden_panel = jnp.concatenate(gather_plane(hidden_blocks), axis=0)
        back_part = lax.dot_general(
            grad_panel, w_down, (((1,), (1,)), ((), ())), preferred_element_type=F32
        )
        pre_part = jnp.dot(hidden_panel, w_up, preferred_element_type=F32)
        back_full = narrow_sum(back_part.astype(BF16))
        pre_full = narrow_sum(pre_part.astype(BF16))
        act_value, slope = gelu_parts(pre_full + up_bias)
        activation = act_value.astype(BF16)
        d_hidden = (back_full * slope).astype(BF16)
        d_normout = lax.dot_general(
            d_hidden, w_up, (((1,), (1,)), ((), ())), preferred_element_type=F32
        ).astype(BF16)
        size = near * rows
        parts = [d_normout[i * size : (i + 1) * size] for i in range(8)]
        low_sum, high_sum = scatter_plane(parts[0::2], parts[1::2])
        plane = [low_sum[i * rows : (i + 1) * rows] for i in range(near)]
        plane += [high_sum[i * rows : (i + 1) * rows] for i in range(outer - near)]
        back_home = [shift(plane[k].astype(BF16), outer - k).astype(F32) for k in range(1, outer)]
        own_sum = pair_sum([plane[0]] + back_home)

        contract_rows = (((0,), (0,)), ((), ()))
        d_down = lax.dot_general(
            activation, grad_panel, contract_rows, preferred_element_type=F32
        ).astype(BF16)
        d_up = lax.dot_general(
            hidden_panel, d_hidden, contract_rows, preferred_element_type=F32
        ).astype(BF16)
        d_upbias = jnp.sum(d_hidden.astype(F32), axis=0)
        d_downbias = jnp.sum(grad_panel.astype(F32), axis=0)

        scaled = own_sum * ln_gain
        row_sums = narrow_sum(jnp.stack([jnp.sum(scaled, axis=1), jnp.sum(scaled * normed, axis=1)]))
        scaled_sum, cross_sum = row_sums
        d_layer = inverse_std * (
            scaled - (scaled_sum / D)[:, None] - normed * (cross_sum / D)[:, None]
        )
        summed_grad = (d_out.astype(F32) + d_layer).astype(BF16)
        gain_term = jnp.sum(own_sum * normed, axis=0)
        bias_term = jnp.sum(own_sum, axis=0)
        index_row = jnp.pad(patch_index.astype(BF16), (0, cols - rows))
        small = jnp.stack([gain_term.astype(BF16), bias_term.astype(BF16), index_row])
        payload = jnp.concatenate([summed_grad, jnp.pad(small, ((0, 5), (0, 0)))], axis=0)
        blocks = gather_outer(payload)
        pos_panel = jnp.concatenate(gather_plane([b[:rows] for b in blocks]), axis=0)
        terms = pair_sum([b[rows : rows + 2].astype(F32) for b in blocks])
        indices = jnp.concatenate([b[rows + 2, :rows] for b in blocks])

        for along in (along_x, along_y):
            tokens = indices.shape[0]
            depth = -(-tokens // cols)
            listed = jnp.pad(indices, (0, depth * cols - tokens)).reshape(depth, cols)
            packed = jnp.concatenate([terms.astype(BF16), listed], axis=0)
            other = along(packed)
            terms = packed[:2].astype(F32) + other[:2].astype(F32)
            indices = jnp.concatenate([indices, other[2:].reshape(-1)[:tokens]])
        indices = indices.astype(jnp.int32)
        d_gain, d_lnbias = terms
        owners = lax.broadcasted_iota(jnp.int32, (table_rows, indices.shape[0]), 0) == indices[None, :]
        d_pos = jnp.dot(
            jnp.where(owners, 1.0, 0.0).astype(BF16), pos_panel, preferred_element_type=F32
        )
        return (summed_grad, d_pos, d_gain, d_lnbias, d_up, d_upbias, d_down, d_downbias)

    return on_device


def solution(mesh):
    in_specs = (
        P("wide", "narrow"),
        P("wide"),
        P(None, "narrow"),
        P("narrow"),
        P("narrow"),
        P("narrow", "wide"),
        P("wide"),
        P("wide", "narrow"),
        P("wide", "narrow"),
    )
    out_specs = (
        P("wide", "narrow"),
        P(None, "narrow"),
        P("narrow"),
        P("narrow"),
        P("narrow", "wide"),
        P("wide"),
        P("wide", "narrow"),
        P("narrow"),
    )
    return jax.shard_map(
        program(mesh.shape["wide"], mesh.shape["narrow"]),
        mesh=mesh,
        in_specs=in_specs,
        out_specs=out_specs,
        check_vma=False,
    )
```

time: 448 us -> 129 us (0.29)
  waiting for transfers between devices: 305 us -> 46.6 us
  blocking collectives: 80.8 us -> 0 us
  starting transfers between devices: 0.2 us -> 55.5 us
  matrix products: 31.8 us -> 17.7 us
  between operations: 13.8 us -> 1.21 us
    reduce_scatter x1 -> x0, waiting for transfers between devices: 132 us -> none  [on_device(): lax.psum_scatter(lax.dot_general(d_hidden, w_up, (((1,), (1,)), ((), ()))...]
    all_gather x2 -> x0, waiting for transfers between devices: 114 us -> none  [the longest x1 59.8 us: on_device(): lax.all_gather(hidden_in, 'wide', axis=0, tiled=True)]
    psum x3 -> x0, blocking collectives: 80.8 us -> none  [the longest x1 75.5 us: on_device(): d_pos, d_gain, d_lnbias = lax.psum((pos_term, gain_term, bias_term), 'wide')]
    psum x2 -> x0, waiting for transfers between devices: 59.2 us -> none  [the longest x1 37.1 us: on_device(): d_pos, d_gain, d_lnbias = lax.psum((pos_term, gain_term, bias_term), 'wide')]
    ppermute x0 -> x42, starting transfers between devices: none -> 55.5 us  [the longest x26 28.9 us: flip(): return lax.ppermute(x, 'wide', [(i, i ^ bit) for i in range(wide)])]
    ppermute x0 -> x42, waiting for transfers between devices: none -> 46.6 us  [the longest x26 36.5 us: flip(): return lax.ppermute(x, 'wide', [(i, i ^ bit) for i in range(wide)])]
    dot_general x3, matrix products: 10.1 us -> 5.14 us  [the longest x1 2.03 us: on_device(): jnp.dot(jnp.where(owners, 1.0, 0.0).astype(BF16), pos_panel, preferred_el...]
    unnamed x19 -> x37, local copies, waits for them, and re-layouts: 6.87 us -> 2.23 us
  transfers between devices with their start and end apart: 5 -> 42, of which waited for: 5 -> 18; matrix products, arithmetic and copies ran while one was open for 4% -> 15% of each run, Pallas kernels for 0% -> 0%
where the time goes in v1:
time: 129 us
  starting transfers between devices  55.5 us (43%)
  waiting for transfers between devices  46.6 us (36%)
  matrix products  17.7 us (14%)
  other arithmetic  4.25 us (3%)
  local copies, waits for them, and re-layouts  3.36 us (3%)
    ppermute x26, waiting for transfers between devices, flip(): return lax.ppermute(x, 'wide', [(i, i ^ bit) for i in range(wide)])  36.5 us
    ppermute x26, starting transfers between devices, flip(): return lax.ppermute(x, 'wide', [(i, i ^ bit) for i in range(wide)])  28.9 us
    ppermute x12, starting transfers between devices, shift(): lax.ppermute(x, 'wide', [(i, (i + 4 * k) % wide) for i in range(wide)])  26 us
    ppermute x12, waiting for transfers between devices, shift(): lax.ppermute(x, 'wide', [(i, (i + 4 * k) % wide) for i in range(wide)])  6.82 us
    dot_general x1, matrix products, on_device(): lax.dot_general(activation, grad_panel, contract_rows, preferred_element_...  4.54 us
    dot_general x1, matrix products, on_device(): lax.dot_general(hidden_panel, d_hidden, contract_rows, preferred_element_...  4.41 us
    ppermute x4, waiting for transfers between devices, other_core(): return lax.ppermute(x, 'narrow', [(0, 1), (1, 0)])  3.28 us
  transfers between devices with their start and end apart: 42, of which 18 were waited for; matrix products, arithmetic and copies ran while one was open for 15% of the time, Pallas kernels for 0%

profile of v1, /device:TPU:0, one launch (start us, length us, event | category | flops | bytes accessed | tf_op | source)
XLA Modules:
  0.0 128.6 jit_solution(67897927359699392)
XLA Ops:
  0.7 4.1 %collective-permute-start.2 = (bf16[24,2048]{1,0:T(8,128)(2,1)}, bf16[24,2048]{1,0:T(8,128)(2,1)S(1)}, u32[]{:S(2)}, u32[]{:S(2)}) collective-permute-start(bf16[24,2048]{1,0:T(8,128)(2,1)} %param.17), channel_id=1, source_target_pairs={{0,16},{2,18},{4,20},{6,22},{8,24},{10,26},{12,28},{14,30},{16,0},... | collective-permute-start | bytes 294920 | tf_op jit(solution)/shard_map/ppermute | solution.py:35
  4.8 1.6 %collective-permute-start.1 = (bf16[24,2048]{1,0:T(8,128)(2,1)}, bf16[24,2048]{1,0:T(8,128)(2,1)S(1)}, u32[]{:S(2)}, u32[]{:S(2)}) collective-permute-start(bf16[24,2048]{1,0:T(8,128)(2,1)} %param.17), channel_id=1, source_target_pairs={{0,8},{2,10},{4,12},{6,14},{8,16},{10,18},{12,20},{14,22},{16,24},... | collective-permute-start | bytes 294920 | tf_op jit(solution)/shard_map/ppermute | solution.py:35
  6.3 2.2 %collective-permute-start.3 = (bf16[24,2048]{1,0:T(8,128)(2,1)}, bf16[24,2048]{1,0:T(8,128)(2,1)S(1)}, u32[]{:S(2)}, u32[]{:S(2)}) collective-permute-start(bf16[24,2048]{1,0:T(8,128)(2,1)} %param.17), channel_id=1, source_target_pairs={{0,24},{2,26},{4,28},{6,30},{8,0},{10,2},{12,4},{14,6},{16,8},{18,... | collective-permute-start | bytes 294920 | tf_op jit(solution)/shard_map/ppermute | solution.py:35
  8.6 1.3 %fusion.35 = (f32[24]{0:T(128)S(1)}, f32[24]{0:T(128)S(1)}, f32[24,2048]{1,0:T(8,128)S(1)}) fusion(bf16[256,2048]{1,0:T(8,128)(2,1)S(1)} %copy-done, s32[24]{0:T(128)} %param.10, bf16[24,2048]{1,0:T(8,128)(2,1)} %param.9), kind=kOutput, calls=%fused_computation.123 | convolution fusion | flops 25429968 | bytes 1343776 | tf_op jit(solution)/shard_map/dot_general | solution.py:82
  10.0 0.9 constant_dynamic-update-slice_fusion.1
  11.4 1.2 collective-permute-start.12
  12.6 6.6 %collective-permute-start.11 = (bf16[24,2048]{1,0:T(8,128)(2,1)S(1)}, bf16[24,2048]{1,0:T(8,128)(2,1)S(1)}, u32[]{:S(2)}, u32[]{:S(2)}) collective-permute-start(bf16[24,2048]{1,0:T(8,128)(2,1)S(1)} %get-tuple-element.20), channel_id=1, source_target_pairs={{0,8},{2,10},{4,12},{6,14},{8,16},{10,18},{12,20},{14,22},{16,24},... | collective-permute-start | bytes 294920 | tf_op jit(solution)/shard_map/ppermute | solution.py:35
  19.3 1.6 %collective-permute-start.7 = (bf16[48,2048]{1,0:T(8,128)(2,1)S(1)}, bf16[48,2048]{1,0:T(8,128)(2,1)S(1)}, u32[]{:S(2)}, u32[]{:S(2)}) collective-permute-start(bf16[48,2048]{1,0:T(8,128)(2,1)S(1)} %get-tuple-element.35), channel_id=1, source_target_pairs={{0,4},{2,6},{4,0},{6,2},{8,12},{10,14},{12,8},{14,10},{16,20},{18,... | collective-permute-start | bytes 589832 | tf_op jit(solution)/shard_map/ppermute | solution.py:26
  20.9 1.5 %collective-permute-start.5 = (bf16[48,2048]{1,0:T(8,128)(2,1)S(1)}, bf16[48,2048]{1,0:T(8,128)(2,1)S(1)}, u32[]{:S(2)}, u32[]{:S(2)}) collective-permute-start(bf16[48,2048]{1,0:T(8,128)(2,1)S(1)} %get-tuple-element.35), channel_id=1, source_target_pairs={{0,2},{2,0},{4,6},{6,4},{8,10},{10,8},{12,14},{14,12},{16,18},{18,... | collective-permute-start | bytes 589832 | tf_op jit(solution)/shard_map/ppermute | solution.py:26
  23.0 1.6 %collective-permute-start.4 = (bf16[48,2048]{1,0:T(8,128)(2,1)S(1)}, bf16[48,2048]{1,0:T(8,128)(2,1)S(1)}, u32[]{:S(2)}, u32[]{:S(2)}) collective-permute-start(bf16[48,2048]{1,0:T(8,128)(2,1)S(1)} %get-tuple-element.39), channel_id=1, source_target_pairs={{0,2},{2,0},{4,6},{6,4},{8,10},{10,8},{12,14},{14,12},{16,18},{18,... | collective-permute-start | bytes 589832 | tf_op jit(solution)/shard_map/ppermute | solution.py:26
  24.6 1.2 collective-permute-start.17
  25.8 5.5 %collective-permute-done.4 = bf16[48,2048]{1,0:T(8,128)(2,1)S(1)} collective-permute-done((bf16[48,2048]{1,0:T(8,128)(2,1)S(1)}, bf16[48,2048]{1,0:T(8,128)(2,1)S(1)}, u32[]{:S(2)}, u32[]{:S(2)}) %collective-permute-start.4) | collective-permute-done | bytes 196640 | tf_op jit(solution)/shard_map/ppermute | solution.py:26
  31.3 1.5 %collective-permute-start.15 = (bf16[48,2048]{1,0:T(8,128)(2,1)S(1)}, bf16[48,2048]{1,0:T(8,128)(2,1)S(1)}, u32[]{:S(2)}, u32[]{:S(2)}) collective-permute-start(bf16[48,2048]{1,0:T(8,128)(2,1)S(1)} %get-tuple-element.43), channel_id=1, source_target_pairs={{0,2},{2,0},{4,6},{6,4},{8,10},{10,8},{12,14},{14,12},{16,18},{18,... | collective-permute-start | bytes 589832 | tf_op jit(solution)/shard_map/ppermute | solution.py:26
  34.0 1.5 %collective-permute-start.9 = (bf16[48,2048]{1,0:T(8,128)(2,1)S(1)}, bf16[48,2048]{1,0:T(8,128)(2,1)S(1)}, u32[]{:S(2)}, u32[]{:S(2)}) collective-permute-start(bf16[48,2048]{1,0:T(8,128)(2,1)S(1)} %collective-permute-done.7), channel_id=1, source_target_pairs={{0,2},{2,0},{4,6},{6,4},{8,10},{10,8},{12,14},{14,12},{16,18},{18,... | collective-permute-start | bytes 589832 | tf_op jit(solution)/shard_map/ppermute | solution.py:26
  35.5 7.7 %collective-permute-done.14 = bf16[48,2048]{1,0:T(8,128)(2,1)S(1)} collective-permute-done((bf16[48,2048]{1,0:T(8,128)(2,1)S(1)}, bf16[48,2048]{1,0:T(8,128)(2,1)S(1)}, u32[]{:S(2)}, u32[]{:S(2)}) %collective-permute-start.14) | collective-permute-done | bytes 196640 | tf_op jit(solution)/shard_map/ppermute | solution.py:26
  43.7 1.7 %collective-permute-start.18 = (bf16[48,2048]{1,0:T(8,128)(2,1)S(1)}, bf16[48,2048]{1,0:T(8,128)(2,1)S(1)}, u32[]{:S(2)}, u32[]{:S(2)}) collective-permute-start(bf16[48,2048]{1,0:T(8,128)(2,1)S(1)} %collective-permute-done.14), channel_id=1, source_target_pairs={{0,4},{2,6},{4,0},{6,2},{8,12},{10,14},{12,8},{14,10},{16,20},{18,... | collective-permute-start | bytes 589832 | tf_op jit(solution)/shard_map/ppermute | solution.py:26
  45.4 1.5 %collective-permute-start.19 = (bf16[48,2048]{1,0:T(8,128)(2,1)S(1)}, bf16[48,2048]{1,0:T(8,128)(2,1)S(1)}, u32[]{:S(2)}, u32[]{:S(2)}) collective-permute-start(bf16[48,2048]{1,0:T(8,128)(2,1)S(1)} %collective-permute-done.17), channel_id=1, source_target_pairs={{0,2},{2,0},{4,6},{6,4},{8,10},{10,8},{12,14},{14,12},{16,18},{18,... | collective-permute-start | bytes 589832 | tf_op jit(solution)/shard_map/ppermute | solution.py:26
  46.9 2.0 %collective-permute-done.8 = bf16[48,2048]{1,0:T(8,128)(2,1)S(1)} collective-permute-done((bf16[48,2048]{1,0:T(8,128)(2,1)S(1)}, bf16[48,2048]{1,0:T(8,128)(2,1)S(1)}, u32[]{:S(2)}, u32[]{:S(2)}) %collective-permute-start.8) | collective-permute-done | bytes 196640 | tf_op jit(solution)/shard_map/ppermute | solution.py:26
  49.0 1.8 %convolution_convert_fusion.4 = bf16[384,1024]{1,0:T(8,128)(2,1)S(1)} fusion(bf16[384,2048]{1,0:T(8,128)(2,1)S(1)} %constant_dynamic-update-slice_fusion.4, bf16[1024,2048]{1,0:T(8,128)(2,1)S(1)} %copy-done.7), kind=kOutput, calls=%fused_computation.17 | convolution fusion | flops 1611005952 | bytes 6553600 | tf_op jit(solution)/shard_map/dot_general | solution.py:94
  51.2 1.8 %convolution_convert_fusion.3 = bf16[384,1024]{1,0:T(8,128)(2,1)S(1)} fusion(bf16[384,2048]{1,0:T(8,128)(2,1)S(1)} %constant_dynamic-update-slice_fusion.16, bf16[2048,1024]{1,0:T(8,128)(2,1)S(1)} %copy-done.8), kind=kOutput, calls=%fused_computation.16 | convolution fusion | flops 1611005952 | bytes 6553600 | tf_op jit(solution)/shard_map/dot_general | solution.py:97
  53.3 2.0 %collective-permute-done.20 = bf16[384,1024]{1,0:T(8,128)(2,1)S(1)} collective-permute-done((bf16[384,1024]{1,0:T(8,128)(2,1)S(1)}, bf16[384,1024]{1,0:T(8,128)(2,1)S(1)}, u32[]{:S(2)}, u32[]{:S(2)}) %collective-permute-start.20) | collective-permute-done | bytes 786464 | tf_op jit(solution)/shard_map/ppermute | solution.py:38
  55.3 1.7 %convert_reduce_fusion.1 = (f32[1024]{0:T(1024)}, bf16[384,1024]{1,0:T(8,128)(2,1)S(1)}) fusion(f32[1024]{0:T(1024)S(1)} %copy-done.5, bf16[384,1024]{1,0:T(8,128)(2,1)S(1)} %collective-permute-done.20, bf16[384,1024]{1,0:T(8,128)(2,1)S(1)} %convolution_convert_fusion.3, bf16[384,1024]{1,0:T(8,128)(2,1)S(1)} %collective-permute-done.10, ...), kind=kLoop, calls=%fused_computation.13 | loop fusion | flops 7470080 | bytes 3940352 | tf_op jit(solution)/shard_map/reduce_sum | solution.py:121
  57.0 1.8 %convolution_convert_fusion.2 = bf16[384,2048]{1,0:T(8,128)(2,1)S(1)} fusion(bf16[384,1024]{1,0:T(8,128)(2,1)S(1)} %get-tuple-element.15, bf16[2048,1024]{1,0:T(8,128)(2,1)S(1)} %copy-done.8), kind=kOutput, calls=%fused_computation.3 | convolution fusion | flops 1611399168 | bytes 6553600 | tf_op jit(solution)/shard_map/dot_general | solution.py:103
  59.4 1.6 %collective-permute-start.21 = (bf16[48,2048]{1,0:T(8,128)(2,1)S(1)}, bf16[48,2048]{1,0:T(8,128)(2,1)S(1)}, u32[]{:S(2)}, u32[]{:S(2)}) collective-permute-start(bf16[48,2048]{1,0:T(8,128)(2,1)S(1)} %get-tuple-element.23), channel_id=1, source_target_pairs={{0,4},{2,6},{4,0},{6,2},{8,12},{10,14},{12,8},{14,10},{16,20},{18,... | collective-permute-start | bytes 589832 | tf_op jit(solution)/shard_map/ppermute | solution.py:26
  61.0 1.5 %collective-permute-start.25 = (bf16[48,2048]{1,0:T(8,128)(2,1)S(1)}, bf16[48,2048]{1,0:T(8,128)(2,1)S(1)}, u32[]{:S(2)}, u32[]{:S(2)}) collective-permute-start(bf16[48,2048]{1,0:T(8,128)(2,1)S(1)} %get-tuple-element.24), channel_id=1, source_target_pairs={{0,2},{2,0},{4,6},{6,4},{8,10},{10,8},{12,14},{14,12},{16,18},{18,... | collective-permute-start | bytes 589832 | tf_op jit(solution)/shard_map/ppermute | solution.py:26
  62.4 4.2 %collective-permute-done.22 = bf16[48,2048]{1,0:T(8,128)(2,1)S(1)} collective-permute-done((bf16[48,2048]{1,0:T(8,128)(2,1)S(1)}, bf16[48,2048]{1,0:T(8,128)(2,1)S(1)}, u32[]{:S(2)}, u32[]{:S(2)}) %collective-permute-start.22) | collective-permute-done | bytes 196640 | tf_op jit(solution)/shard_map/ppermute | solution.py:26
  66.7 1.5 %collective-permute-start.23 = (bf16[48,2048]{1,0:T(8,128)(2,1)S(1)}, bf16[48,2048]{1,0:T(8,128)(2,1)S(1)}, u32[]{:S(2)}, u32[]{:S(2)}) collective-permute-start(bf16[48,2048]{1,0:T(8,128)(2,1)S(1)} %add_convert_fusion.2), channel_id=1, source_target_pairs={{0,2},{2,0},{4,6},{6,4},{8,10},{10,8},{12,14},{14,12},{16,18},{18,... | collective-permute-start | bytes 589832 | tf_op jit(solution)/shard_map/ppermute | solution.py:26
  68.9 1.4 %collective-permute-done.21 = bf16[48,2048]{1,0:T(8,128)(2,1)S(1)} collective-permute-done((bf16[48,2048]{1,0:T(8,128)(2,1)S(1)}, bf16[48,2048]{1,0:T(8,128)(2,1)S(1)}, u32[]{:S(2)}, u32[]{:S(2)}) %collective-permute-start.21) | collective-permute-done | bytes 196640 | tf_op jit(solution)/shard_map/ppermute | solution.py:26
  70.3 4.3 %collective-permute-done.23 = bf16[48,2048]{1,0:T(8,128)(2,1)S(1)} collective-permute-done((bf16[48,2048]{1,0:T(8,128)(2,1)S(1)}, bf16[48,2048]{1,0:T(8,128)(2,1)S(1)}, u32[]{:S(2)}, u32[]{:S(2)}) %collective-permute-start.23) | collective-permute-done | bytes 196640 | tf_op jit(solution)/shard_map/ppermute | solution.py:26
  76.1 2.7 %collective-permute-start.28 = (bf16[24,2048]{1,0:T(8,128)(2,1)S(1)}, bf16[24,2048]{1,0:T(8,128)(2,1)S(1)}, u32[]{:S(2)}, u32[]{:S(2)}) collective-permute-start(bf16[24,2048]{1,0:T(8,128)(2,1)S(1)} %slice.166), channel_id=1, source_target_pairs={{0,24},{2,26},{4,28},{6,30},{8,0},{10,2},{12,4},{14,6},{16,8},{18,... | collective-permute-start | bytes 294920 | tf_op jit(solution)/shard_map/ppermute | solution.py:35
  78.8 1.6 %collective-permute-done.26 = bf16[48,2048]{1,0:T(8,128)(2,1)S(1)} collective-permute-done((bf16[48,2048]{1,0:T(8,128)(2,1)S(1)}, bf16[48,2048]{1,0:T(8,128)(2,1)S(1)}, u32[]{:S(2)}, u32[]{:S(2)}) %collective-permute-start.26) | collective-permute-done | bytes 196640 | tf_op jit(solution)/shard_map/ppermute | solution.py:26
  80.5 2.1 %collective-permute-start.27 = (bf16[24,2048]{1,0:T(8,128)(2,1)S(1)}, bf16[24,2048]{1,0:T(8,128)(2,1)S(1)}, u32[]{:S(2)}, u32[]{:S(2)}) collective-permute-start(bf16[24,2048]{1,0:T(8,128)(2,1)S(1)} %get-tuple-element.27), channel_id=1, source_target_pairs={{0,16},{2,18},{4,20},{6,22},{8,24},{10,26},{12,28},{14,30},{16,0},... | collective-permute-start | bytes 294920 | tf_op jit(solution)/shard_map/ppermute | solution.py:35
  82.7 1.4 %collective-permute-start.29 = (bf16[24,2048]{1,0:T(8,128)(2,1)S(1)}, bf16[24,2048]{1,0:T(8,128)(2,1)S(1)}, u32[]{:S(2)}, u32[]{:S(2)}) collective-permute-start(bf16[24,2048]{1,0:T(8,128)(2,1)S(1)} %get-tuple-element.28), channel_id=1, source_target_pairs={{0,8},{2,10},{4,12},{6,14},{8,16},{10,18},{12,20},{14,22},{16,24},... | collective-permute-start | bytes 294920 | tf_op jit(solution)/shard_map/ppermute | solution.py:35
  84.1 4.5 %convolution_convert_fusion = bf16[1024,2048]{1,0:T(8,128)(2,1)} fusion(bf16[384,2048]{1,0:T(8,128)(2,1)S(1)} %constant_dynamic-update-slice_fusion.4, bf16[384,1024]{1,0:T(8,128)(2,1)S(1)} %collective-permute-done.20, bf16[384,1024]{1,0:T(8,128)(2,1)S(1)} %convolution_convert_fusion.3, f32[1024]{0:T(1024)S(1)} %copy-done.5), kind=kOutput, calls=%fused_computation | convolution fusion | flops 1616248832 | bytes 7344128 | tf_op jit(solution)/shard_map/dot_general | solution.py:115
  89.5 1.1 collective-permute-done.30
  90.8 4.4 %convolution_convert_fusion.1 = bf16[2048,1024]{1,0:T(8,128)(2,1)} fusion(bf16[384,2048]{1,0:T(8,128)(2,1)S(1)} %constant_dynamic-update-slice_fusion.16, bf16[384,1024]{1,0:T(8,128)(2,1)S(1)} %get-tuple-element.15), kind=kOutput, calls=%fused_computation.1 | convolution fusion | flops 1612709888 | bytes 6553600 | tf_op jit(solution)/shard_map/dot_general | solution.py:118
  95.2 3.8 %collective-permute-start.33 = (bf16[32,2048]{1,0:T(8,128)(2,1)S(1)}, bf16[32,2048]{1,0:T(8,128)(2,1)S(1)}, u32[]{:S(2)}, u32[]{:S(2)}) collective-permute-start(bf16[32,2048]{1,0:T(8,128)(2,1)S(1)} %pad_maximum_fusion.3), channel_id=1, source_target_pairs={{0,24},{2,26},{4,28},{6,30},{8,0},{10,2},{12,4},{14,6},{16,8},{18,... | collective-permute-start | bytes 393224 | tf_op jit(solution)/shard_map/ppermute | solution.py:35
  99.7 1.5 %collective-permute-start.36 = (bf16[48,2048]{1,0:T(8,128)(2,1)S(1)}, bf16[48,2048]{1,0:T(8,128)(2,1)S(1)}, u32[]{:S(2)}, u32[]{:S(2)}) collective-permute-start(bf16[48,2048]{1,0:T(8,128)(2,1)S(1)} %pad_maximum_fusion.1), channel_id=1, source_target_pairs={{0,2},{2,0},{4,6},{6,4},{8,10},{10,8},{12,14},{14,12},{16,18},{18,... | collective-permute-start | bytes 589832 | tf_op jit(solution)/shard_map/ppermute | solution.py:26
  101.2 1.8 %collective-permute-done.33 = bf16[32,2048]{1,0:T(8,128)(2,1)S(1)} collective-permute-done((bf16[32,2048]{1,0:T(8,128)(2,1)S(1)}, bf16[32,2048]{1,0:T(8,128)(2,1)S(1)}, u32[]{:S(2)}, u32[]{:S(2)}) %collective-permute-start.33) | collective-permute-done | bytes 131104 | tf_op jit(solution)/shard_map/ppermute | solution.py:35
  103.0 4.6 %collective-permute-done.32 = bf16[32,2048]{1,0:T(8,128)(2,1)S(1)} collective-permute-done((bf16[32,2048]{1,0:T(8,128)(2,1)S(1)}, bf16[32,2048]{1,0:T(8,128)(2,1)S(1)}, u32[]{:S(2)}, u32[]{:S(2)}) %collective-permute-start.32) | collective-permute-done | bytes 131104 | tf_op jit(solution)/shard_map/ppermute | solution.py:35
  107.7 1.6 %collective-permute-start.34 = (bf16[3,2048]{1,0:T(4,128)(2,1)S(1)}, bf16[3,2048]{1,0:T(4,128)(2,1)S(1)}, u32[]{:S(2)}, u32[]{:S(2)}) collective-permute-start(bf16[3,2048]{1,0:T(4,128)(2,1)S(1)} %pad_maximum_fusion.4), channel_id=1, source_target_pairs={{0,2},{2,0},{4,6},{6,4},{8,10},{10,8},{12,14},{14,12},{16,18},{18,... | collective-permute-start | bytes 36872 | tf_op jit(solution)/shard_map/ppermute | solution.py:26
  109.3 2.2 %collective-permute-done.34 = bf16[3,2048]{1,0:T(4,128)(2,1)S(1)} collective-permute-done((bf16[3,2048]{1,0:T(4,128)(2,1)S(1)}, bf16[3,2048]{1,0:T(4,128)(2,1)S(1)}, u32[]{:S(2)}, u32[]{:S(2)}) %collective-permute-start.34) | collective-permute-done | bytes 12320 | tf_op jit(solution)/shard_map/ppermute | solution.py:26
  113.0 1.5 %collective-permute-start.39 = (bf16[48,2048]{1,0:T(8,128)(2,1)}, bf16[48,2048]{1,0:T(8,128)(2,1)S(1)}, u32[]{:S(2)}, u32[]{:S(2)}) collective-permute-start(bf16[48,2048]{1,0:T(8,128)(2,1)} %pad_maximum_fusion.2), channel_id=1, source_target_pairs={{0,4},{2,6},{4,0},{6,2},{8,12},{10,14},{12,8},{14,10},{16,20},{18,... | collective-permute-start | bytes 589832 | tf_op jit(solution)/shard_map/ppermute | solution.py:26
  114.5 1.5 %collective-permute-start.37 = (bf16[48,2048]{1,0:T(8,128)(2,1)}, bf16[48,2048]{1,0:T(8,128)(2,1)}, u32[]{:S(2)}, u32[]{:S(2)}) collective-permute-start(bf16[48,2048]{1,0:T(8,128)(2,1)} %pad_maximum_fusion.2), channel_id=1, source_target_pairs={{0,2},{2,0},{4,6},{6,4},{8,10},{10,8},{12,14},{14,12},{16,18},{18,... | collective-permute-start | bytes 589832 | tf_op jit(solution)/shard_map/ppermute | solution.py:26
  117.3 3.6 %collective-permute-done.39 = bf16[48,2048]{1,0:T(8,128)(2,1)S(1)} collective-permute-done((bf16[48,2048]{1,0:T(8,128)(2,1)}, bf16[48,2048]{1,0:T(8,128)(2,1)S(1)}, u32[]{:S(2)}, u32[]{:S(2)}) %collective-permute-start.39) | collective-permute-done | bytes 196640 | tf_op jit(solution)/shard_map/ppermute | solution.py:26
  122.4 0.9 constant_dynamic-update-slice_fusion.30
  123.4 3.1 %collective-permute-done.41 = bf16[48,2048]{1,0:T(8,128)(2,1)S(1)} collective-permute-done((bf16[48,2048]{1,0:T(8,128)(2,1)S(1)}, bf16[48,2048]{1,0:T(8,128)(2,1)S(1)}, u32[]{:S(2)}, u32[]{:S(2)}) %collective-permute-start.41) | collective-permute-done | bytes 196640 | tf_op jit(solution)/shard_map/ppermute | solution.py:26
  126.6 2.0 %fusion.7 = f32[256,2048]{1,0:T(8,128)} fusion(bf16[384,2048]{1,0:T(8,128)(2,1)S(1)} %constant_dynamic-update-slice_fusion.26, s32[384]{0:T(512)S(1)} %convert_element_type.220), kind=kOutput, calls=%fused_computation.25 | convolution fusion | flops 402948096 | bytes 3671552 | tf_op jit(solution)/shard_map/dot_general | solution.py:152
  (136 shorter events, 12.7 us)
Async XLA Ops:
  0.6 8.0 %copy-start = (bf16[256,2048]{1,0:T(8,128)(2,1)S(1)}, bf16[256,2048]{1,0:T(8,128)(2,1)}, u32[]{:S(2)}) copy-start(bf16[256,2048]{1,0:T(8,128)(2,1)} %param.11) | copy-start | bytes 3145732
  0.6 10.5 %copy-start.3 = (f32[2048]{0:T(1024)S(1)}, f32[2048]{0:T(1024)}, u32[]{:S(2)}) copy-start(f32[2048]{0:T(1024)} %param.12) | copy-start | bytes 24580
  0.7 10.5 %copy-start.4 = (f32[2048]{0:T(1024)S(1)}, f32[2048]{0:T(1024)}, u32[]{:S(2)}) copy-start(f32[2048]{0:T(1024)} %param.13) | copy-start | bytes 24580
  0.7 18.6 %collective-permute-start.2 = (bf16[24,2048]{1,0:T(8,128)(2,1)}, bf16[24,2048]{1,0:T(8,128)(2,1)S(1)}, u32[]{:S(2)}, u32[]{:S(2)}) collective-permute-start(bf16[24,2048]{1,0:T(8,128)(2,1)} %param.17), channel_id=1, source_target_pairs={{0,16},{2,18},{4,20},{6,22},{8,24},{10,26},{12,28},{14,30},{16,0},... | collective-permute-start | bytes 294920 | tf_op jit(solution)/shard_map/ppermute | solution.py:35
  4.8 7.8 %collective-permute-start.1 = (bf16[24,2048]{1,0:T(8,128)(2,1)}, bf16[24,2048]{1,0:T(8,128)(2,1)S(1)}, u32[]{:S(2)}, u32[]{:S(2)}) collective-permute-start(bf16[24,2048]{1,0:T(8,128)(2,1)} %param.17), channel_id=1, source_target_pairs={{0,8},{2,10},{4,12},{6,14},{8,16},{10,18},{12,20},{14,22},{16,24},... | collective-permute-start | bytes 294920 | tf_op jit(solution)/shard_map/ppermute | solution.py:35
  6.3 12.9 %collective-permute-start.3 = (bf16[24,2048]{1,0:T(8,128)(2,1)}, bf16[24,2048]{1,0:T(8,128)(2,1)S(1)}, u32[]{:S(2)}, u32[]{:S(2)}) collective-permute-start(bf16[24,2048]{1,0:T(8,128)(2,1)} %param.17), channel_id=1, source_target_pairs={{0,24},{2,26},{4,28},{6,30},{8,0},{10,2},{12,4},{14,6},{16,8},{18,... | collective-permute-start | bytes 294920 | tf_op jit(solution)/shard_map/ppermute | solution.py:35
  9.9 1.2 collective-permute-start
  11.3 13.3 %collective-permute-start.13 = (bf16[24,2048]{1,0:T(8,128)(2,1)S(1)}, bf16[24,2048]{1,0:T(8,128)(2,1)S(1)}, u32[]{:S(2)}, u32[]{:S(2)}) collective-permute-start(bf16[24,2048]{1,0:T(8,128)(2,1)S(1)} %get-tuple-element.20), channel_id=1, source_target_pairs={{0,24},{2,26},{4,28},{6,30},{8,0},{10,2},{12,4},{14,6},{16,8},{18,... | collective-permute-start | bytes 294920 | tf_op jit(solution)/shard_map/ppermute | solution.py:35
  11.4 11.6 %collective-permute-start.12 = (bf16[24,2048]{1,0:T(8,128)(2,1)S(1)}, bf16[24,2048]{1,0:T(8,128)(2,1)S(1)}, u32[]{:S(2)}, u32[]{:S(2)}) collective-permute-start(bf16[24,2048]{1,0:T(8,128)(2,1)S(1)} %get-tuple-element.20), channel_id=1, source_target_pairs={{0,16},{2,18},{4,20},{6,22},{8,24},{10,26},{12,28},{14,30},{16,0},... | collective-permute-start | bytes 294920 | tf_op jit(solution)/shard_map/ppermute | solution.py:35
  12.6 9.8 %collective-permute-start.11 = (bf16[24,2048]{1,0:T(8,128)(2,1)S(1)}, bf16[24,2048]{1,0:T(8,128)(2,1)S(1)}, u32[]{:S(2)}, u32[]{:S(2)}) collective-permute-start(bf16[24,2048]{1,0:T(8,128)(2,1)S(1)} %get-tuple-element.20), channel_id=1, source_target_pairs={{0,8},{2,10},{4,12},{6,14},{8,16},{10,18},{12,20},{14,22},{16,24},... | collective-permute-start | bytes 294920 | tf_op jit(solution)/shard_map/ppermute | solution.py:35
  19.3 14.1 %collective-permute-start.7 = (bf16[48,2048]{1,0:T(8,128)(2,1)S(1)}, bf16[48,2048]{1,0:T(8,128)(2,1)S(1)}, u32[]{:S(2)}, u32[]{:S(2)}) collective-permute-start(bf16[48,2048]{1,0:T(8,128)(2,1)S(1)} %get-tuple-element.35), channel_id=1, source_target_pairs={{0,4},{2,6},{4,0},{6,2},{8,12},{10,14},{12,8},{14,10},{16,20},{18,... | collective-permute-start | bytes 589832 | tf_op jit(solution)/shard_map/ppermute | solution.py:26
  20.9 11.9 %collective-permute-start.5 = (bf16[48,2048]{1,0:T(8,128)(2,1)S(1)}, bf16[48,2048]{1,0:T(8,128)(2,1)S(1)}, u32[]{:S(2)}, u32[]{:S(2)}) collective-permute-start(bf16[48,2048]{1,0:T(8,128)(2,1)S(1)} %get-tuple-element.35), channel_id=1, source_target_pairs={{0,2},{2,0},{4,6},{6,4},{8,10},{10,8},{12,14},{14,12},{16,18},{18,... | collective-permute-start | bytes 589832 | tf_op jit(solution)/shard_map/ppermute | solution.py:26
  22.4 11.6 %collective-permute-start.6 = (bf16[48,2048]{1,0:T(8,128)(2,1)S(1)}, bf16[48,2048]{1,0:T(8,128)(2,1)S(1)}, u32[]{:S(2)}, u32[]{:S(2)}) collective-permute-start(bf16[48,2048]{1,0:T(8,128)(2,1)S(1)} %get-tuple-element.39), channel_id=1, source_target_pairs={{0,4},{2,6},{4,0},{6,2},{8,12},{10,14},{12,8},{14,10},{16,20},{18,... | collective-permute-start | bytes 589832 | tf_op jit(solution)/shard_map/ppermute | solution.py:26
  23.0 8.3 %collective-permute-start.4 = (bf16[48,2048]{1,0:T(8,128)(2,1)S(1)}, bf16[48,2048]{1,0:T(8,128)(2,1)S(1)}, u32[]{:S(2)}, u32[]{:S(2)}) collective-permute-start(bf16[48,2048]{1,0:T(8,128)(2,1)S(1)} %get-tuple-element.39), channel_id=1, source_target_pairs={{0,2},{2,0},{4,6},{6,4},{8,10},{10,8},{12,14},{14,12},{16,18},{18,... | collective-permute-start | bytes 589832 | tf_op jit(solution)/shard_map/ppermute | solution.py:26
  24.6 19.1 %collective-permute-start.17 = (bf16[48,2048]{1,0:T(8,128)(2,1)S(1)}, bf16[48,2048]{1,0:T(8,128)(2,1)S(1)}, u32[]{:S(2)}, u32[]{:S(2)}) collective-permute-start(bf16[48,2048]{1,0:T(8,128)(2,1)S(1)} %get-tuple-element.43), channel_id=1, source_target_pairs={{0,4},{2,6},{4,0},{6,2},{8,12},{10,14},{12,8},{14,10},{16,20},{18,... | collective-permute-start | bytes 589832 | tf_op jit(solution)/shard_map/ppermute | solution.py:26
  25.7 23.2 %copy-start.7 = (bf16[1024,2048]{1,0:T(8,128)(2,1)S(1)}, bf16[1024,2048]{1,0:T(8,128)(2,1)}, u32[]{:S(2)}) copy-start(bf16[1024,2048]{1,0:T(8,128)(2,1)} %param.16) | copy-start | bytes 12582916
  31.3 14.1 %collective-permute-start.15 = (bf16[48,2048]{1,0:T(8,128)(2,1)S(1)}, bf16[48,2048]{1,0:T(8,128)(2,1)S(1)}, u32[]{:S(2)}, u32[]{:S(2)}) collective-permute-start(bf16[48,2048]{1,0:T(8,128)(2,1)S(1)} %get-tuple-element.43), channel_id=1, source_target_pairs={{0,2},{2,0},{4,6},{6,4},{8,10},{10,8},{12,14},{14,12},{16,18},{18,... | collective-permute-start | bytes 589832 | tf_op jit(solution)/shard_map/ppermute | solution.py:26
  32.8 14.0 %collective-permute-start.16 = (bf16[48,2048]{1,0:T(8,128)(2,1)S(1)}, bf16[48,2048]{1,0:T(8,128)(2,1)S(1)}, u32[]{:S(2)}, u32[]{:S(2)}) collective-permute-start(bf16[48,2048]{1,0:T(8,128)(2,1)S(1)} %pad_maximum_fusion), channel_id=1, source_target_pairs={{0,4},{2,6},{4,0},{6,2},{8,12},{10,14},{12,8},{14,10},{16,20},{18,... | collective-permute-start | bytes 589832 | tf_op jit(solution)/shard_map/ppermute | solution.py:26
  33.4 9.8 %collective-permute-start.14 = (bf16[48,2048]{1,0:T(8,128)(2,1)S(1)}, bf16[48,2048]{1,0:T(8,128)(2,1)S(1)}, u32[]{:S(2)}, u32[]{:S(2)}) collective-permute-start(bf16[48,2048]{1,0:T(8,128)(2,1)S(1)} %pad_maximum_fusion), channel_id=1, source_target_pairs={{0,2},{2,0},{4,6},{6,4},{8,10},{10,8},{12,14},{14,12},{16,18},{18,... | collective-permute-start | bytes 589832 | tf_op jit(solution)/shard_map/ppermute | solution.py:26
  34.0 14.9 %collective-permute-start.9 = (bf16[48,2048]{1,0:T(8,128)(2,1)S(1)}, bf16[48,2048]{1,0:T(8,128)(2,1)S(1)}, u32[]{:S(2)}, u32[]{:S(2)}) collective-permute-start(bf16[48,2048]{1,0:T(8,128)(2,1)S(1)} %collective-permute-done.7), channel_id=1, source_target_pairs={{0,2},{2,0},{4,6},{6,4},{8,10},{10,8},{12,14},{14,12},{16,18},{18,... | collective-permute-start | bytes 589832 | tf_op jit(solution)/shard_map/ppermute | solution.py:26
  43.2 5.7 %collective-permute-start.8 = (bf16[48,2048]{1,0:T(8,128)(2,1)S(1)}, bf16[48,2048]{1,0:T(8,128)(2,1)S(1)}, u32[]{:S(2)}, u32[]{:S(2)}) collective-permute-start(bf16[48,2048]{1,0:T(8,128)(2,1)S(1)} %collective-permute-done.4), channel_id=1, source_target_pairs={{0,4},{2,6},{4,0},{6,2},{8,12},{10,14},{12,8},{14,10},{16,20},{18,... | collective-permute-start | bytes 589832 | tf_op jit(solution)/shard_map/ppermute | solution.py:26
  43.7 7.3 %collective-permute-start.18 = (bf16[48,2048]{1,0:T(8,128)(2,1)S(1)}, bf16[48,2048]{1,0:T(8,128)(2,1)S(1)}, u32[]{:S(2)}, u32[]{:S(2)}) collective-permute-start(bf16[48,2048]{1,0:T(8,128)(2,1)S(1)} %collective-permute-done.14), channel_id=1, source_target_pairs={{0,4},{2,6},{4,0},{6,2},{8,12},{10,14},{12,8},{14,10},{16,20},{18,... | collective-permute-start | bytes 589832 | tf_op jit(solution)/shard_map/ppermute | solution.py:26
  45.4 5.7 %collective-permute-start.19 = (bf16[48,2048]{1,0:T(8,128)(2,1)S(1)}, bf16[48,2048]{1,0:T(8,128)(2,1)S(1)}, u32[]{:S(2)}, u32[]{:S(2)}) collective-permute-start(bf16[48,2048]{1,0:T(8,128)(2,1)S(1)} %collective-permute-done.17), channel_id=1, source_target_pairs={{0,2},{2,0},{4,6},{6,4},{8,10},{10,8},{12,14},{14,12},{16,18},{18,... | collective-permute-start | bytes 589832 | tf_op jit(solution)/shard_map/ppermute | solution.py:26
  50.8 2.5 %collective-permute-start.10 = (bf16[384,1024]{1,0:T(8,128)(2,1)S(1)}, bf16[384,1024]{1,0:T(8,128)(2,1)S(1)}, u32[]{:S(2)}, u32[]{:S(2)}) collective-permute-start(bf16[384,1024]{1,0:T(8,128)(2,1)S(1)} %convolution_convert_fusion.4), channel_id=1, source_target_pairs={{0,1},{1,0},{2,3},{3,2},{4,5},{5,4},{6,7},{7,6},{8,9},{9,8},{10,11... | collective-permute-start | bytes 2359304 | tf_op jit(solution)/shard_map/ppermute | solution.py:38
  53.0 2.4 %collective-permute-start.20 = (bf16[384,1024]{1,0:T(8,128)(2,1)S(1)}, bf16[384,1024]{1,0:T(8,128)(2,1)S(1)}, u32[]{:S(2)}, u32[]{:S(2)}) collective-permute-start(bf16[384,1024]{1,0:T(8,128)(2,1)S(1)} %convolution_convert_fusion.3), channel_id=1, source_target_pairs={{0,1},{1,0},{2,3},{3,2},{4,5},{5,4},{6,7},{7,6},{8,9},{9,8},{10,11... | collective-permute-start | bytes 2359304 | tf_op jit(solution)/shard_map/ppermute | solution.py:38
  58.8 9.5 %copy-start.6 = (s32[24]{0:T(128)S(1)}, s32[24]{0:T(128)}, u32[]{:S(2)}) copy-start(s32[24]{0:T(128)} %param.10) | copy-start | bytes 292
  58.9 7.8 %collective-permute-start.22 = (bf16[48,2048]{1,0:T(8,128)(2,1)S(1)}, bf16[48,2048]{1,0:T(8,128)(2,1)S(1)}, u32[]{:S(2)}, u32[]{:S(2)}) collective-permute-start(bf16[48,2048]{1,0:T(8,128)(2,1)S(1)} %get-tuple-element.26), channel_id=1, source_target_pairs={{0,4},{2,6},{4,0},{6,2},{8,12},{10,14},{12,8},{14,10},{16,20},{18,... | collective-permute-start | bytes 589832 | tf_op jit(solution)/shard_map/ppermute | solution.py:26
  59.4 10.9 %collective-permute-start.21 = (bf16[48,2048]{1,0:T(8,128)(2,1)S(1)}, bf16[48,2048]{1,0:T(8,128)(2,1)S(1)}, u32[]{:S(2)}, u32[]{:S(2)}) collective-permute-start(bf16[48,2048]{1,0:T(8,128)(2,1)S(1)} %get-tuple-element.23), channel_id=1, source_target_pairs={{0,4},{2,6},{4,0},{6,2},{8,12},{10,14},{12,8},{14,10},{16,20},{18,... | collective-permute-start | bytes 589832 | tf_op jit(solution)/shard_map/ppermute | solution.py:26
  61.0 9.3 %collective-permute-start.25 = (bf16[48,2048]{1,0:T(8,128)(2,1)S(1)}, bf16[48,2048]{1,0:T(8,128)(2,1)S(1)}, u32[]{:S(2)}, u32[]{:S(2)}) collective-permute-start(bf16[48,2048]{1,0:T(8,128)(2,1)S(1)} %get-tuple-element.24), channel_id=1, source_target_pairs={{0,2},{2,0},{4,6},{6,4},{8,10},{10,8},{12,14},{14,12},{16,18},{18,... | collective-permute-start | bytes 589832 | tf_op jit(solution)/shard_map/ppermute | solution.py:26
  66.7 7.8 %collective-permute-start.23 = (bf16[48,2048]{1,0:T(8,128)(2,1)S(1)}, bf16[48,2048]{1,0:T(8,128)(2,1)S(1)}, u32[]{:S(2)}, u32[]{:S(2)}) collective-permute-start(bf16[48,2048]{1,0:T(8,128)(2,1)S(1)} %add_convert_fusion.2), channel_id=1, source_target_pairs={{0,2},{2,0},{4,6},{6,4},{8,10},{10,8},{12,14},{14,12},{16,18},{18,... | collective-permute-start | bytes 589832 | tf_op jit(solution)/shard_map/ppermute | solution.py:26
  68.3 10.5 %collective-permute-start.24 = (bf16[48,2048]{1,0:T(8,128)(2,1)S(1)}, bf16[48,2048]{1,0:T(8,128)(2,1)S(1)}, u32[]{:S(2)}, u32[]{:S(2)}) collective-permute-start(bf16[48,2048]{1,0:T(8,128)(2,1)S(1)} %get-tuple-element.25), channel_id=1, source_target_pairs={{0,2},{2,0},{4,6},{6,4},{8,10},{10,8},{12,14},{14,12},{16,18},{18,... | collective-permute-start | bytes 589832 | tf_op jit(solution)/shard_map/ppermute | solution.py:26
  74.7 5.7 %collective-permute-start.26 = (bf16[48,2048]{1,0:T(8,128)(2,1)S(1)}, bf16[48,2048]{1,0:T(8,128)(2,1)S(1)}, u32[]{:S(2)}, u32[]{:S(2)}) collective-permute-start(bf16[48,2048]{1,0:T(8,128)(2,1)S(1)} %get-tuple-element.22), channel_id=1, source_target_pairs={{0,4},{2,6},{4,0},{6,2},{8,12},{10,14},{12,8},{14,10},{16,20},{18,... | collective-permute-start | bytes 589832 | tf_op jit(solution)/shard_map/ppermute | solution.py:26
  76.1 12.6 %collective-permute-start.28 = (bf16[24,2048]{1,0:T(8,128)(2,1)S(1)}, bf16[24,2048]{1,0:T(8,128)(2,1)S(1)}, u32[]{:S(2)}, u32[]{:S(2)}) collective-permute-start(bf16[24,2048]{1,0:T(8,128)(2,1)S(1)} %slice.166), channel_id=1, source_target_pairs={{0,24},{2,26},{4,28},{6,30},{8,0},{10,2},{12,4},{14,6},{16,8},{18,... | collective-permute-start | bytes 294920 | tf_op jit(solution)/shard_map/ppermute | solution.py:35
  80.5 8.1 %collective-permute-start.27 = (bf16[24,2048]{1,0:T(8,128)(2,1)S(1)}, bf16[24,2048]{1,0:T(8,128)(2,1)S(1)}, u32[]{:S(2)}, u32[]{:S(2)}) collective-permute-start(bf16[24,2048]{1,0:T(8,128)(2,1)S(1)} %get-tuple-element.27), channel_id=1, source_target_pairs={{0,16},{2,18},{4,20},{6,22},{8,24},{10,26},{12,28},{14,30},{16,0},... | collective-permute-start | bytes 294920 | tf_op jit(solution)/shard_map/ppermute | solution.py:35
  82.7 6.4 %collective-permute-start.29 = (bf16[24,2048]{1,0:T(8,128)(2,1)S(1)}, bf16[24,2048]{1,0:T(8,128)(2,1)S(1)}, u32[]{:S(2)}, u32[]{:S(2)}) collective-permute-start(bf16[24,2048]{1,0:T(8,128)(2,1)S(1)} %get-tuple-element.28), channel_id=1, source_target_pairs={{0,8},{2,10},{4,12},{6,14},{8,16},{10,18},{12,20},{14,22},{16,24},... | collective-permute-start | bytes 294920 | tf_op jit(solution)/shard_map/ppermute | solution.py:35
  89.4 1.2 collective-permute-start.30
  90.7 8.3 %copy-start.1 = (bf16[24,2048]{1,0:T(8,128)(2,1)}, bf16[24,2048]{1,0:T(8,128)(2,1)S(1)}, u32[]{:S(2)}) copy-start(bf16[24,2048]{1,0:T(8,128)(2,1)S(1)} %get-tuple-element.17) | copy-start | bytes 294916
  90.8 8.3 %collective-permute-start.31 = (bf16[32,2048]{1,0:T(8,128)(2,1)S(1)}, bf16[32,2048]{1,0:T(8,128)(2,1)S(1)}, u32[]{:S(2)}, u32[]{:S(2)}) collective-permute-start(bf16[32,2048]{1,0:T(8,128)(2,1)S(1)} %pad_maximum_fusion.3), channel_id=1, source_target_pairs={{0,8},{2,10},{4,12},{6,14},{8,16},{10,18},{12,20},{14,22},{16,24},... | collective-permute-start | bytes 393224 | tf_op jit(solution)/shard_map/ppermute | solution.py:35
  95.2 7.7 %collective-permute-start.33 = (bf16[32,2048]{1,0:T(8,128)(2,1)S(1)}, bf16[32,2048]{1,0:T(8,128)(2,1)S(1)}, u32[]{:S(2)}, u32[]{:S(2)}) collective-permute-start(bf16[32,2048]{1,0:T(8,128)(2,1)S(1)} %pad_maximum_fusion.3), channel_id=1, source_target_pairs={{0,24},{2,26},{4,28},{6,30},{8,0},{10,2},{12,4},{14,6},{16,8},{18,... | collective-permute-start | bytes 393224 | tf_op jit(solution)/shard_map/ppermute | solution.py:35
  99.1 8.5 %collective-permute-start.32 = (bf16[32,2048]{1,0:T(8,128)(2,1)S(1)}, bf16[32,2048]{1,0:T(8,128)(2,1)S(1)}, u32[]{:S(2)}, u32[]{:S(2)}) collective-permute-start(bf16[32,2048]{1,0:T(8,128)(2,1)S(1)} %pad_maximum_fusion.3), channel_id=1, source_target_pairs={{0,16},{2,18},{4,20},{6,22},{8,24},{10,26},{12,28},{14,30},{16,0},... | collective-permute-start | bytes 393224 | tf_op jit(solution)/shard_map/ppermute | solution.py:35
  99.1 24.2 %collective-permute-start.38 = (bf16[48,2048]{1,0:T(8,128)(2,1)S(1)}, bf16[48,2048]{1,0:T(8,128)(2,1)S(1)}, u32[]{:S(2)}, u32[]{:S(2)}) collective-permute-start(bf16[48,2048]{1,0:T(8,128)(2,1)S(1)} %pad_maximum_fusion.1), channel_id=1, source_target_pairs={{0,4},{2,6},{4,0},{6,2},{8,12},{10,14},{12,8},{14,10},{16,20},{18,... | collective-permute-start | bytes 589832 | tf_op jit(solution)/shard_map/ppermute | solution.py:26
  99.7 17.1 %collective-permute-start.36 = (bf16[48,2048]{1,0:T(8,128)(2,1)S(1)}, bf16[48,2048]{1,0:T(8,128)(2,1)S(1)}, u32[]{:S(2)}, u32[]{:S(2)}) collective-permute-start(bf16[48,2048]{1,0:T(8,128)(2,1)S(1)} %pad_maximum_fusion.1), channel_id=1, source_target_pairs={{0,2},{2,0},{4,6},{6,4},{8,10},{10,8},{12,14},{14,12},{16,18},{18,... | collective-permute-start | bytes 589832 | tf_op jit(solution)/shard_map/ppermute | solution.py:26
  107.7 3.8 %collective-permute-start.34 = (bf16[3,2048]{1,0:T(4,128)(2,1)S(1)}, bf16[3,2048]{1,0:T(4,128)(2,1)S(1)}, u32[]{:S(2)}, u32[]{:S(2)}) collective-permute-start(bf16[3,2048]{1,0:T(4,128)(2,1)S(1)} %pad_maximum_fusion.4), channel_id=1, source_target_pairs={{0,2},{2,0},{4,6},{6,4},{8,10},{10,8},{12,14},{14,12},{16,18},{18,... | collective-permute-start | bytes 36872 | tf_op jit(solution)/shard_map/ppermute | solution.py:26
  111.7 4.3 %collective-permute-start.35 = (bf16[3,2048]{1,0:T(4,128)(2,1)S(1)}, bf16[3,2048]{1,0:T(4,128)(2,1)S(1)}, u32[]{:S(2)}, u32[]{:S(2)}) collective-permute-start(bf16[3,2048]{1,0:T(4,128)(2,1)S(1)} %pad_maximum_fusion.5), channel_id=1, source_target_pairs={{0,4},{2,6},{4,0},{6,2},{8,12},{10,14},{12,8},{14,10},{16,20},{18,... | collective-permute-start | bytes 36872 | tf_op jit(solution)/shard_map/ppermute | solution.py:26
  113.0 7.9 %collective-permute-start.39 = (bf16[48,2048]{1,0:T(8,128)(2,1)}, bf16[48,2048]{1,0:T(8,128)(2,1)S(1)}, u32[]{:S(2)}, u32[]{:S(2)}) collective-permute-start(bf16[48,2048]{1,0:T(8,128)(2,1)} %pad_maximum_fusion.2), channel_id=1, source_target_pairs={{0,4},{2,6},{4,0},{6,2},{8,12},{10,14},{12,8},{14,10},{16,20},{18,... | collective-permute-start | bytes 589832 | tf_op jit(solution)/shard_map/ppermute | solution.py:26
  114.5 7.9 %collective-permute-start.37 = (bf16[48,2048]{1,0:T(8,128)(2,1)}, bf16[48,2048]{1,0:T(8,128)(2,1)}, u32[]{:S(2)}, u32[]{:S(2)}) collective-permute-start(bf16[48,2048]{1,0:T(8,128)(2,1)} %pad_maximum_fusion.2), channel_id=1, source_target_pairs={{0,2},{2,0},{4,6},{6,4},{8,10},{10,8},{12,14},{14,12},{16,18},{18,... | collective-permute-start | bytes 589832 | tf_op jit(solution)/shard_map/ppermute | solution.py:26
  116.7 6.6 %collective-permute-start.40 = (bf16[48,2048]{1,0:T(8,128)(2,1)S(1)}, bf16[48,2048]{1,0:T(8,128)(2,1)S(1)}, u32[]{:S(2)}, u32[]{:S(2)}) collective-permute-start(bf16[48,2048]{1,0:T(8,128)(2,1)S(1)} %collective-permute-done.36), channel_id=1, source_target_pairs={{0,4},{2,6},{4,0},{6,2},{8,12},{10,14},{12,8},{14,10},{16,20},{18,... | collective-permute-start | bytes 589832 | tf_op jit(solution)/shard_map/ppermute | solution.py:26
  120.9 5.7 %collective-permute-start.41 = (bf16[48,2048]{1,0:T(8,128)(2,1)S(1)}, bf16[48,2048]{1,0:T(8,128)(2,1)S(1)}, u32[]{:S(2)}, u32[]{:S(2)}) collective-permute-start(bf16[48,2048]{1,0:T(8,128)(2,1)S(1)} %collective-permute-done.39), channel_id=1, source_target_pairs={{0,2},{2,0},{4,6},{6,4},{8,10},{10,8},{12,14},{14,12},{16,18},{18,... | collective-permute-start | bytes 589832 | tf_op jit(solution)/shard_map/ppermute | solution.py:26
  (3 other events, 14.3 us)

commit v2 on v1

v2 whole, which is shorter than its diff:
```python
import jax
import jax.numpy as jnp
from jax import lax
from jax.experimental import pallas as pl
from jax.experimental.pallas import tpu as pltpu
from jax.sharding import PartitionSpec as P

D = 4096

EPS = 1e-06
INV_ROOT_TWO = 0.7071067811865476
INV_ROOT_TWO_PI = 0.3989422804014327
BF16 = jnp.bfloat16
F32 = jnp.float32


def gelu_parts(values):
    normal_cdf = 0.5 * (1.0 + jax.scipy.special.erf(values * INV_ROOT_TWO))
    normal_pdf = jnp.exp(-0.5 * values * values) * INV_ROOT_TWO_PI
    return (values * normal_cdf, normal_cdf + values * normal_pdf)


def array(shape, dtype):
    return jax.ShapeDtypeStruct(shape, dtype)


def params():
    return pltpu.CompilerParams(vmem_limit_bytes=6 << 20)


def cost(flops, read):
    return pl.CostEstimate(flops=flops, bytes_accessed=read, transcendentals=0)


def once(shape):
    return pl.BlockSpec(shape, lambda i: (0, 0), pipeline_mode=pl.Buffered(1))


def place_kernel(*refs):
    pieces, indices, d_pos = refs[:4], *refs[4:]
    shape = (d_pos.shape[0], indices.shape[1])
    owners = lax.broadcasted_iota(jnp.int32, shape, 0) == indices[...]
    rows = jnp.concatenate([piece[...] for piece in pieces])
    d_pos[...] = jnp.dot(
        jnp.where(owners, 1.0, 0.0).astype(BF16), rows, preferred_element_type=F32
    )


def place(pieces, indices, places):
    size, cols = pieces[0].shape
    tile = min(cols, 512)
    return pl.pallas_call(
        place_kernel,
        grid=(cols // tile,),
        out_shape=array((places, cols), F32),
        in_specs=[pl.BlockSpec((size, tile), lambda i: (0, i))] * 4 + [once((1, 4 * size))],
        out_specs=pl.BlockSpec((places, tile), lambda i: (0, i)),
        compiler_params=params(),
        cost_estimate=cost(8 * size * places * cols, 8 * size * cols),
        name="place",
    )(*pieces, indices)


def program(wide, narrow):
    outer = wide // 4

    def flip(x, bits):
        return lax.ppermute(x, "wide", [(i, i ^ bits) for i in range(wide)])

    def turn(x, step):
        bits = [((1, 2), (2, 1))[c if narrow == 2 else 0][step] for c in range(narrow)]
        pairs = [
            (i * narrow + c, (i ^ bits[c]) * narrow + c) for i in range(wide) for c in range(narrow)
        ]
        return lax.ppermute(x, ("wide", "narrow"), pairs)

    def other_core(x):
        return lax.ppermute(x, "narrow", [(0, 1), (1, 0)])

    def narrow_sum(x):
        if narrow == 2:
            return x.astype(F32) + other_core(x).astype(F32)
        return lax.psum(x.astype(F32), "narrow")

    def narrow_sum_tokens(x):
        if narrow != 2:
            return narrow_sum(x)
        got, size = other_core(x), x.shape[0] // 4
        quarters = [got[i * size : (i + 1) * size] for i in (0, 2, 1, 3)]
        return x.astype(F32) + jnp.concatenate(quarters).astype(F32)

    def gather(own, rider=None):
        column = jnp.concatenate([own] + [flip(own, 4 * k) for k in range(1, outer)])
        first, second = lax.optimization_barrier((turn(column, 0), turn(column, 1)))
        both = turn(first, 1)
        if rider is not None:
            for step in range(outer.bit_length() - 1):
                rider += flip(rider, 4 << step)
            rider, _ = lax.optimization_barrier((rider, column))
            rider += turn(rider, 0)
            rider, _ = lax.optimization_barrier((rider, first))
            rider += turn(rider, 1)
        return (column, first, second, both), rider

    def order():
        core = lax.axis_index("narrow") if narrow == 2 else 0
        quarters = jnp.where(core == 0, jnp.array([0, 1, 2, 3]), jnp.array([0, 2, 1, 3]))
        patterns = quarters[:, None] + 4 * jnp.arange(outer)[None]
        return jnp.bitwise_xor(lax.axis_index("wide"), patterns.reshape(-1))

    def on_device(patches, patch_index, pos_table, ln_gain, ln_bias, w_up, up_bias, w_down, d_out):
        rows, cols = patches.shape
        table_rows = pos_table.shape[0]
        picked = lax.broadcasted_iota(jnp.int32, (rows, table_rows), 1) == patch_index[:, None]
        onehot = jnp.where(picked, 1.0, 0.0).astype(BF16)
        pos_rows = jnp.dot(onehot, pos_table, preferred_element_type=F32)
        layer_in = patches.astype(F32) + pos_rows
        sums = jnp.stack([jnp.sum(layer_in, axis=1), jnp.sum(layer_in * layer_in, axis=1)])
        first_sum, square_sum = narrow_sum(sums)
        centre_mean = (first_sum / D)[:, None]
        variance = (square_sum / D)[:, None] - centre_mean * centre_mean
        inverse_std = lax.rsqrt(variance + EPS)
        normed = (layer_in - centre_mean) * inverse_std
        hidden_in = (normed * ln_gain + ln_bias).astype(BF16)
        grad_panel = jnp.concatenate(gather(d_out)[0])
        hidden_panel = jnp.concatenate(gather(hidden_in)[0])
        back_part = lax.dot_general(
            grad_panel, w_down, (((1,), (1,)), ((), ())), preferred_element_type=F32
        )
        pre_part = jnp.dot(hidden_panel, w_up, preferred_element_type=F32)
        back_full = narrow_sum_tokens(back_part.astype(BF16))
        pre_full = narrow_sum_tokens(pre_part.astype(BF16))
        act_value, slope = gelu_parts(pre_full + up_bias)
        activation = act_value.astype(BF16)
        d_hidden = (back_full * slope).astype(BF16)
        d_normout = lax.dot_general(
            d_hidden, w_up, (((1,), (1,)), ((), ())), preferred_element_type=F32
        ).astype(BF16)
        size = outer * rows
        parts = [d_normout[i * size : (i + 1) * size] for i in range(4)]
        own, first, second, both = parts
        far, near = turn(both, 1), turn(second, 1)
        back = turn((first.astype(F32) + far.astype(F32)).astype(BF16), 0)
        activation, grad_panel, _ = lax.optimization_barrier((activation, grad_panel, far))
        contract_rows = (((0,), (0,)), ((), ()))
        d_down = lax.dot_general(
            activation, grad_panel, contract_rows, preferred_element_type=F32
        ).astype(BF16)
        d_downbias = jnp.sum(grad_panel.astype(F32), axis=0)
        back, d_down, d_downbias = lax.optimization_barrier((back, d_down, d_downbias))
        column = own.astype(F32) + near.astype(F32) + back.astype(F32)
        blocks = [column[i * rows : (i + 1) * rows] for i in range(outer)]
        home = [flip(blocks[k].astype(BF16), 4 * k) for k in range(1, outer)]
        d_hidden, hidden_panel, _ = lax.optimization_barrier((d_hidden, hidden_panel, back))
        d_up = lax.dot_general(
            hidden_panel, d_hidden, contract_rows, preferred_element_type=F32
        ).astype(BF16)
        d_upbias = jnp.sum(d_hidden.astype(F32), axis=0)
        d_up, d_upbias, home = lax.optimization_barrier((d_up, d_upbias, home))
        own_sum = sum([block.astype(F32) for block in home], blocks[0])

        scaled = own_sum * ln_gain
        row_sums = narrow_sum(jnp.stack([jnp.sum(scaled, axis=1), jnp.sum(scaled * normed, axis=1)]))
        scaled_sum, cross_sum = row_sums
        d_layer = inverse_std * (
            scaled - (scaled_sum / D)[:, None] - normed * (cross_sum / D)[:, None]
        )
        summed_grad = (d_out.astype(F32) + d_layer).astype(BF16)
        gain_term = jnp.sum(own_sum * normed, axis=0)
        bias_term = jnp.sum(own_sum, axis=0)
        tokens = wide * rows
        depth = -(-tokens // cols)
        lane = lax.broadcasted_iota(jnp.int32, (wide, rows), 0)
        mine = jnp.where(lane == lax.axis_index("wide"), patch_index.astype(F32)[None], 0.0)
        mine = jnp.pad(mine.reshape(-1), (0, depth * cols - tokens)).reshape(depth, cols)
        rider = jnp.concatenate([jnp.stack([gain_term, bias_term]), mine])
        pos_pieces, rider = gather(summed_grad, rider)
        d_gain, d_lnbias = rider[0], rider[1]
        indices = rider[2:].reshape(-1)[:tokens].astype(jnp.int32).reshape(wide, rows)
        indices = jnp.take(indices, order(), axis=0, mode="clip").reshape(-1)
        d_pos = place(pos_pieces, indices[None], table_rows)
        return (summed_grad, d_pos, d_gain, d_lnbias, d_up, d_upbias, d_down, d_downbias)

    return on_device


def solution(mesh):
    in_specs = (
        P("wide", "narrow"),
        P("wide"),
        P(None, "narrow"),
        P("narrow"),
        P("narrow"),
        P("narrow", "wide"),
        P("wide"),
        P("wide", "narrow"),
        P("wide", "narrow"),
    )
    out_specs = (
        P("wide", "narrow"),
        P(None, "narrow"),
        P("narrow"),
        P("narrow"),
        P("narrow", "wide"),
        P("wide"),
        P("wide", "narrow"),
        P("narrow"),
    )
    return jax.shard_map(
        program(mesh.shape["wide"], mesh.shape["narrow"]),
        mesh=mesh,
        in_specs=in_specs,
        out_specs=out_specs,
        check_vma=False,
    )
```

time: 129 us -> 125 us (0.969)
  starting transfers between devices: 55.5 us -> 38.8 us
  other arithmetic: 4.25 us -> 8.95 us
  waiting for transfers between devices: 46.6 us -> 50.7 us
  Pallas kernels: 0 us -> 2.61 us
  local copies, waits for them, and re-layouts: 3.36 us -> 4.89 us
    ppermute x38 -> x28, starting transfers between devices: 54.9 us -> 38.7 us  [the longest x14 22 us: flip(): return lax.ppermute(x, 'wide', [(i, i ^ bits) for i in range(wide)])]
    ppermute x38 -> x28, waiting for transfers between devices: 43.3 us -> 47.4 us  [the longest x14 32.8 us: turn(): return lax.ppermute(x, ('wide', 'narrow'), pairs)]
    convert_element_type x5, other arithmetic: 0.11 us -> 3.96 us  [the longest x1 2.58 us: on_device(): activation = act_value.astype(BF16)]
    pallas_call x0 -> x1, Pallas kernels: none -> 2.61 us  [place(): pl.pallas_call(place_kernel, grid=(cols // tile,), out_shape=array((place...]
    dot_general x1 -> x0, matrix products: 2.03 us -> none  [on_device(): jnp.dot(jnp.where(owners, 1.0, 0.0).astype(BF16), pos_panel, preferred_el...]
    slice x7 -> x5, local copies, waits for them, and re-layouts: 0.14 us -> 1.56 us  [the longest x1 0.81 us: on_device(): parts = [d_normout[i * size:(i + 1) * size] for i in range(4)]]
    reduce_sum x1, other arithmetic: 0.85 us -> 2.26 us  [on_device(): d_downbias = jnp.sum(grad_panel.astype(F32), axis=0)]
  transfers between devices with their start and end apart: 42 -> 32, of which waited for: 18 -> 16; matrix products, arithmetic and copies ran while one was open for 15% -> 19% of each run, Pallas kernels for 0% -> 0%
where the time goes in v2:
time: 125 us; the launch traced here: 124 us
  waiting for transfers between devices  50.7 us (41%)
  starting transfers between devices  38.8 us (31%)
  matrix products  17.3 us (14%)
  other arithmetic  8.95 us (7%)
  local copies, waits for them, and re-layouts  4.89 us (4%)
  Pallas kernels  2.61 us (2%)
    ppermute x14, waiting for transfers between devices, turn(): return lax.ppermute(x, ('wide', 'narrow'), pairs)  32.8 us
    ppermute x14, starting transfers between devices, flip(): return lax.ppermute(x, 'wide', [(i, i ^ bits) for i in range(wide)])  22 us
    ppermute x14, starting transfers between devices, turn(): return lax.ppermute(x, ('wide', 'narrow'), pairs)  16.7 us
    ppermute x14, waiting for transfers between devices, flip(): return lax.ppermute(x, 'wide', [(i, i ^ bits) for i in range(wide)])  14.7 us
    dot_general x1, matrix products, on_device(): lax.dot_general(activation, grad_panel, contract_rows, preferred_element_...  4.41 us
    dot_general x1, matrix products, on_device(): lax.dot_general(hidden_panel, d_hidden, contract_rows, preferred_element_...  4.4 us
    ppermute x4, waiting for transfers between devices, other_core(): return lax.ppermute(x, 'narrow', [(0, 1), (1, 0)])  3.24 us
    dot_general x1, matrix products, on_device(): lax.dot_general(grad_panel, w_down, (((1,), (1,)), ((), ())), preferred_e...  2.71 us
  transfers between devices with their start and end apart: 32, of which 16 were waited for; matrix products, arithmetic and copies ran while one was open for 19% of the time, Pallas kernels for 0%

profile of v2, /device:TPU:0, one launch (start us, length us, event | category | flops | bytes accessed | tf_op | source)
XLA Modules:
  0.0 124.4 jit_solution(7300687035879175092)
XLA Ops:
  0.7 4.1 %collective-permute-start.2 = (bf16[24,2048]{1,0:T(8,128)(2,1)}, bf16[24,2048]{1,0:T(8,128)(2,1)S(1)}, u32[]{:S(2)}, u32[]{:S(2)}) collective-permute-start(bf16[24,2048]{1,0:T(8,128)(2,1)} %param.19), channel_id=1, source_target_pairs={{0,16},{2,18},{4,20},{6,22},{8,24},{10,26},{12,28},{14,30},{16,0},... | collective-permute-start | bytes 294920 | tf_op jit(solution)/shard_map/ppermute | solution.py:68
  4.8 1.6 %collective-permute-start.1 = (bf16[24,2048]{1,0:T(8,128)(2,1)}, bf16[24,2048]{1,0:T(8,128)(2,1)S(1)}, u32[]{:S(2)}, u32[]{:S(2)}) collective-permute-start(bf16[24,2048]{1,0:T(8,128)(2,1)} %param.19), channel_id=1, source_target_pairs={{0,8},{2,10},{4,12},{6,14},{8,0},{10,2},{12,4},{14,6},{16,24},{18,... | collective-permute-start | bytes 294920 | tf_op jit(solution)/shard_map/ppermute | solution.py:68
  6.4 1.3 %fusion.19 = (f32[24]{0:T(128)S(1)}, f32[24]{0:T(128)S(1)}, f32[24,2048]{1,0:T(8,128)S(1)}) fusion(bf16[256,2048]{1,0:T(8,128)(2,1)S(1)} %copy-done, s32[24]{0:T(128)} %param.12, bf16[24,2048]{1,0:T(8,128)(2,1)} %param.11), kind=kOutput, calls=%fused_computation.79 | convolution fusion | flops 25429968 | bytes 1343776 | tf_op jit(solution)/shard_map/dot_general | solution.py:116
  7.8 0.9 constant_dynamic-update-slice_fusion.3
  9.1 3.9 %collective-permute-start.10 = (bf16[24,2048]{1,0:T(8,128)(2,1)S(1)}, bf16[24,2048]{1,0:T(8,128)(2,1)S(1)}, u32[]{:S(2)}, u32[]{:S(2)}) collective-permute-start(bf16[24,2048]{1,0:T(8,128)(2,1)S(1)} %get-tuple-element.58), channel_id=1, source_target_pairs={{0,24},{2,26},{4,28},{6,30},{8,16},{10,18},{12,20},{14,22},{16,8},... | collective-permute-start | bytes 294920 | tf_op jit(solution)/shard_map/ppermute | solution.py:68
  13.7 1.7 %collective-permute-start.5 = (bf16[96,2048]{1,0:T(8,128)(2,1)S(1)}, bf16[96,2048]{1,0:T(8,128)(2,1)S(1)}, u32[]{:S(2)}, u32[]{:S(2)}) collective-permute-start(bf16[96,2048]{1,0:T(8,128)(2,1)S(1)} %get-tuple-element.74), channel_id=1, source_target_pairs={{0,4},{1,3},{2,6},{3,1},{4,0},{5,7},{6,2},{7,5},{8,12},{9,11},{10,... | collective-permute-start | bytes 1179656 | tf_op jit(solution)/shard_map/ppermute | solution.py:75
  15.4 1.5 %collective-permute-start.4 = (bf16[96,2048]{1,0:T(8,128)(2,1)S(1)}, bf16[96,2048]{1,0:T(8,128)(2,1)S(1)}, u32[]{:S(2)}, u32[]{:S(2)}) collective-permute-start(bf16[96,2048]{1,0:T(8,128)(2,1)S(1)} %get-tuple-element.74), channel_id=1, source_target_pairs={{0,2},{1,5},{2,0},{3,7},{4,6},{5,1},{6,4},{7,3},{8,10},{9,13},{10,... | collective-permute-start | bytes 1179656 | tf_op jit(solution)/shard_map/ppermute | solution.py:75
  16.9 5.6 %collective-permute-done.9 = bf16[24,2048]{1,0:T(8,128)(2,1)S(1)} collective-permute-done((bf16[24,2048]{1,0:T(8,128)(2,1)S(1)}, bf16[24,2048]{1,0:T(8,128)(2,1)S(1)}, u32[]{:S(2)}, u32[]{:S(2)}) %collective-permute-start.9) | collective-permute-done | bytes 98336 | tf_op jit(solution)/shard_map/ppermute | solution.py:68
  22.6 1.6 %collective-permute-start.12 = (bf16[96,2048]{1,0:T(8,128)(2,1)S(1)}, bf16[96,2048]{1,0:T(8,128)(2,1)S(1)}, u32[]{:S(2)}, u32[]{:S(2)}) collective-permute-start(bf16[96,2048]{1,0:T(8,128)(2,1)S(1)} %pad_maximum_fusion.1), channel_id=1, source_target_pairs={{0,4},{1,3},{2,6},{3,1},{4,0},{5,7},{6,2},{7,5},{8,12},{9,11},{10,... | collective-permute-start | bytes 1179656 | tf_op jit(solution)/shard_map/ppermute | solution.py:75
  24.2 1.5 %collective-permute-start.11 = (bf16[96,2048]{1,0:T(8,128)(2,1)S(1)}, bf16[96,2048]{1,0:T(8,128)(2,1)S(1)}, u32[]{:S(2)}, u32[]{:S(2)}) collective-permute-start(bf16[96,2048]{1,0:T(8,128)(2,1)S(1)} %pad_maximum_fusion.1), channel_id=1, source_target_pairs={{0,2},{1,5},{2,0},{3,7},{4,6},{5,1},{6,4},{7,3},{8,10},{9,13},{10,... | collective-permute-start | bytes 1179656 | tf_op jit(solution)/shard_map/ppermute | solution.py:75
  25.8 1.5 %collective-permute-start.6 = (bf16[96,2048]{1,0:T(8,128)(2,1)S(1)}, bf16[96,2048]{1,0:T(8,128)(2,1)S(1)}, u32[]{:S(2)}, u32[]{:S(2)}) collective-permute-start(bf16[96,2048]{1,0:T(8,128)(2,1)S(1)} %collective-permute-done.4), channel_id=1, source_target_pairs={{0,4},{1,3},{2,6},{3,1},{4,0},{5,7},{6,2},{7,5},{8,12},{9,11},{10,... | collective-permute-start | bytes 1179656 | tf_op jit(solution)/shard_map/ppermute | solution.py:75
  27.3 6.9 %collective-permute-done.12 = bf16[96,2048]{1,0:T(8,128)(2,1)S(1)} collective-permute-done((bf16[96,2048]{1,0:T(8,128)(2,1)S(1)}, bf16[96,2048]{1,0:T(8,128)(2,1)S(1)}, u32[]{:S(2)}, u32[]{:S(2)}) %collective-permute-start.12) | collective-permute-done | bytes 393248 | tf_op jit(solution)/shard_map/ppermute | solution.py:75
  34.2 2.0 %collective-permute-done.11 = bf16[96,2048]{1,0:T(8,128)(2,1)S(1)} collective-permute-done((bf16[96,2048]{1,0:T(8,128)(2,1)S(1)}, bf16[96,2048]{1,0:T(8,128)(2,1)S(1)}, u32[]{:S(2)}, u32[]{:S(2)}) %collective-permute-start.11) | collective-permute-done | bytes 393248 | tf_op jit(solution)/shard_map/ppermute | solution.py:75
  36.8 1.7 %collective-permute-done.6 = bf16[96,2048]{1,0:T(8,128)(2,1)S(1)} collective-permute-done((bf16[96,2048]{1,0:T(8,128)(2,1)S(1)}, bf16[96,2048]{1,0:T(8,128)(2,1)S(1)}, u32[]{:S(2)}, u32[]{:S(2)}) %collective-permute-start.6) | collective-permute-done | bytes 393248 | tf_op jit(solution)/shard_map/ppermute | solution.py:75
  38.5 2.7 %convolution_convert_fusion.4 = bf16[384,1024]{1,0:T(8,128)(2,1)} fusion(bf16[384,2048]{1,0:T(8,128)(2,1)S(1)} %constant_dynamic-update-slice_fusion.4, bf16[1024,2048]{1,0:T(8,128)(2,1)S(1)} %copy-done.13), kind=kOutput, calls=%fused_computation.18 | convolution fusion | flops 1611005952 | bytes 6553600 | tf_op jit(solution)/shard_map/dot_general | solution.py:127
  41.2 2.8 %collective-permute-done.13 = bf16[96,2048]{1,0:T(8,128)(2,1)S(1)} collective-permute-done((bf16[96,2048]{1,0:T(8,128)(2,1)S(1)}, bf16[96,2048]{1,0:T(8,128)(2,1)S(1)}, u32[]{:S(2)}, u32[]{:S(2)}) %collective-permute-start.13) | collective-permute-done | bytes 393248 | tf_op jit(solution)/shard_map/ppermute | solution.py:75
  44.1 2.7 %convolution_convert_fusion.3 = bf16[384,1024]{1,0:T(8,128)(2,1)} fusion(bf16[384,2048]{1,0:T(8,128)(2,1)S(1)} %constant_dynamic-update-slice_fusion.11, bf16[2048,1024]{1,0:T(8,128)(2,1)S(1)} %copy-done.14), kind=kOutput, calls=%fused_computation.17 | convolution fusion | flops 1611005952 | bytes 6553600 | tf_op jit(solution)/shard_map/dot_general | solution.py:130
  46.9 2.4 %collective-permute-done.14 = bf16[384,1024]{1,0:T(8,128)(2,1)S(1)} collective-permute-done((bf16[384,1024]{1,0:T(8,128)(2,1)}, bf16[384,1024]{1,0:T(8,128)(2,1)S(1)}, u32[]{:S(2)}, u32[]{:S(2)}) %collective-permute-start.14) | collective-permute-done | bytes 786464 | tf_op jit(solution)/shard_map/ppermute | solution.py:78
  49.3 2.6 %multiply_convert_fusion = (bf16[384,1024]{1,0:T(8,128)(2,1)S(1)}, bf16[384,1024]{1,0:T(8,128)(2,1)S(1)}) fusion(bf16[384,1024]{1,0:T(8,128)(2,1)} %convolution_convert_fusion.3, f32[1024]{0:T(1024)S(1)} %copy-done.10, bf16[96,1024]{1,0:T(8,128)(2,1)S(1)} %get-tuple-element.64, bf16[96,1024]{1,0:T(8,128)(2,1)S(1)} %get-tuple-element.65, ...), kind=kLoop, calls=%fused_computation.14 | loop fusion | flops 12976128 | bytes 4722688 | tf_op jit(solution)/shard_map/convert_element_type | solution.py:134
  52.0 1.8 %convolution_convert_fusion.2 = bf16[384,2048]{1,0:T(8,128)(2,1)S(1)} fusion(bf16[384,1024]{1,0:T(8,128)(2,1)S(1)} %get-tuple-element.36, bf16[2048,1024]{1,0:T(8,128)(2,1)S(1)} %copy-done.15), kind=kOutput, calls=%fused_computation.4 | convolution fusion | flops 1611399168 | bytes 6553600 | tf_op jit(solution)/shard_map/dot_general | solution.py:136
  53.8 1.1 copy-done.3
  55.0 0.8 fusion.22
  56.5 1.6 %collective-permute-start.15 = (bf16[96,2048]{1,0:T(8,128)(2,1)S(1)}, bf16[96,2048]{1,0:T(8,128)(2,1)S(1)}, u32[]{:S(2)}, u32[]{:S(2)}) collective-permute-start(bf16[96,2048]{1,0:T(8,128)(2,1)S(1)} %get-tuple-element.61), channel_id=1, source_target_pairs={{0,4},{1,3},{2,6},{3,1},{4,0},{5,7},{6,2},{7,5},{8,12},{9,11},{10,... | collective-permute-start | bytes 1179656 | tf_op jit(solution)/shard_map/ppermute | solution.py:75
  58.1 5.8 %collective-permute-done.16 = bf16[96,2048]{1,0:T(8,128)(2,1)} collective-permute-done((bf16[96,2048]{1,0:T(8,128)(2,1)}, bf16[96,2048]{1,0:T(8,128)(2,1)}, u32[]{:S(2)}, u32[]{:S(2)}) %collective-permute-start.16) | collective-permute-done | bytes 393248 | tf_op jit(solution)/shard_map/ppermute | solution.py:75
  63.9 1.2 add_convert_fusion
  65.1 1.6 %collective-permute-start.17 = (bf16[96,2048]{1,0:T(8,128)(2,1)S(1)}, bf16[96,2048]{1,0:T(8,128)(2,1)S(1)}, u32[]{:S(2)}, u32[]{:S(2)}) collective-permute-start(bf16[96,2048]{1,0:T(8,128)(2,1)S(1)} %add_convert_fusion), channel_id=1, source_target_pairs={{0,2},{1,5},{2,0},{3,7},{4,6},{5,1},{6,4},{7,3},{8,10},{9,13},{10,... | collective-permute-start | bytes 1179656 | tf_op jit(solution)/shard_map/ppermute | solution.py:75
  66.7 2.3 %convert_reduce_fusion = f32[2048]{0:T(1024)} fusion(bf16[384,2048]{1,0:T(8,128)(2,1)} %copy-done.1), kind=kLoop, calls=%fused_computation.3 | loop fusion | flops 1570816 | bytes 1581056 | tf_op jit(solution)/shard_map/reduce_sum | solution.py:149
  68.9 4.4 %convolution_convert_fusion.1 = bf16[1024,2048]{1,0:T(8,128)(2,1)} fusion(bf16[384,1024]{1,0:T(8,128)(2,1)S(1)} %get-tuple-element.32, bf16[384,2048]{1,0:T(8,128)(2,1)S(1)} %copy-done.2), kind=kOutput, calls=%fused_computation.2 | convolution fusion | flops 1612709888 | bytes 6553600 | tf_op jit(solution)/shard_map/dot_general | solution.py:146
  73.3 1.3 %fusion.21 = (bf16[96,2048]{1,0:T(8,128)(2,1)S(1)}, f32[96,2048]{1,0:T(8,128)S(1)}) fusion(bf16[96,2048]{1,0:T(8,128)(2,1)S(1)} %collective-permute-done.17, bf16[96,2048]{1,0:T(8,128)(2,1)S(1)} %collective-permute-done.15, bf16[384,2048]{1,0:T(8,128)(2,1)} %copy-done.3), kind=kLoop, calls=%fused_computation.80 | loop fusion | flops 1179648 | bytes 2359296 | tf_op jit(solution)/shard_map/convert.2
  74.7 3.6 %collective-permute-start.20 = (bf16[24,2048]{1,0:T(8,128)(2,1)S(1)}, bf16[24,2048]{1,0:T(8,128)(2,1)S(1)}, u32[]{:S(2)}, u32[]{:S(2)}) collective-permute-start(bf16[24,2048]{1,0:T(8,128)(2,1)S(1)} %get-tuple-element.71), channel_id=1, source_target_pairs={{0,24},{2,26},{4,28},{6,30},{8,16},{10,18},{12,20},{14,22},{16,8},... | collective-permute-start | bytes 294920 | tf_op jit(solution)/shard_map/ppermute | solution.py:68
  78.2 2.3 %collective-permute-start.19 = (bf16[24,2048]{1,0:T(8,128)(2,1)S(1)}, bf16[24,2048]{1,0:T(8,128)(2,1)S(1)}, u32[]{:S(2)}, u32[]{:S(2)}) collective-permute-start(bf16[24,2048]{1,0:T(8,128)(2,1)S(1)} %get-tuple-element.72), channel_id=1, source_target_pairs={{0,16},{2,18},{4,20},{6,22},{8,24},{10,26},{12,28},{14,30},{16,0},... | collective-permute-start | bytes 294920 | tf_op jit(solution)/shard_map/ppermute | solution.py:68
  80.6 4.4 %convolution_convert_fusion = bf16[2048,1024]{1,0:T(8,128)(2,1)} fusion(bf16[384,2048]{1,0:T(8,128)(2,1)S(1)} %copy-done.9, bf16[384,1024]{1,0:T(8,128)(2,1)S(1)} %get-tuple-element.36), kind=kOutput, calls=%fused_computation.1 | convolution fusion | flops 1612709888 | bytes 6553600 | tf_op jit(solution)/shard_map/dot_general | solution.py:155
  85.0 0.7 convert_reduce_fusion.1
  85.7 1.7 %collective-permute-done.19 = bf16[24,2048]{1,0:T(8,128)(2,1)S(1)} collective-permute-done((bf16[24,2048]{1,0:T(8,128)(2,1)S(1)}, bf16[24,2048]{1,0:T(8,128)(2,1)S(1)}, u32[]{:S(2)}, u32[]{:S(2)}) %collective-permute-start.19) | collective-permute-done | bytes 98336 | tf_op jit(solution)/shard_map/ppermute | solution.py:68
  89.0 2.3 %collective-permute-start.24 = (bf16[24,2048]{1,0:T(8,128)(2,1)S(1)}, bf16[24,2048]{1,0:T(8,128)(2,1)S(1)}, u32[]{:S(2)}, u32[]{:S(2)}) collective-permute-start(bf16[24,2048]{1,0:T(8,128)(2,1)S(1)} %add_convert_fusion.1), channel_id=1, source_target_pairs={{0,24},{2,26},{4,28},{6,30},{8,16},{10,18},{12,20},{14,22},{16,8},... | collective-permute-start | bytes 294920 | tf_op jit(solution)/shard_map/ppermute | solution.py:68
  91.5 1.9 %collective-permute-start.22 = (bf16[24,2048]{1,0:T(8,128)(2,1)S(1)}, bf16[24,2048]{1,0:T(8,128)(2,1)S(1)}, u32[]{:S(2)}, u32[]{:S(2)}) collective-permute-start(bf16[24,2048]{1,0:T(8,128)(2,1)S(1)} %add_convert_fusion.1), channel_id=1, source_target_pairs={{0,8},{2,10},{4,12},{6,14},{8,0},{10,2},{12,4},{14,6},{16,24},{18,... | collective-permute-start | bytes 294920 | tf_op jit(solution)/shard_map/ppermute | solution.py:68
  93.5 0.9 collective-permute-start.29
  94.4 2.2 %collective-permute-done.24 = bf16[24,2048]{1,0:T(8,128)(2,1)S(1)} collective-permute-done((bf16[24,2048]{1,0:T(8,128)(2,1)S(1)}, bf16[24,2048]{1,0:T(8,128)(2,1)S(1)}, u32[]{:S(2)}, u32[]{:S(2)}) %collective-permute-start.24) | collective-permute-done | bytes 98336 | tf_op jit(solution)/shard_map/ppermute | solution.py:68
  96.6 5.2 %collective-permute-done.23 = bf16[24,2048]{1,0:T(8,128)(2,1)S(1)} collective-permute-done((bf16[24,2048]{1,0:T(8,128)(2,1)S(1)}, bf16[24,2048]{1,0:T(8,128)(2,1)S(1)}, u32[]{:S(2)}, u32[]{:S(2)}) %collective-permute-start.23) | collective-permute-done | bytes 98336 | tf_op jit(solution)/shard_map/ppermute | solution.py:68
  102.5 1.2 collective-permute-start.25
  103.7 0.9 collective-permute-start.30
  104.8 7.6 %collective-permute-done.30 = f32[3,2048]{1,0:T(4,128)S(1)} collective-permute-done((f32[3,2048]{1,0:T(4,128)S(1)}, f32[3,2048]{1,0:T(4,128)S(1)}, u32[]{:S(2)}, u32[]{:S(2)}) %collective-permute-start.30) | collective-permute-done | bytes 24608 | tf_op jit(solution)/shard_map/ppermute | solution.py:75
  112.4 0.8 collective-permute-done.26.refs_2_
  113.2 0.8 collective-permute-start.31
  114.0 1.2 collective-permute-start.27
  115.2 1.9 %collective-permute-done.31 = f32[3,2048]{1,0:T(4,128)S(1)} collective-permute-done((f32[3,2048]{1,0:T(4,128)S(1)}, f32[3,2048]{1,0:T(4,128)S(1)}, u32[]{:S(2)}, u32[]{:S(2)}) %collective-permute-start.31) | collective-permute-done | bytes 24608 | tf_op jit(solution)/shard_map/ppermute | solution.py:75
  118.5 3.3 %collective-permute-done.27.refs_3_ = bf16[96,2048]{1,0:T(8,128)(2,1)S(1)} collective-permute-done((bf16[96,2048]{1,0:T(8,128)(2,1)S(1)}, bf16[96,2048]{1,0:T(8,128)(2,1)S(1)}, u32[]{:S(2)}, u32[]{:S(2)}) %collective-permute-start.27) | collective-permute-done | bytes 393248 | tf_op jit(solution)/shard_map/ppermute | solution.py:75
  121.8 2.6 %place.1 = f32[256,2048]{1,0:T(8,128)} custom-call(bf16[96,2048]{1,0:T(8,128)(2,1)S(1)} %pad_maximum_fusion.2.refs_0_, bf16[96,2048]{1,0:T(8,128)(2,1)S(1)} %collective-permute-done.25.refs_1_, bf16[96,2048]{1,0:T(8,128)(2,1)S(1)} %collective-permute-done.26.refs_2_, bf16[96,2048]{1,0:T(8,128)(2,1)S(1)} %collective-permute-done.27.refs_3_, ...), custom_call_target="tpu_custom_call" | custom-call | flops 402653184 | bytes 1572864 | tf_op jit(solution)/shard_map/place/pallas_call | solution.py:52
  (108 shorter events, 6.9 us)
Async XLA Ops:
  0.6 5.7 %copy-start = (bf16[256,2048]{1,0:T(8,128)(2,1)S(1)}, bf16[256,2048]{1,0:T(8,128)(2,1)}, u32[]{:S(2)}) copy-start(bf16[256,2048]{1,0:T(8,128)(2,1)} %param.13) | copy-start | bytes 3145732
  0.6 8.3 %copy-start.6 = (f32[2048]{0:T(1024)S(1)}, f32[2048]{0:T(1024)}, u32[]{:S(2)}) copy-start(f32[2048]{0:T(1024)} %param.14) | copy-start | bytes 24580
  0.7 8.3 %copy-start.7 = (f32[2048]{0:T(1024)S(1)}, f32[2048]{0:T(1024)}, u32[]{:S(2)}) copy-start(f32[2048]{0:T(1024)} %param.15) | copy-start | bytes 24580
  0.7 12.9 %collective-permute-start.2 = (bf16[24,2048]{1,0:T(8,128)(2,1)}, bf16[24,2048]{1,0:T(8,128)(2,1)S(1)}, u32[]{:S(2)}, u32[]{:S(2)}) collective-permute-start(bf16[24,2048]{1,0:T(8,128)(2,1)} %param.19), channel_id=1, source_target_pairs={{0,16},{2,18},{4,20},{6,22},{8,24},{10,26},{12,28},{14,30},{16,0},... | collective-permute-start | bytes 294920 | tf_op jit(solution)/shard_map/ppermute | solution.py:68
  4.8 8.2 %collective-permute-start.1 = (bf16[24,2048]{1,0:T(8,128)(2,1)}, bf16[24,2048]{1,0:T(8,128)(2,1)S(1)}, u32[]{:S(2)}, u32[]{:S(2)}) collective-permute-start(bf16[24,2048]{1,0:T(8,128)(2,1)} %param.19), channel_id=1, source_target_pairs={{0,8},{2,10},{4,12},{6,14},{8,0},{10,2},{12,4},{14,6},{16,24},{18,... | collective-permute-start | bytes 294920 | tf_op jit(solution)/shard_map/ppermute | solution.py:68
  6.3 7.3 %collective-permute-start.3 = (bf16[24,2048]{1,0:T(8,128)(2,1)}, bf16[24,2048]{1,0:T(8,128)(2,1)S(1)}, u32[]{:S(2)}, u32[]{:S(2)}) collective-permute-start(bf16[24,2048]{1,0:T(8,128)(2,1)} %param.19), channel_id=1, source_target_pairs={{0,24},{2,26},{4,28},{6,30},{8,16},{10,18},{12,20},{14,22},{16,8},... | collective-permute-start | bytes 294920 | tf_op jit(solution)/shard_map/ppermute | solution.py:68
  7.7 1.2 collective-permute-start
  9.1 7.8 %collective-permute-start.10 = (bf16[24,2048]{1,0:T(8,128)(2,1)S(1)}, bf16[24,2048]{1,0:T(8,128)(2,1)S(1)}, u32[]{:S(2)}, u32[]{:S(2)}) collective-permute-start(bf16[24,2048]{1,0:T(8,128)(2,1)S(1)} %get-tuple-element.58), channel_id=1, source_target_pairs={{0,24},{2,26},{4,28},{6,30},{8,16},{10,18},{12,20},{14,22},{16,8},... | collective-permute-start | bytes 294920 | tf_op jit(solution)/shard_map/ppermute | solution.py:68
  12.9 9.6 %collective-permute-start.9 = (bf16[24,2048]{1,0:T(8,128)(2,1)S(1)}, bf16[24,2048]{1,0:T(8,128)(2,1)S(1)}, u32[]{:S(2)}, u32[]{:S(2)}) collective-permute-start(bf16[24,2048]{1,0:T(8,128)(2,1)S(1)} %get-tuple-element.58), channel_id=1, source_target_pairs={{0,16},{2,18},{4,20},{6,22},{8,24},{10,26},{12,28},{14,30},{16,0},... | collective-permute-start | bytes 294920 | tf_op jit(solution)/shard_map/ppermute | solution.py:68
  12.9 9.6 %collective-permute-start.8 = (bf16[24,2048]{1,0:T(8,128)(2,1)S(1)}, bf16[24,2048]{1,0:T(8,128)(2,1)S(1)}, u32[]{:S(2)}, u32[]{:S(2)}) collective-permute-start(bf16[24,2048]{1,0:T(8,128)(2,1)S(1)} %get-tuple-element.58), channel_id=1, source_target_pairs={{0,8},{2,10},{4,12},{6,14},{8,0},{10,2},{12,4},{14,6},{16,24},{18,... | collective-permute-start | bytes 294920 | tf_op jit(solution)/shard_map/ppermute | solution.py:68
  13.7 12.1 %collective-permute-start.5 = (bf16[96,2048]{1,0:T(8,128)(2,1)S(1)}, bf16[96,2048]{1,0:T(8,128)(2,1)S(1)}, u32[]{:S(2)}, u32[]{:S(2)}) collective-permute-start(bf16[96,2048]{1,0:T(8,128)(2,1)S(1)} %get-tuple-element.74), channel_id=1, source_target_pairs={{0,4},{1,3},{2,6},{3,1},{4,0},{5,7},{6,2},{7,5},{8,12},{9,11},{10,... | collective-permute-start | bytes 1179656 | tf_op jit(solution)/shard_map/ppermute | solution.py:75
  15.4 10.3 %collective-permute-start.4 = (bf16[96,2048]{1,0:T(8,128)(2,1)S(1)}, bf16[96,2048]{1,0:T(8,128)(2,1)S(1)}, u32[]{:S(2)}, u32[]{:S(2)}) collective-permute-start(bf16[96,2048]{1,0:T(8,128)(2,1)S(1)} %get-tuple-element.74), channel_id=1, source_target_pairs={{0,2},{1,5},{2,0},{3,7},{4,6},{5,1},{6,4},{7,3},{8,10},{9,13},{10,... | collective-permute-start | bytes 1179656 | tf_op jit(solution)/shard_map/ppermute | solution.py:75
  22.6 11.7 %collective-permute-start.12 = (bf16[96,2048]{1,0:T(8,128)(2,1)S(1)}, bf16[96,2048]{1,0:T(8,128)(2,1)S(1)}, u32[]{:S(2)}, u32[]{:S(2)}) collective-permute-start(bf16[96,2048]{1,0:T(8,128)(2,1)S(1)} %pad_maximum_fusion.1), channel_id=1, source_target_pairs={{0,4},{1,3},{2,6},{3,1},{4,0},{5,7},{6,2},{7,5},{8,12},{9,11},{10,... | collective-permute-start | bytes 1179656 | tf_op jit(solution)/shard_map/ppermute | solution.py:75
  24.2 12.1 %collective-permute-start.11 = (bf16[96,2048]{1,0:T(8,128)(2,1)S(1)}, bf16[96,2048]{1,0:T(8,128)(2,1)S(1)}, u32[]{:S(2)}, u32[]{:S(2)}) collective-permute-start(bf16[96,2048]{1,0:T(8,128)(2,1)S(1)} %pad_maximum_fusion.1), channel_id=1, source_target_pairs={{0,2},{1,5},{2,0},{3,7},{4,6},{5,1},{6,4},{7,3},{8,10},{9,13},{10,... | collective-permute-start | bytes 1179656 | tf_op jit(solution)/shard_map/ppermute | solution.py:75
  25.7 12.8 %copy-start.13 = (bf16[1024,2048]{1,0:T(8,128)(2,1)S(1)}, bf16[1024,2048]{1,0:T(8,128)(2,1)}, u32[]{:S(2)}) copy-start(bf16[1024,2048]{1,0:T(8,128)(2,1)} %param.18) | copy-start | bytes 12582916
  25.8 12.7 %collective-permute-start.6 = (bf16[96,2048]{1,0:T(8,128)(2,1)S(1)}, bf16[96,2048]{1,0:T(8,128)(2,1)S(1)}, u32[]{:S(2)}, u32[]{:S(2)}) collective-permute-start(bf16[96,2048]{1,0:T(8,128)(2,1)S(1)} %collective-permute-done.4), channel_id=1, source_target_pairs={{0,4},{1,3},{2,6},{3,1},{4,0},{5,7},{6,2},{7,5},{8,12},{9,11},{10,... | collective-permute-start | bytes 1179656 | tf_op jit(solution)/shard_map/ppermute | solution.py:75
  36.2 7.8 %collective-permute-start.13 = (bf16[96,2048]{1,0:T(8,128)(2,1)S(1)}, bf16[96,2048]{1,0:T(8,128)(2,1)S(1)}, u32[]{:S(2)}, u32[]{:S(2)}) collective-permute-start(bf16[96,2048]{1,0:T(8,128)(2,1)S(1)} %collective-permute-done.11), channel_id=1, source_target_pairs={{0,4},{1,3},{2,6},{3,1},{4,0},{5,7},{6,2},{7,5},{8,12},{9,11},{10,... | collective-permute-start | bytes 1179656 | tf_op jit(solution)/shard_map/ppermute | solution.py:75
  38.5 2.7 %copy-start.1 = (bf16[384,2048]{1,0:T(8,128)(2,1)}, bf16[384,2048]{1,0:T(8,128)(2,1)S(1)}, u32[]{:S(2)}) copy-start(bf16[384,2048]{1,0:T(8,128)(2,1)S(1)} %constant_dynamic-update-slice_fusion.4) | copy-start | bytes 4718596
  38.5 5.6 %copy-start.14 = (bf16[2048,1024]{1,0:T(8,128)(2,1)S(1)}, bf16[2048,1024]{1,0:T(8,128)(2,1)}, u32[]{:S(2)}) copy-start(bf16[2048,1024]{1,0:T(8,128)(2,1)} %param.16) | copy-start | bytes 12582916
  41.2 5.6 %collective-permute-start.7 = (bf16[384,1024]{1,0:T(8,128)(2,1)}, bf16[384,1024]{1,0:T(8,128)(2,1)S(1)}, u32[]{:S(2)}, u32[]{:S(2)}) collective-permute-start(bf16[384,1024]{1,0:T(8,128)(2,1)} %convolution_convert_fusion.4), channel_id=1, source_target_pairs={{0,1},{1,0},{2,3},{3,2},{4,5},{5,4},{6,7},{7,6},{8,9},{9,8},{10,11... | collective-permute-start | bytes 2359304 | tf_op jit(solution)/shard_map/ppermute | solution.py:78
  44.1 2.7 %copy-start.8 = (bf16[384,2048]{1,0:T(8,128)(2,1)}, bf16[384,2048]{1,0:T(8,128)(2,1)S(1)}, u32[]{:S(2)}) copy-start(bf16[384,2048]{1,0:T(8,128)(2,1)S(1)} %constant_dynamic-update-slice_fusion.11) | copy-start | bytes 4718596
  44.1 2.7 %copy-start.11 = (s32[24]{0:T(128)S(1)}, s32[24]{0:T(128)}, u32[]{:S(2)}) copy-start(s32[24]{0:T(128)} %param.12) | copy-start | bytes 292
  46.8 2.5 %collective-permute-start.14 = (bf16[384,1024]{1,0:T(8,128)(2,1)}, bf16[384,1024]{1,0:T(8,128)(2,1)S(1)}, u32[]{:S(2)}, u32[]{:S(2)}) collective-permute-start(bf16[384,1024]{1,0:T(8,128)(2,1)} %convolution_convert_fusion.3), channel_id=1, source_target_pairs={{0,1},{1,0},{2,3},{3,2},{4,5},{5,4},{6,7},{7,6},{8,9},{9,8},{10,11... | collective-permute-start | bytes 2359304 | tf_op jit(solution)/shard_map/ppermute | solution.py:78
  46.8 2.5 %copy-start.10 = (f32[1024]{0:T(1024)S(1)}, f32[1024]{0:T(1024)}, u32[]{:S(2)}) copy-start(f32[1024]{0:T(1024)} %param.17) | copy-start | bytes 12292
  49.3 2.7 %copy-start.15 = (bf16[2048,1024]{1,0:T(8,128)(2,1)S(1)}, bf16[2048,1024]{1,0:T(8,128)(2,1)}, u32[]{:S(2)}) copy-start(bf16[2048,1024]{1,0:T(8,128)(2,1)} %param.16) | copy-start | bytes 12582916
  53.8 1.1 copy-start.3
  55.0 1.5 %copy-start.12 = (s32[4]{0:T(128)S(1)}, s32[4]{0:T(128)}, u32[]{:S(2)}) copy-start(s32[4]{0:T(128)} %constant.38.clone) | copy-start | bytes 52
  55.8 8.1 %collective-permute-start.16 = (bf16[96,2048]{1,0:T(8,128)(2,1)}, bf16[96,2048]{1,0:T(8,128)(2,1)}, u32[]{:S(2)}, u32[]{:S(2)}) collective-permute-start(bf16[96,2048]{1,0:T(8,128)(2,1)} %get-tuple-element.62), channel_id=1, source_target_pairs={{0,4},{1,3},{2,6},{3,1},{4,0},{5,7},{6,2},{7,5},{8,12},{9,11},{10,... | collective-permute-start | bytes 1179656 | tf_op jit(solution)/shard_map/ppermute | solution.py:75
  56.4 12.5 %copy-start.2 = (bf16[384,2048]{1,0:T(8,128)(2,1)S(1)}, bf16[384,2048]{1,0:T(8,128)(2,1)}, u32[]{:S(2)}) copy-start(bf16[384,2048]{1,0:T(8,128)(2,1)} %copy-done.1) | copy-start | bytes 4718596
  56.5 16.9 %collective-permute-start.15 = (bf16[96,2048]{1,0:T(8,128)(2,1)S(1)}, bf16[96,2048]{1,0:T(8,128)(2,1)S(1)}, u32[]{:S(2)}, u32[]{:S(2)}) collective-permute-start(bf16[96,2048]{1,0:T(8,128)(2,1)S(1)} %get-tuple-element.61), channel_id=1, source_target_pairs={{0,4},{1,3},{2,6},{3,1},{4,0},{5,7},{6,2},{7,5},{8,12},{9,11},{10,... | collective-permute-start | bytes 1179656 | tf_op jit(solution)/shard_map/ppermute | solution.py:75
  65.1 8.2 %collective-permute-start.17 = (bf16[96,2048]{1,0:T(8,128)(2,1)S(1)}, bf16[96,2048]{1,0:T(8,128)(2,1)S(1)}, u32[]{:S(2)}, u32[]{:S(2)}) collective-permute-start(bf16[96,2048]{1,0:T(8,128)(2,1)S(1)} %add_convert_fusion), channel_id=1, source_target_pairs={{0,2},{1,5},{2,0},{3,7},{4,6},{5,1},{6,4},{7,3},{8,10},{9,13},{10,... | collective-permute-start | bytes 1179656 | tf_op jit(solution)/shard_map/ppermute | solution.py:75
  73.3 7.2 %copy-start.9 = (bf16[384,2048]{1,0:T(8,128)(2,1)S(1)}, bf16[384,2048]{1,0:T(8,128)(2,1)}, u32[]{:S(2)}) copy-start(bf16[384,2048]{1,0:T(8,128)(2,1)} %copy-done.8) | copy-start | bytes 4718596
  74.7 11.0 %collective-permute-start.20 = (bf16[24,2048]{1,0:T(8,128)(2,1)S(1)}, bf16[24,2048]{1,0:T(8,128)(2,1)S(1)}, u32[]{:S(2)}, u32[]{:S(2)}) collective-permute-start(bf16[24,2048]{1,0:T(8,128)(2,1)S(1)} %get-tuple-element.71), channel_id=1, source_target_pairs={{0,24},{2,26},{4,28},{6,30},{8,16},{10,18},{12,20},{14,22},{16,8},... | collective-permute-start | bytes 294920 | tf_op jit(solution)/shard_map/ppermute | solution.py:68
  78.2 9.1 %collective-permute-start.19 = (bf16[24,2048]{1,0:T(8,128)(2,1)S(1)}, bf16[24,2048]{1,0:T(8,128)(2,1)S(1)}, u32[]{:S(2)}, u32[]{:S(2)}) collective-permute-start(bf16[24,2048]{1,0:T(8,128)(2,1)S(1)} %get-tuple-element.72), channel_id=1, source_target_pairs={{0,16},{2,18},{4,20},{6,22},{8,24},{10,26},{12,28},{14,30},{16,0},... | collective-permute-start | bytes 294920 | tf_op jit(solution)/shard_map/ppermute | solution.py:68
  80.6 6.8 %collective-permute-start.18 = (bf16[24,2048]{1,0:T(8,128)(2,1)S(1)}, bf16[24,2048]{1,0:T(8,128)(2,1)S(1)}, u32[]{:S(2)}, u32[]{:S(2)}) collective-permute-start(bf16[24,2048]{1,0:T(8,128)(2,1)S(1)} %get-tuple-element.73), channel_id=1, source_target_pairs={{0,8},{2,10},{4,12},{6,14},{8,0},{10,2},{12,4},{14,6},{16,24},{18,... | collective-permute-start | bytes 294920 | tf_op jit(solution)/shard_map/ppermute | solution.py:68
  85.0 3.9 %copy-start.5 = (bf16[24,2048]{1,0:T(8,128)(2,1)S(1)}, bf16[24,2048]{1,0:T(8,128)(2,1)}, u32[]{:S(2)}) copy-start(bf16[24,2048]{1,0:T(8,128)(2,1)} %param.19) | copy-start | bytes 294916
  87.6 1.2 collective-permute-start.21
  87.7 5.7 %collective-permute-start.28 = (f32[3,2048]{1,0:T(4,128)S(1)}, f32[3,2048]{1,0:T(4,128)S(1)}, u32[]{:S(2)}, u32[]{:S(2)}) collective-permute-start(f32[3,2048]{1,0:T(4,128)S(1)} %pad_maximum_fusion.3), channel_id=1, source_target_pairs={{0,8},{2,10},{4,12},{6,14},{8,0},{10,2},{12,4},{14,6},{16,24},{18,... | collective-permute-start | bytes 73736 | tf_op jit(solution)/shard_map/ppermute | solution.py:68
  89.0 35.4 %copy-start.4 = (bf16[24,2048]{1,0:T(8,128)(2,1)}, bf16[24,2048]{1,0:T(8,128)(2,1)S(1)}, u32[]{:S(2)}) copy-start(bf16[24,2048]{1,0:T(8,128)(2,1)S(1)} %add_convert_fusion.1) | copy-start | bytes 294916
  89.0 7.6 %collective-permute-start.24 = (bf16[24,2048]{1,0:T(8,128)(2,1)S(1)}, bf16[24,2048]{1,0:T(8,128)(2,1)S(1)}, u32[]{:S(2)}, u32[]{:S(2)}) collective-permute-start(bf16[24,2048]{1,0:T(8,128)(2,1)S(1)} %add_convert_fusion.1), channel_id=1, source_target_pairs={{0,24},{2,26},{4,28},{6,30},{8,16},{10,18},{12,20},{14,22},{16,8},... | collective-permute-start | bytes 294920 | tf_op jit(solution)/shard_map/ppermute | solution.py:68
  91.3 10.5 %collective-permute-start.23 = (bf16[24,2048]{1,0:T(8,128)(2,1)S(1)}, bf16[24,2048]{1,0:T(8,128)(2,1)S(1)}, u32[]{:S(2)}, u32[]{:S(2)}) collective-permute-start(bf16[24,2048]{1,0:T(8,128)(2,1)S(1)} %add_convert_fusion.1), channel_id=1, source_target_pairs={{0,16},{2,18},{4,20},{6,22},{8,24},{10,26},{12,28},{14,30},{16,0},... | collective-permute-start | bytes 294920 | tf_op jit(solution)/shard_map/ppermute | solution.py:68
  91.5 10.3 %collective-permute-start.22 = (bf16[24,2048]{1,0:T(8,128)(2,1)S(1)}, bf16[24,2048]{1,0:T(8,128)(2,1)S(1)}, u32[]{:S(2)}, u32[]{:S(2)}) collective-permute-start(bf16[24,2048]{1,0:T(8,128)(2,1)S(1)} %add_convert_fusion.1), channel_id=1, source_target_pairs={{0,8},{2,10},{4,12},{6,14},{8,0},{10,2},{12,4},{14,6},{16,24},{18,... | collective-permute-start | bytes 294920 | tf_op jit(solution)/shard_map/ppermute | solution.py:68
  93.5 10.2 %collective-permute-start.29 = (f32[3,2048]{1,0:T(4,128)S(1)}, f32[3,2048]{1,0:T(4,128)S(1)}, u32[]{:S(2)}, u32[]{:S(2)}) collective-permute-start(f32[3,2048]{1,0:T(4,128)S(1)} %fusion.18), channel_id=1, source_target_pairs={{0,16},{2,18},{4,20},{6,22},{8,24},{10,26},{12,28},{14,30},{16,0},... | collective-permute-start | bytes 73736 | tf_op jit(solution)/shard_map/ppermute | solution.py:68
  101.8 11.4 %collective-permute-start.26 = (bf16[96,2048]{1,0:T(8,128)(2,1)S(1)}, bf16[96,2048]{1,0:T(8,128)(2,1)S(1)}, u32[]{:S(2)}, u32[]{:S(2)}) collective-permute-start(bf16[96,2048]{1,0:T(8,128)(2,1)S(1)} %pad_maximum_fusion.2.refs_0_), channel_id=1, source_target_pairs={{0,4},{1,3},{2,6},{3,1},{4,0},{5,7},{6,2},{7,5},{8,12},{9,11},{10,... | collective-permute-start | bytes 1179656 | tf_op jit(solution)/shard_map/ppermute | solution.py:75
  102.5 10.7 %collective-permute-start.25 = (bf16[96,2048]{1,0:T(8,128)(2,1)S(1)}, bf16[96,2048]{1,0:T(8,128)(2,1)S(1)}, u32[]{:S(2)}, u32[]{:S(2)}) collective-permute-start(bf16[96,2048]{1,0:T(8,128)(2,1)S(1)} %pad_maximum_fusion.2.refs_0_), channel_id=1, source_target_pairs={{0,2},{1,5},{2,0},{3,7},{4,6},{5,1},{6,4},{7,3},{8,10},{9,13},{10,... | collective-permute-start | bytes 1179656 | tf_op jit(solution)/shard_map/ppermute | solution.py:75
  103.7 8.7 %collective-permute-start.30 = (f32[3,2048]{1,0:T(4,128)S(1)}, f32[3,2048]{1,0:T(4,128)S(1)}, u32[]{:S(2)}, u32[]{:S(2)}) collective-permute-start(f32[3,2048]{1,0:T(4,128)S(1)} %fusion.38), channel_id=1, source_target_pairs={{0,2},{1,5},{2,0},{3,7},{4,6},{5,1},{6,4},{7,3},{8,10},{9,13},{10,... | collective-permute-start | bytes 73736 | tf_op jit(solution)/shard_map/ppermute | solution.py:75
  113.2 3.9 %collective-permute-start.31 = (f32[3,2048]{1,0:T(4,128)S(1)}, f32[3,2048]{1,0:T(4,128)S(1)}, u32[]{:S(2)}, u32[]{:S(2)}) collective-permute-start(f32[3,2048]{1,0:T(4,128)S(1)} %add.127), channel_id=1, source_target_pairs={{0,4},{1,3},{2,6},{3,1},{4,0},{5,7},{6,2},{7,5},{8,12},{9,11},{10,... | collective-permute-start | bytes 73736 | tf_op jit(solution)/shard_map/ppermute | solution.py:75
  114.0 7.8 %collective-permute-start.27 = (bf16[96,2048]{1,0:T(8,128)(2,1)S(1)}, bf16[96,2048]{1,0:T(8,128)(2,1)S(1)}, u32[]{:S(2)}, u32[]{:S(2)}) collective-permute-start(bf16[96,2048]{1,0:T(8,128)(2,1)S(1)} %collective-permute-done.25.refs_1_), channel_id=1, source_target_pairs={{0,4},{1,3},{2,6},{3,1},{4,0},{5,7},{6,2},{7,5},{8,12},{9,11},{10,... | collective-permute-start | bytes 1179656 | tf_op jit(solution)/shard_map/ppermute | solution.py:75

commit v3 on v2

--- a/solution.py
+++ b/solution.py
@@ -89,8 +89,12 @@
         quarters = [got[i * size : (i + 1) * size] for i in (0, 2, 1, 3)]
         return x.astype(F32) + jnp.concatenate(quarters).astype(F32)
 
-    def gather(own, rider=None):
-        column = jnp.concatenate([own] + [flip(own, 4 * k) for k in range(1, outer)])
+    def gather(own, rider=None, beside=None, ahead=None):
+        later, _ = lax.optimization_barrier((own, ahead))
+        along = [flip(own if k < 3 else later, 4 * k) for k in range(1, outer)]
+        if beside is not None:
+            along, beside = lax.optimization_barrier((along, beside))
+        column = jnp.concatenate([own] + along)
         first, second = lax.optimization_barrier((turn(column, 0), turn(column, 1)))
         both = turn(first, 1)
         if rider is not None:
@@ -100,7 +104,7 @@
             rider += turn(rider, 0)
             rider, _ = lax.optimization_barrier((rider, first))
             rider += turn(rider, 1)
-        return (column, first, second, both), rider
+        return (column, first, second, both), rider, beside
 
     def order():
         core = lax.axis_index("narrow") if narrow == 2 else 0
@@ -122,7 +126,7 @@
         inverse_std = lax.rsqrt(variance + EPS)
         normed = (layer_in - centre_mean) * inverse_std
         hidden_in = (normed * ln_gain + ln_bias).astype(BF16)
-        grad_panel = jnp.concatenate(gather(d_out)[0])
+        grad_panel = jnp.concatenate(gather(d_out, ahead=sums)[0])
         hidden_panel = jnp.concatenate(gather(hidden_in)[0])
         back_part = lax.dot_general(
             grad_panel, w_down, (((1,), (1,)), ((), ())), preferred_element_type=F32
@@ -133,12 +137,16 @@
         act_value, slope = gelu_parts(pre_full + up_bias)
         activation = act_value.astype(BF16)
         d_hidden = (back_full * slope).astype(BF16)
-        d_normout = lax.dot_general(
-            d_hidden, w_up, (((1,), (1,)), ((), ())), preferred_element_type=F32
-        ).astype(BF16)
+
+        def norm_grads(d_hidden):
+            return lax.dot_general(
+                d_hidden, w_up, (((1,), (1,)), ((), ())), preferred_element_type=F32
+            ).astype(BF16)
+
         size = outer * rows
-        parts = [d_normout[i * size : (i + 1) * size] for i in range(4)]
-        own, first, second, both = parts
+        both = norm_grads(d_hidden[3 * size :])
+        others = norm_grads(d_hidden[: 3 * size])
+        own, first, second = [others[i * size : (i + 1) * size] for i in range(3)]
         far, near = turn(both, 1), turn(second, 1)
         back = turn((first.astype(F32) + far.astype(F32)).astype(BF16), 0)
         activation, grad_panel, _ = lax.optimization_barrier((activation, grad_panel, far))
@@ -146,17 +154,14 @@
         d_down = lax.dot_general(
             activation, grad_panel, contract_rows, preferred_element_type=F32
         ).astype(BF16)
+        back, d_down = lax.optimization_barrier((back, d_down))
+        grad_panel, _ = lax.optimization_barrier((grad_panel, back))
         d_downbias = jnp.sum(grad_panel.astype(F32), axis=0)
-        back, d_down, d_downbias = lax.optimization_barrier((back, d_down, d_downbias))
         column = own.astype(F32) + near.astype(F32) + back.astype(F32)
         blocks = [column[i * rows : (i + 1) * rows] for i in range(outer)]
-        home = [flip(blocks[k].astype(BF16), 4 * k) for k in range(1, outer)]
-        d_hidden, hidden_panel, _ = lax.optimization_barrier((d_hidden, hidden_panel, back))
-        d_up = lax.dot_general(
-            hidden_panel, d_hidden, contract_rows, preferred_element_type=F32
-        ).astype(BF16)
-        d_upbias = jnp.sum(d_hidden.astype(F32), axis=0)
-        d_up, d_upbias, home = lax.optimization_barrier((d_up, d_upbias, home))
+        blocks[1:] = [block.astype(BF16) for block in blocks[1:]]
+        later, _ = lax.optimization_barrier((blocks, d_downbias))
+        home = [flip((blocks if k < 3 else later)[k], 4 * k) for k in range(1, outer)]
         own_sum = sum([block.astype(F32) for block in home], blocks[0])
 
         scaled = own_sum * ln_gain
@@ -174,7 +179,13 @@
         mine = jnp.where(lane == lax.axis_index("wide"), patch_index.astype(F32)[None], 0.0)
         mine = jnp.pad(mine.reshape(-1), (0, depth * cols - tokens)).reshape(depth, cols)
         rider = jnp.concatenate([jnp.stack([gain_term, bias_term]), mine])
-        pos_pieces, rider = gather(summed_grad, rider)
+        d_hidden, hidden_panel, summed_grad = lax.optimization_barrier((d_hidden, hidden_panel, summed_grad))
+        d_up = lax.dot_general(
+            hidden_panel, d_hidden, contract_rows, preferred_element_type=F32
+        ).astype(BF16)
+        d_upbias = jnp.sum(d_hidden.astype(F32), axis=0)
+        rider, _ = lax.optimization_barrier((rider, summed_grad))
+        pos_pieces, rider, (d_up, d_upbias) = gather(summed_grad, rider, (d_up, d_upbias))
         d_gain, d_lnbias = rider[0], rider[1]
         indices = rider[2:].reshape(-1)[:tokens].astype(jnp.int32).reshape(wide, rows)
         indices = jnp.take(indices, order(), axis=0, mode="clip").reshape(-1)

time: 125 us -> 121 us (0.968)
  starting transfers between devices: 38.8 us -> 43 us
  other arithmetic: 8.95 us -> 5.22 us
  waiting for transfers between devices: 50.7 us -> 47.1 us
  local copies, waits for them, and re-layouts: 4.89 us -> 3.03 us
    ppermute x14, starting transfers between devices: 22 us -> 25 us  [flip(): return lax.ppermute(x, 'wide', [(i, i ^ bits) for i in range(wide)])]
    ppermute x14, waiting for transfers between devices: 14.7 us -> 12.5 us  [flip(): return lax.ppermute(x, 'wide', [(i, i ^ bits) for i in range(wide)])]
    ppermute x14, waiting for transfers between devices: 32.8 us -> 31.1 us  [turn(): return lax.ppermute(x, ('wide', 'narrow'), pairs)]
    reduce_sum x1, other arithmetic: 2.26 us -> 0.85 us  [on_device(): d_downbias = jnp.sum(grad_panel.astype(F32), axis=0)]
    dot_general x1 -> x2, matrix products: 1.84 us -> 2.82 us  [norm_grads(): lax.dot_general(d_hidden, w_up, (((1,), (1,)), ((), ())), preferred_eleme...]
  transfers between devices with their start and end apart: 32 -> 32, of which waited for: 16 -> 19; matrix products, arithmetic and copies ran while one was open for 19% -> 17% of each run, Pallas kernels for 0% -> 0%
where the time goes in v3:
time: 121 us; the launch traced here: 120 us
  waiting for transfers between devices  47.1 us (39%)
  starting transfers between devices  43 us (36%)
  matrix products  18.4 us (15%)
  other arithmetic  5.22 us (4%)
  local copies, waits for them, and re-layouts  3.03 us (3%)
  Pallas kernels  2.61 us (2%)
    ppermute x14, waiting for transfers between devices, turn(): return lax.ppermute(x, ('wide', 'narrow'), pairs)  31.1 us
    ppermute x14, starting transfers between devices, flip(): return lax.ppermute(x, 'wide', [(i, i ^ bits) for i in range(wide)])  25 us
    ppermute x14, starting transfers between devices, turn(): return lax.ppermute(x, ('wide', 'narrow'), pairs)  17.8 us
    ppermute x14, waiting for transfers between devices, flip(): return lax.ppermute(x, 'wide', [(i, i ^ bits) for i in range(wide)])  12.5 us
    dot_general x1, matrix products, on_device(): lax.dot_general(hidden_panel, d_hidden, contract_rows, preferred_element_...  4.42 us
    dot_general x1, matrix products, on_device(): lax.dot_general(activation, grad_panel, contract_rows, preferred_element_...  4.41 us
    ppermute x4, waiting for transfers between devices, other_core(): return lax.ppermute(x, 'narrow', [(0, 1), (1, 0)])  3.52 us
    dot_general x2, matrix products, norm_grads(): lax.dot_general(d_hidden, w_up, (((1,), (1,)), ((), ())), preferred_eleme...  2.82 us
  transfers between devices with their start and end apart: 32, of which 19 were waited for; matrix products, arithmetic and copies ran while one was open for 17% of the time, Pallas kernels for 0%

profile of v3, /device:TPU:0, one launch (start us, length us, event | category | flops | bytes accessed | tf_op | source)
XLA Modules:
  0.0 120.5 jit_solution(1387409755676355091)
XLA Ops:
  0.7 4.1 %collective-permute-start.1 = (bf16[24,2048]{1,0:T(8,128)(2,1)}, bf16[24,2048]{1,0:T(8,128)(2,1)S(1)}, u32[]{:S(2)}, u32[]{:S(2)}) collective-permute-start(bf16[24,2048]{1,0:T(8,128)(2,1)} %param.19), channel_id=1, source_target_pairs={{0,16},{2,18},{4,20},{6,22},{8,24},{10,26},{12,28},{14,30},{16,0},... | collective-permute-start | bytes 294920 | tf_op jit(solution)/shard_map/ppermute | solution.py:68
  4.8 1.6 %collective-permute-start = (bf16[24,2048]{1,0:T(8,128)(2,1)}, bf16[24,2048]{1,0:T(8,128)(2,1)S(1)}, u32[]{:S(2)}, u32[]{:S(2)}) collective-permute-start(bf16[24,2048]{1,0:T(8,128)(2,1)} %param.19), channel_id=1, source_target_pairs={{0,8},{2,10},{4,12},{6,14},{8,0},{10,2},{12,4},{14,6},{16,24},{18,... | collective-permute-start | bytes 294920 | tf_op jit(solution)/shard_map/ppermute | solution.py:68
  6.4 1.3 %fusion.18 = (f32[24]{0:T(128)S(1)}, f32[24]{0:T(128)S(1)}, f32[24,2048]{1,0:T(8,128)S(1)}) fusion(bf16[256,2048]{1,0:T(8,128)(2,1)S(1)} %copy-done, s32[24]{0:T(128)} %param.12, bf16[24,2048]{1,0:T(8,128)(2,1)} %param.11), kind=kOutput, calls=%fused_computation.82 | convolution fusion | flops 25429968 | bytes 1343776 | tf_op jit(solution)/shard_map/dot_general | solution.py:120
  8.4 0.9 constant_dynamic-update-slice_fusion.3
  9.5 1.4 %collective-permute-start.9 = (bf16[24,2048]{1,0:T(8,128)(2,1)S(1)}, bf16[24,2048]{1,0:T(8,128)(2,1)S(1)}, u32[]{:S(2)}, u32[]{:S(2)}) collective-permute-start(bf16[24,2048]{1,0:T(8,128)(2,1)S(1)} %get-tuple-element.66), channel_id=1, source_target_pairs={{0,16},{2,18},{4,20},{6,22},{8,24},{10,26},{12,28},{14,30},{16,0},... | collective-permute-start | bytes 294920 | tf_op jit(solution)/shard_map/ppermute | solution.py:68
  10.9 2.5 %collective-permute-start.8 = (bf16[24,2048]{1,0:T(8,128)(2,1)S(1)}, bf16[24,2048]{1,0:T(8,128)(2,1)S(1)}, u32[]{:S(2)}, u32[]{:S(2)}) collective-permute-start(bf16[24,2048]{1,0:T(8,128)(2,1)S(1)} %get-tuple-element.66), channel_id=1, source_target_pairs={{0,8},{2,10},{4,12},{6,14},{8,0},{10,2},{12,4},{14,6},{16,24},{18,... | collective-permute-start | bytes 294920 | tf_op jit(solution)/shard_map/ppermute | solution.py:68
  14.0 1.5 %collective-permute-done.2 = bf16[24,2048]{1,0:T(8,128)(2,1)S(1)} collective-permute-done((bf16[24,2048]{1,0:T(8,128)(2,1)}, bf16[24,2048]{1,0:T(8,128)(2,1)S(1)}, u32[]{:S(2)}, u32[]{:S(2)}) %collective-permute-start.2) | collective-permute-done | bytes 98336 | tf_op jit(solution)/shard_map/ppermute | solution.py:68
  15.5 1.6 %collective-permute-start.4 = (bf16[96,2048]{1,0:T(8,128)(2,1)S(1)}, bf16[96,2048]{1,0:T(8,128)(2,1)S(1)}, u32[]{:S(2)}, u32[]{:S(2)}) collective-permute-start(bf16[96,2048]{1,0:T(8,128)(2,1)S(1)} %get-tuple-element.80), channel_id=1, source_target_pairs={{0,4},{1,3},{2,6},{3,1},{4,0},{5,7},{6,2},{7,5},{8,12},{9,11},{10,... | collective-permute-start | bytes 1179656 | tf_op jit(solution)/shard_map/ppermute | solution.py:75
  17.1 1.5 %collective-permute-start.3 = (bf16[96,2048]{1,0:T(8,128)(2,1)S(1)}, bf16[96,2048]{1,0:T(8,128)(2,1)S(1)}, u32[]{:S(2)}, u32[]{:S(2)}) collective-permute-start(bf16[96,2048]{1,0:T(8,128)(2,1)S(1)} %get-tuple-element.80), channel_id=1, source_target_pairs={{0,2},{1,5},{2,0},{3,7},{4,6},{5,1},{6,4},{7,3},{8,10},{9,13},{10,... | collective-permute-start | bytes 1179656 | tf_op jit(solution)/shard_map/ppermute | solution.py:75
  18.6 2.8 %collective-permute-done.10 = bf16[24,2048]{1,0:T(8,128)(2,1)S(1)} collective-permute-done((bf16[24,2048]{1,0:T(8,128)(2,1)S(1)}, bf16[24,2048]{1,0:T(8,128)(2,1)S(1)}, u32[]{:S(2)}, u32[]{:S(2)}) %collective-permute-start.10) | collective-permute-done | bytes 98336 | tf_op jit(solution)/shard_map/ppermute | solution.py:68
  21.6 1.6 %collective-permute-start.12 = (bf16[96,2048]{1,0:T(8,128)(2,1)S(1)}, bf16[96,2048]{1,0:T(8,128)(2,1)S(1)}, u32[]{:S(2)}, u32[]{:S(2)}) collective-permute-start(bf16[96,2048]{1,0:T(8,128)(2,1)S(1)} %pad_maximum_fusion.1), channel_id=1, source_target_pairs={{0,4},{1,3},{2,6},{3,1},{4,0},{5,7},{6,2},{7,5},{8,12},{9,11},{10,... | collective-permute-start | bytes 1179656 | tf_op jit(solution)/shard_map/ppermute | solution.py:75
  23.1 1.5 %collective-permute-start.11 = (bf16[96,2048]{1,0:T(8,128)(2,1)S(1)}, bf16[96,2048]{1,0:T(8,128)(2,1)S(1)}, u32[]{:S(2)}, u32[]{:S(2)}) collective-permute-start(bf16[96,2048]{1,0:T(8,128)(2,1)S(1)} %pad_maximum_fusion.1), channel_id=1, source_target_pairs={{0,2},{1,5},{2,0},{3,7},{4,6},{5,1},{6,4},{7,3},{8,10},{9,13},{10,... | collective-permute-start | bytes 1179656 | tf_op jit(solution)/shard_map/ppermute | solution.py:75
  24.7 2.9 %collective-permute-done.4 = bf16[96,2048]{1,0:T(8,128)(2,1)S(1)} collective-permute-done((bf16[96,2048]{1,0:T(8,128)(2,1)S(1)}, bf16[96,2048]{1,0:T(8,128)(2,1)S(1)}, u32[]{:S(2)}, u32[]{:S(2)}) %collective-permute-start.4) | collective-permute-done | bytes 393248 | tf_op jit(solution)/shard_map/ppermute | solution.py:75
  27.6 1.5 %collective-permute-start.5 = (bf16[96,2048]{1,0:T(8,128)(2,1)S(1)}, bf16[96,2048]{1,0:T(8,128)(2,1)S(1)}, u32[]{:S(2)}, u32[]{:S(2)}) collective-permute-start(bf16[96,2048]{1,0:T(8,128)(2,1)S(1)} %collective-permute-done.3), channel_id=1, source_target_pairs={{0,4},{1,3},{2,6},{3,1},{4,0},{5,7},{6,2},{7,5},{8,12},{9,11},{10,... | collective-permute-start | bytes 1179656 | tf_op jit(solution)/shard_map/ppermute | solution.py:75
  29.1 6.3 %collective-permute-done.12 = bf16[96,2048]{1,0:T(8,128)(2,1)S(1)} collective-permute-done((bf16[96,2048]{1,0:T(8,128)(2,1)S(1)}, bf16[96,2048]{1,0:T(8,128)(2,1)S(1)}, u32[]{:S(2)}, u32[]{:S(2)}) %collective-permute-start.12) | collective-permute-done | bytes 393248 | tf_op jit(solution)/shard_map/ppermute | solution.py:75
  35.7 1.5 %collective-permute-start.13 = (bf16[96,2048]{1,0:T(8,128)(2,1)S(1)}, bf16[96,2048]{1,0:T(8,128)(2,1)S(1)}, u32[]{:S(2)}, u32[]{:S(2)}) collective-permute-start(bf16[96,2048]{1,0:T(8,128)(2,1)S(1)} %collective-permute-done.11), channel_id=1, source_target_pairs={{0,4},{1,3},{2,6},{3,1},{4,0},{5,7},{6,2},{7,5},{8,12},{9,11},{10,... | collective-permute-start | bytes 1179656 | tf_op jit(solution)/shard_map/ppermute | solution.py:75
  37.2 2.4 %collective-permute-done.5 = bf16[96,2048]{1,0:T(8,128)(2,1)S(1)} collective-permute-done((bf16[96,2048]{1,0:T(8,128)(2,1)S(1)}, bf16[96,2048]{1,0:T(8,128)(2,1)S(1)}, u32[]{:S(2)}, u32[]{:S(2)}) %collective-permute-start.5) | collective-permute-done | bytes 393248 | tf_op jit(solution)/shard_map/ppermute | solution.py:75
  39.7 2.7 %convolution_convert_fusion.5 = bf16[384,1024]{1,0:T(8,128)(2,1)} fusion(bf16[384,2048]{1,0:T(8,128)(2,1)S(1)} %constant_dynamic-update-slice_fusion.4, bf16[1024,2048]{1,0:T(8,128)(2,1)S(1)} %copy-done.14), kind=kOutput, calls=%fused_computation.19 | convolution fusion | flops 1611005952 | bytes 6553600 | tf_op jit(solution)/shard_map/dot_general | solution.py:131
  42.4 1.4 %collective-permute-done.13 = bf16[96,2048]{1,0:T(8,128)(2,1)S(1)} collective-permute-done((bf16[96,2048]{1,0:T(8,128)(2,1)S(1)}, bf16[96,2048]{1,0:T(8,128)(2,1)S(1)}, u32[]{:S(2)}, u32[]{:S(2)}) %collective-permute-start.13) | collective-permute-done | bytes 393248 | tf_op jit(solution)/shard_map/ppermute | solution.py:75
  43.9 2.7 %convolution_convert_fusion.4 = bf16[384,1024]{1,0:T(8,128)(2,1)} fusion(bf16[384,2048]{1,0:T(8,128)(2,1)S(1)} %constant_dynamic-update-slice_fusion.11, bf16[2048,1024]{1,0:T(8,128)(2,1)S(1)} %copy-done.1), kind=kOutput, calls=%fused_computation.18 | convolution fusion | flops 1611005952 | bytes 6553600 | tf_op jit(solution)/shard_map/dot_general | solution.py:134
  46.6 2.4 %collective-permute-done.14 = bf16[384,1024]{1,0:T(8,128)(2,1)S(1)} collective-permute-done((bf16[384,1024]{1,0:T(8,128)(2,1)}, bf16[384,1024]{1,0:T(8,128)(2,1)S(1)}, u32[]{:S(2)}, u32[]{:S(2)}) %collective-permute-start.14) | collective-permute-done | bytes 786464 | tf_op jit(solution)/shard_map/ppermute | solution.py:78
  49.2 2.6 %multiply_convert_fusion = (bf16[384,1024]{1,0:T(8,128)(2,1)S(1)}, bf16[384,1024]{1,0:T(8,128)(2,1)S(1)}) fusion(bf16[384,1024]{1,0:T(8,128)(2,1)} %convolution_convert_fusion.4, f32[1024]{0:T(1024)S(1)} %copy-done.11, bf16[96,1024]{1,0:T(8,128)(2,1)S(1)} %get-tuple-element.70, bf16[96,1024]{1,0:T(8,128)(2,1)S(1)} %get-tuple-element.71, ...), kind=kLoop, calls=%fused_computation.15 | loop fusion | flops 12976128 | bytes 4722688 | tf_op jit(solution)/shard_map/convert_element_type | solution.py:138
  51.8 1.4 %convolution_convert_fusion.3 = bf16[96,2048]{1,0:T(8,128)(2,1)S(1)} fusion(bf16[2048,1024]{1,0:T(8,128)(2,1)S(1)} %copy-done.2, bf16[384,1024]{1,0:T(8,128)(2,1)S(1)} %get-tuple-element.44), kind=kOutput, calls=%fused_computation.6 | convolution fusion | flops 402849792 | bytes 4784128 | tf_op jit(solution)/shard_map/dot_general | solution.py:142
  53.2 1.6 %collective-permute-start.16 = (bf16[96,2048]{1,0:T(8,128)(2,1)S(1)}, bf16[96,2048]{1,0:T(8,128)(2,1)S(1)}, u32[]{:S(2)}, u32[]{:S(2)}) collective-permute-start(bf16[96,2048]{1,0:T(8,128)(2,1)S(1)} %convolution_convert_fusion.3), channel_id=1, source_target_pairs={{0,4},{1,3},{2,6},{3,1},{4,0},{5,7},{6,2},{7,5},{8,12},{9,11},{10,... | collective-permute-start | bytes 1179656 | tf_op jit(solution)/shard_map/ppermute | solution.py:75
  54.8 1.4 %convolution_convert_fusion.2 = bf16[288,2048]{1,0:T(8,128)(2,1)S(1)} fusion(bf16[2048,1024]{1,0:T(8,128)(2,1)S(1)} %copy-done.2, bf16[384,1024]{1,0:T(8,128)(2,1)S(1)} %get-tuple-element.44), kind=kOutput, calls=%fused_computation.4 | convolution fusion | flops 1208549376 | bytes 5963776 | tf_op jit(solution)/shard_map/dot_general | solution.py:142
  56.9 4.2 %collective-permute-done.16 = bf16[96,2048]{1,0:T(8,128)(2,1)S(1)} collective-permute-done((bf16[96,2048]{1,0:T(8,128)(2,1)S(1)}, bf16[96,2048]{1,0:T(8,128)(2,1)S(1)}, u32[]{:S(2)}, u32[]{:S(2)}) %collective-permute-start.16) | collective-permute-done | bytes 393248 | tf_op jit(solution)/shard_map/ppermute | solution.py:75
  61.2 1.1 collective-permute-start.17
  62.3 4.4 %convolution_convert_fusion.1 = bf16[1024,2048]{1,0:T(8,128)(2,1)} fusion(bf16[384,1024]{1,0:T(8,128)(2,1)S(1)} %get-tuple-element.37, bf16[384,2048]{1,0:T(8,128)(2,1)S(1)} %copy-done.4), kind=kOutput, calls=%fused_computation.2 | convolution fusion | flops 1612709888 | bytes 6553600 | tf_op jit(solution)/shard_map/dot_general | solution.py:154
  66.7 2.3 %collective-permute-done.17 = bf16[96,2048]{1,0:T(8,128)(2,1)S(1)} collective-permute-done((bf16[96,2048]{1,0:T(8,128)(2,1)S(1)}, bf16[96,2048]{1,0:T(8,128)(2,1)S(1)}, u32[]{:S(2)}, u32[]{:S(2)}) %collective-permute-start.17) | collective-permute-done | bytes 393248 | tf_op jit(solution)/shard_map/ppermute | solution.py:75
  69.2 0.9 convert_reduce_fusion
  70.1 5.9 %collective-permute-start.19 = (bf16[24,2048]{1,0:T(8,128)(2,1)S(1)}, bf16[24,2048]{1,0:T(8,128)(2,1)S(1)}, u32[]{:S(2)}, u32[]{:S(2)}) collective-permute-start(bf16[24,2048]{1,0:T(8,128)(2,1)S(1)} %get-tuple-element.78), channel_id=1, source_target_pairs={{0,16},{2,18},{4,20},{6,22},{8,24},{10,26},{12,28},{14,30},{16,0},... | collective-permute-start | bytes 294920 | tf_op jit(solution)/shard_map/ppermute | solution.py:68
  76.0 1.5 %collective-permute-start.20 = (bf16[24,2048]{1,0:T(8,128)(2,1)S(1)}, bf16[24,2048]{1,0:T(8,128)(2,1)S(1)}, u32[]{:S(2)}, u32[]{:S(2)}) collective-permute-start(bf16[24,2048]{1,0:T(8,128)(2,1)S(1)} %get-tuple-element.41), channel_id=1, source_target_pairs={{0,24},{2,26},{4,28},{6,30},{8,16},{10,18},{12,20},{14,22},{16,8},... | collective-permute-start | bytes 294920 | tf_op jit(solution)/shard_map/ppermute | solution.py:68
  77.6 5.1 %collective-permute-done.20 = bf16[24,2048]{1,0:T(8,128)(2,1)S(1)} collective-permute-done((bf16[24,2048]{1,0:T(8,128)(2,1)S(1)}, bf16[24,2048]{1,0:T(8,128)(2,1)S(1)}, u32[]{:S(2)}, u32[]{:S(2)}) %collective-permute-start.20) | collective-permute-done | bytes 98336 | tf_op jit(solution)/shard_map/ppermute | solution.py:68
  82.7 1.7 %collective-permute-done.18 = bf16[24,2048]{1,0:T(8,128)(2,1)S(1)} collective-permute-done((bf16[24,2048]{1,0:T(8,128)(2,1)S(1)}, bf16[24,2048]{1,0:T(8,128)(2,1)S(1)}, u32[]{:S(2)}, u32[]{:S(2)}) %collective-permute-start.18) | collective-permute-done | bytes 98336 | tf_op jit(solution)/shard_map/ppermute | solution.py:68
  84.7 1.1 collective-permute-done.21
  86.3 3.0 %collective-permute-start.22 = (bf16[24,2048]{1,0:T(8,128)(2,1)S(1)}, bf16[24,2048]{1,0:T(8,128)(2,1)S(1)}, u32[]{:S(2)}, u32[]{:S(2)}) collective-permute-start(bf16[24,2048]{1,0:T(8,128)(2,1)S(1)} %add_convert_fusion.1), channel_id=1, source_target_pairs={{0,8},{2,10},{4,12},{6,14},{8,0},{10,2},{12,4},{14,6},{16,24},{18,... | collective-permute-start | bytes 294920 | tf_op jit(solution)/shard_map/ppermute | solution.py:68
  89.4 1.8 %collective-permute-start.24 = (bf16[24,2048]{1,0:T(8,128)(2,1)S(1)}, bf16[24,2048]{1,0:T(8,128)(2,1)S(1)}, u32[]{:S(2)}, u32[]{:S(2)}) collective-permute-start(bf16[24,2048]{1,0:T(8,128)(2,1)S(1)} %add_convert_fusion.1), channel_id=1, source_target_pairs={{0,24},{2,26},{4,28},{6,30},{8,16},{10,18},{12,20},{14,22},{16,8},... | collective-permute-start | bytes 294920 | tf_op jit(solution)/shard_map/ppermute | solution.py:68
  91.1 4.4 %convolution_convert_fusion = bf16[2048,1024]{1,0:T(8,128)(2,1)} fusion(bf16[384,2048]{1,0:T(8,128)(2,1)S(1)} %copy-done.10, bf16[384,1024]{1,0:T(8,128)(2,1)S(1)} %get-tuple-element.44), kind=kOutput, calls=%fused_computation.1 | convolution fusion | flops 1612709888 | bytes 6553600 | tf_op jit(solution)/shard_map/dot_general | solution.py:183
  96.3 1.8 %collective-permute-start.29 = (f32[3,2048]{1,0:T(4,128)S(1)}, f32[3,2048]{1,0:T(4,128)S(1)}, u32[]{:S(2)}, u32[]{:S(2)}) collective-permute-start(f32[3,2048]{1,0:T(4,128)S(1)} %add.125), channel_id=1, source_target_pairs={{0,16},{2,18},{4,20},{6,22},{8,24},{10,26},{12,28},{14,30},{16,0},... | collective-permute-start | bytes 73736 | tf_op jit(solution)/shard_map/ppermute | solution.py:68
  98.8 1.4 %collective-permute-start.25 = (bf16[96,2048]{1,0:T(8,128)(2,1)S(1)}, bf16[96,2048]{1,0:T(8,128)(2,1)S(1)}, u32[]{:S(2)}, u32[]{:S(2)}) collective-permute-start(bf16[96,2048]{1,0:T(8,128)(2,1)S(1)} %constant_dynamic-update-slice_fusion.18.refs_0_), channel_id=1, source_target_pairs={{0,2},{1,5},{2,0},{3,7},{4,6},{5,1},{6,4},{7,3},{8,10},{9,13},{10,... | collective-permute-start | bytes 1179656 | tf_op jit(solution)/shard_map/ppermute | solution.py:75
  100.2 1.3 %collective-permute-done.29 = f32[3,2048]{1,0:T(4,128)S(1)} collective-permute-done((f32[3,2048]{1,0:T(4,128)S(1)}, f32[3,2048]{1,0:T(4,128)S(1)}, u32[]{:S(2)}, u32[]{:S(2)}) %collective-permute-start.29) | collective-permute-done | bytes 24608 | tf_op jit(solution)/shard_map/ppermute | solution.py:68
  101.5 1.3 %collective-permute-start.30 = (f32[3,2048]{1,0:T(4,128)S(1)}, f32[3,2048]{1,0:T(4,128)S(1)}, u32[]{:S(2)}, u32[]{:S(2)}) collective-permute-start(f32[3,2048]{1,0:T(4,128)S(1)} %add.126), channel_id=1, source_target_pairs={{0,2},{1,5},{2,0},{3,7},{4,6},{5,1},{6,4},{7,3},{8,10},{9,13},{10,... | collective-permute-start | bytes 73736 | tf_op jit(solution)/shard_map/ppermute | solution.py:75
  102.9 5.4 %collective-permute-done.30 = f32[3,2048]{1,0:T(4,128)S(1)} collective-permute-done((f32[3,2048]{1,0:T(4,128)S(1)}, f32[3,2048]{1,0:T(4,128)S(1)}, u32[]{:S(2)}, u32[]{:S(2)}) %collective-permute-start.30) | collective-permute-done | bytes 24608 | tf_op jit(solution)/shard_map/ppermute | solution.py:75
  108.4 1.2 collective-permute-done.26.refs_2_
  110.1 1.5 %collective-permute-start.27 = (bf16[96,2048]{1,0:T(8,128)(2,1)S(1)}, bf16[96,2048]{1,0:T(8,128)(2,1)S(1)}, u32[]{:S(2)}, u32[]{:S(2)}) collective-permute-start(bf16[96,2048]{1,0:T(8,128)(2,1)S(1)} %collective-permute-done.25.refs_1_), channel_id=1, source_target_pairs={{0,4},{1,3},{2,6},{3,1},{4,0},{5,7},{6,2},{7,5},{8,12},{9,11},{10,... | collective-permute-start | bytes 1179656 | tf_op jit(solution)/shard_map/ppermute | solution.py:75
  111.6 1.9 %collective-permute-done.31 = f32[3,2048]{1,0:T(4,128)S(1)} collective-permute-done((f32[3,2048]{1,0:T(4,128)S(1)}, f32[3,2048]{1,0:T(4,128)S(1)}, u32[]{:S(2)}, u32[]{:S(2)}) %collective-permute-start.31) | collective-permute-done | bytes 24608 | tf_op jit(solution)/shard_map/ppermute | solution.py:75
  114.9 3.0 %collective-permute-done.27.refs_3_ = bf16[96,2048]{1,0:T(8,128)(2,1)S(1)} collective-permute-done((bf16[96,2048]{1,0:T(8,128)(2,1)S(1)}, bf16[96,2048]{1,0:T(8,128)(2,1)S(1)}, u32[]{:S(2)}, u32[]{:S(2)}) %collective-permute-start.27) | collective-permute-done | bytes 393248 | tf_op jit(solution)/shard_map/ppermute | solution.py:75
  117.9 2.6 %place.1 = f32[256,2048]{1,0:T(8,128)} custom-call(bf16[96,2048]{1,0:T(8,128)(2,1)S(1)} %constant_dynamic-update-slice_fusion.18.refs_0_, bf16[96,2048]{1,0:T(8,128)(2,1)S(1)} %collective-permute-done.25.refs_1_, bf16[96,2048]{1,0:T(8,128)(2,1)S(1)} %collective-permute-done.26.refs_2_, bf16[96,2048]{1,0:T(8,128)(2,1)S(1)} %collective-permute-done.27.refs_3_, ...), custom_call_target="tpu_custom_call" | custom-call | flops 402653184 | bytes 1572864 | tf_op jit(solution)/shard_map/place/pallas_call | solution.py:52
  (110 shorter events, 7.7 us)
Async XLA Ops:
  0.6 5.7 %copy-start = (bf16[256,2048]{1,0:T(8,128)(2,1)S(1)}, bf16[256,2048]{1,0:T(8,128)(2,1)}, u32[]{:S(2)}) copy-start(bf16[256,2048]{1,0:T(8,128)(2,1)} %param.13) | copy-start | bytes 3145732
  0.6 8.7 %copy-start.7 = (f32[2048]{0:T(1024)S(1)}, f32[2048]{0:T(1024)}, u32[]{:S(2)}) copy-start(f32[2048]{0:T(1024)} %param.14) | copy-start | bytes 24580
  0.7 8.7 %copy-start.8 = (f32[2048]{0:T(1024)S(1)}, f32[2048]{0:T(1024)}, u32[]{:S(2)}) copy-start(f32[2048]{0:T(1024)} %param.15) | copy-start | bytes 24580
  0.7 13.3 %collective-permute-start.1 = (bf16[24,2048]{1,0:T(8,128)(2,1)}, bf16[24,2048]{1,0:T(8,128)(2,1)S(1)}, u32[]{:S(2)}, u32[]{:S(2)}) collective-permute-start(bf16[24,2048]{1,0:T(8,128)(2,1)} %param.19), channel_id=1, source_target_pairs={{0,16},{2,18},{4,20},{6,22},{8,24},{10,26},{12,28},{14,30},{16,0},... | collective-permute-start | bytes 294920 | tf_op jit(solution)/shard_map/ppermute | solution.py:68
  4.8 8.6 %collective-permute-start = (bf16[24,2048]{1,0:T(8,128)(2,1)}, bf16[24,2048]{1,0:T(8,128)(2,1)S(1)}, u32[]{:S(2)}, u32[]{:S(2)}) collective-permute-start(bf16[24,2048]{1,0:T(8,128)(2,1)} %param.19), channel_id=1, source_target_pairs={{0,8},{2,10},{4,12},{6,14},{8,0},{10,2},{12,4},{14,6},{16,24},{18,... | collective-permute-start | bytes 294920 | tf_op jit(solution)/shard_map/ppermute | solution.py:68
  7.7 1.7 %collective-permute-start.7 = (f32[2,24]{1,0:T(2,128)S(1)}, f32[2,24]{1,0:T(2,128)S(1)}, u32[]{:S(2)}, u32[]{:S(2)}) collective-permute-start(f32[2,24]{1,0:T(2,128)S(1)} %pad_maximum_fusion.3), channel_id=1, source_target_pairs={{0,1},{1,0},{2,3},{3,2},{4,5},{5,4},{6,7},{7,6},{8,9},{9,8},{10,11... | collective-permute-start | bytes 584 | tf_op jit(solution)/shard_map/ppermute | solution.py:78
  7.8 7.8 %collective-permute-start.2 = (bf16[24,2048]{1,0:T(8,128)(2,1)}, bf16[24,2048]{1,0:T(8,128)(2,1)S(1)}, u32[]{:S(2)}, u32[]{:S(2)}) collective-permute-start(bf16[24,2048]{1,0:T(8,128)(2,1)} %param.19), channel_id=1, source_target_pairs={{0,24},{2,26},{4,28},{6,30},{8,16},{10,18},{12,20},{14,22},{16,8},... | collective-permute-start | bytes 294920 | tf_op jit(solution)/shard_map/ppermute | solution.py:68
  9.5 12.0 %collective-permute-start.9 = (bf16[24,2048]{1,0:T(8,128)(2,1)S(1)}, bf16[24,2048]{1,0:T(8,128)(2,1)S(1)}, u32[]{:S(2)}, u32[]{:S(2)}) collective-permute-start(bf16[24,2048]{1,0:T(8,128)(2,1)S(1)} %get-tuple-element.66), channel_id=1, source_target_pairs={{0,16},{2,18},{4,20},{6,22},{8,24},{10,26},{12,28},{14,30},{16,0},... | collective-permute-start | bytes 294920 | tf_op jit(solution)/shard_map/ppermute | solution.py:68
  10.9 10.6 %collective-permute-start.8 = (bf16[24,2048]{1,0:T(8,128)(2,1)S(1)}, bf16[24,2048]{1,0:T(8,128)(2,1)S(1)}, u32[]{:S(2)}, u32[]{:S(2)}) collective-permute-start(bf16[24,2048]{1,0:T(8,128)(2,1)S(1)} %get-tuple-element.66), channel_id=1, source_target_pairs={{0,8},{2,10},{4,12},{6,14},{8,0},{10,2},{12,4},{14,6},{16,24},{18,... | collective-permute-start | bytes 294920 | tf_op jit(solution)/shard_map/ppermute | solution.py:68
  13.4 8.0 %collective-permute-start.10 = (bf16[24,2048]{1,0:T(8,128)(2,1)S(1)}, bf16[24,2048]{1,0:T(8,128)(2,1)S(1)}, u32[]{:S(2)}, u32[]{:S(2)}) collective-permute-start(bf16[24,2048]{1,0:T(8,128)(2,1)S(1)} %get-tuple-element.66), channel_id=1, source_target_pairs={{0,24},{2,26},{4,28},{6,30},{8,16},{10,18},{12,20},{14,22},{16,8},... | collective-permute-start | bytes 294920 | tf_op jit(solution)/shard_map/ppermute | solution.py:68
  15.5 12.0 %collective-permute-start.4 = (bf16[96,2048]{1,0:T(8,128)(2,1)S(1)}, bf16[96,2048]{1,0:T(8,128)(2,1)S(1)}, u32[]{:S(2)}, u32[]{:S(2)}) collective-permute-start(bf16[96,2048]{1,0:T(8,128)(2,1)S(1)} %get-tuple-element.80), channel_id=1, source_target_pairs={{0,4},{1,3},{2,6},{3,1},{4,0},{5,7},{6,2},{7,5},{8,12},{9,11},{10,... | collective-permute-start | bytes 1179656 | tf_op jit(solution)/shard_map/ppermute | solution.py:75
  17.1 10.4 %collective-permute-start.3 = (bf16[96,2048]{1,0:T(8,128)(2,1)S(1)}, bf16[96,2048]{1,0:T(8,128)(2,1)S(1)}, u32[]{:S(2)}, u32[]{:S(2)}) collective-permute-start(bf16[96,2048]{1,0:T(8,128)(2,1)S(1)} %get-tuple-element.80), channel_id=1, source_target_pairs={{0,2},{1,5},{2,0},{3,7},{4,6},{5,1},{6,4},{7,3},{8,10},{9,13},{10,... | collective-permute-start | bytes 1179656 | tf_op jit(solution)/shard_map/ppermute | solution.py:75
  21.6 13.9 %collective-permute-start.12 = (bf16[96,2048]{1,0:T(8,128)(2,1)S(1)}, bf16[96,2048]{1,0:T(8,128)(2,1)S(1)}, u32[]{:S(2)}, u32[]{:S(2)}) collective-permute-start(bf16[96,2048]{1,0:T(8,128)(2,1)S(1)} %pad_maximum_fusion.1), channel_id=1, source_target_pairs={{0,4},{1,3},{2,6},{3,1},{4,0},{5,7},{6,2},{7,5},{8,12},{9,11},{10,... | collective-permute-start | bytes 1179656 | tf_op jit(solution)/shard_map/ppermute | solution.py:75
  23.1 12.5 %collective-permute-start.11 = (bf16[96,2048]{1,0:T(8,128)(2,1)S(1)}, bf16[96,2048]{1,0:T(8,128)(2,1)S(1)}, u32[]{:S(2)}, u32[]{:S(2)}) collective-permute-start(bf16[96,2048]{1,0:T(8,128)(2,1)S(1)} %pad_maximum_fusion.1), channel_id=1, source_target_pairs={{0,2},{1,5},{2,0},{3,7},{4,6},{5,1},{6,4},{7,3},{8,10},{9,13},{10,... | collective-permute-start | bytes 1179656 | tf_op jit(solution)/shard_map/ppermute | solution.py:75
  24.6 15.0 %copy-start.14 = (bf16[1024,2048]{1,0:T(8,128)(2,1)S(1)}, bf16[1024,2048]{1,0:T(8,128)(2,1)}, u32[]{:S(2)}) copy-start(bf16[1024,2048]{1,0:T(8,128)(2,1)} %param.18) | copy-start | bytes 12582916
  27.6 12.1 %collective-permute-start.5 = (bf16[96,2048]{1,0:T(8,128)(2,1)S(1)}, bf16[96,2048]{1,0:T(8,128)(2,1)S(1)}, u32[]{:S(2)}, u32[]{:S(2)}) collective-permute-start(bf16[96,2048]{1,0:T(8,128)(2,1)S(1)} %collective-permute-done.3), channel_id=1, source_target_pairs={{0,4},{1,3},{2,6},{3,1},{4,0},{5,7},{6,2},{7,5},{8,12},{9,11},{10,... | collective-permute-start | bytes 1179656 | tf_op jit(solution)/shard_map/ppermute | solution.py:75
  35.7 8.2 %collective-permute-start.13 = (bf16[96,2048]{1,0:T(8,128)(2,1)S(1)}, bf16[96,2048]{1,0:T(8,128)(2,1)S(1)}, u32[]{:S(2)}, u32[]{:S(2)}) collective-permute-start(bf16[96,2048]{1,0:T(8,128)(2,1)S(1)} %collective-permute-done.11), channel_id=1, source_target_pairs={{0,4},{1,3},{2,6},{3,1},{4,0},{5,7},{6,2},{7,5},{8,12},{9,11},{10,... | collective-permute-start | bytes 1179656 | tf_op jit(solution)/shard_map/ppermute | solution.py:75
  39.7 2.7 %copy-start.3 = (bf16[384,2048]{1,0:T(8,128)(2,1)}, bf16[384,2048]{1,0:T(8,128)(2,1)S(1)}, u32[]{:S(2)}) copy-start(bf16[384,2048]{1,0:T(8,128)(2,1)S(1)} %constant_dynamic-update-slice_fusion.4) | copy-start | bytes 4718596
  39.7 4.2 %copy-start.1 = (bf16[2048,1024]{1,0:T(8,128)(2,1)S(1)}, bf16[2048,1024]{1,0:T(8,128)(2,1)}, u32[]{:S(2)}) copy-start(bf16[2048,1024]{1,0:T(8,128)(2,1)} %param.16) | copy-start | bytes 12582916
  42.4 4.2 %collective-permute-start.6 = (bf16[384,1024]{1,0:T(8,128)(2,1)}, bf16[384,1024]{1,0:T(8,128)(2,1)S(1)}, u32[]{:S(2)}, u32[]{:S(2)}) collective-permute-start(bf16[384,1024]{1,0:T(8,128)(2,1)} %convolution_convert_fusion.5), channel_id=1, source_target_pairs={{0,1},{1,0},{2,3},{3,2},{4,5},{5,4},{6,7},{7,6},{8,9},{9,8},{10,11... | collective-permute-start | bytes 2359304 | tf_op jit(solution)/shard_map/ppermute | solution.py:78
  43.9 2.7 %copy-start.9 = (bf16[384,2048]{1,0:T(8,128)(2,1)}, bf16[384,2048]{1,0:T(8,128)(2,1)S(1)}, u32[]{:S(2)}) copy-start(bf16[384,2048]{1,0:T(8,128)(2,1)S(1)} %constant_dynamic-update-slice_fusion.11) | copy-start | bytes 4718596
  46.6 2.5 %collective-permute-start.14 = (bf16[384,1024]{1,0:T(8,128)(2,1)}, bf16[384,1024]{1,0:T(8,128)(2,1)S(1)}, u32[]{:S(2)}, u32[]{:S(2)}) collective-permute-start(bf16[384,1024]{1,0:T(8,128)(2,1)} %convolution_convert_fusion.4), channel_id=1, source_target_pairs={{0,1},{1,0},{2,3},{3,2},{4,5},{5,4},{6,7},{7,6},{8,9},{9,8},{10,11... | collective-permute-start | bytes 2359304 | tf_op jit(solution)/shard_map/ppermute | solution.py:78
  46.6 2.6 %copy-start.11 = (f32[1024]{0:T(1024)S(1)}, f32[1024]{0:T(1024)}, u32[]{:S(2)}) copy-start(f32[1024]{0:T(1024)} %param.17) | copy-start | bytes 12292
  49.1 2.7 %copy-start.2 = (bf16[2048,1024]{1,0:T(8,128)(2,1)S(1)}, bf16[2048,1024]{1,0:T(8,128)(2,1)}, u32[]{:S(2)}) copy-start(bf16[2048,1024]{1,0:T(8,128)(2,1)} %param.16) | copy-start | bytes 12582916
  53.2 7.8 %collective-permute-start.16 = (bf16[96,2048]{1,0:T(8,128)(2,1)S(1)}, bf16[96,2048]{1,0:T(8,128)(2,1)S(1)}, u32[]{:S(2)}, u32[]{:S(2)}) collective-permute-start(bf16[96,2048]{1,0:T(8,128)(2,1)S(1)} %convolution_convert_fusion.3), channel_id=1, source_target_pairs={{0,4},{1,3},{2,6},{3,1},{4,0},{5,7},{6,2},{7,5},{8,12},{9,11},{10,... | collective-permute-start | bytes 1179656 | tf_op jit(solution)/shard_map/ppermute | solution.py:75
  56.2 6.1 %copy-start.12 = (s32[24]{0:T(128)S(1)}, s32[24]{0:T(128)}, u32[]{:S(2)}) copy-start(s32[24]{0:T(128)} %param.12) | copy-start | bytes 292
  56.2 6.1 %copy-start.4 = (bf16[384,2048]{1,0:T(8,128)(2,1)S(1)}, bf16[384,2048]{1,0:T(8,128)(2,1)}, u32[]{:S(2)}) copy-start(bf16[384,2048]{1,0:T(8,128)(2,1)} %copy-done.3) | copy-start | bytes 4718596
  56.3 12.7 %collective-permute-start.15 = (bf16[96,2048]{1,0:T(8,128)(2,1)S(1)}, bf16[96,2048]{1,0:T(8,128)(2,1)S(1)}, u32[]{:S(2)}, u32[]{:S(2)}) collective-permute-start(bf16[96,2048]{1,0:T(8,128)(2,1)S(1)} %slice.98), channel_id=1, source_target_pairs={{0,4},{1,3},{2,6},{3,1},{4,0},{5,7},{6,2},{7,5},{8,12},{9,11},{10,... | collective-permute-start | bytes 1179656 | tf_op jit(solution)/shard_map/ppermute | solution.py:75
  61.2 7.8 %collective-permute-start.17 = (bf16[96,2048]{1,0:T(8,128)(2,1)S(1)}, bf16[96,2048]{1,0:T(8,128)(2,1)S(1)}, u32[]{:S(2)}, u32[]{:S(2)}) collective-permute-start(bf16[96,2048]{1,0:T(8,128)(2,1)S(1)} %add_convert_fusion), channel_id=1, source_target_pairs={{0,2},{1,5},{2,0},{3,7},{4,6},{5,1},{6,4},{7,3},{8,10},{9,13},{10,... | collective-permute-start | bytes 1179656 | tf_op jit(solution)/shard_map/ppermute | solution.py:75
  69.2 16.7 %copy-start.5 = (bf16[24,2048]{1,0:T(8,128)(2,1)S(1)}, bf16[24,2048]{1,0:T(8,128)(2,1)}, u32[]{:S(2)}) copy-start(bf16[24,2048]{1,0:T(8,128)(2,1)} %param.19) | copy-start | bytes 294916
  70.1 12.7 %collective-permute-start.19 = (bf16[24,2048]{1,0:T(8,128)(2,1)S(1)}, bf16[24,2048]{1,0:T(8,128)(2,1)S(1)}, u32[]{:S(2)}, u32[]{:S(2)}) collective-permute-start(bf16[24,2048]{1,0:T(8,128)(2,1)S(1)} %get-tuple-element.78), channel_id=1, source_target_pairs={{0,16},{2,18},{4,20},{6,22},{8,24},{10,26},{12,28},{14,30},{16,0},... | collective-permute-start | bytes 294920 | tf_op jit(solution)/shard_map/ppermute | solution.py:68
  76.0 8.4 %collective-permute-start.18 = (bf16[24,2048]{1,0:T(8,128)(2,1)S(1)}, bf16[24,2048]{1,0:T(8,128)(2,1)S(1)}, u32[]{:S(2)}, u32[]{:S(2)}) collective-permute-start(bf16[24,2048]{1,0:T(8,128)(2,1)S(1)} %get-tuple-element.79), channel_id=1, source_target_pairs={{0,8},{2,10},{4,12},{6,14},{8,0},{10,2},{12,4},{14,6},{16,24},{18,... | collective-permute-start | bytes 294920 | tf_op jit(solution)/shard_map/ppermute | solution.py:68
  76.0 6.7 %collective-permute-start.20 = (bf16[24,2048]{1,0:T(8,128)(2,1)S(1)}, bf16[24,2048]{1,0:T(8,128)(2,1)S(1)}, u32[]{:S(2)}, u32[]{:S(2)}) collective-permute-start(bf16[24,2048]{1,0:T(8,128)(2,1)S(1)} %get-tuple-element.41), channel_id=1, source_target_pairs={{0,24},{2,26},{4,28},{6,30},{8,16},{10,18},{12,20},{14,22},{16,8},... | collective-permute-start | bytes 294920 | tf_op jit(solution)/shard_map/ppermute | solution.py:68
  77.6 13.5 %copy-start.10 = (bf16[384,2048]{1,0:T(8,128)(2,1)S(1)}, bf16[384,2048]{1,0:T(8,128)(2,1)}, u32[]{:S(2)}) copy-start(bf16[384,2048]{1,0:T(8,128)(2,1)} %copy-done.9) | copy-start | bytes 4718596
  84.6 1.2 collective-permute-start.21
  86.0 9.6 %copy-start.6 = (bf16[24,2048]{1,0:T(8,128)(2,1)}, bf16[24,2048]{1,0:T(8,128)(2,1)S(1)}, u32[]{:S(2)}) copy-start(bf16[24,2048]{1,0:T(8,128)(2,1)S(1)} %add_convert_fusion.1) | copy-start | bytes 294916
  86.0 12.1 %collective-permute-start.23 = (bf16[24,2048]{1,0:T(8,128)(2,1)S(1)}, bf16[24,2048]{1,0:T(8,128)(2,1)S(1)}, u32[]{:S(2)}, u32[]{:S(2)}) collective-permute-start(bf16[24,2048]{1,0:T(8,128)(2,1)S(1)} %add_convert_fusion.1), channel_id=1, source_target_pairs={{0,16},{2,18},{4,20},{6,22},{8,24},{10,26},{12,28},{14,30},{16,0},... | collective-permute-start | bytes 294920 | tf_op jit(solution)/shard_map/ppermute | solution.py:68
  86.3 11.8 %collective-permute-start.22 = (bf16[24,2048]{1,0:T(8,128)(2,1)S(1)}, bf16[24,2048]{1,0:T(8,128)(2,1)S(1)}, u32[]{:S(2)}, u32[]{:S(2)}) collective-permute-start(bf16[24,2048]{1,0:T(8,128)(2,1)S(1)} %add_convert_fusion.1), channel_id=1, source_target_pairs={{0,8},{2,10},{4,12},{6,14},{8,0},{10,2},{12,4},{14,6},{16,24},{18,... | collective-permute-start | bytes 294920 | tf_op jit(solution)/shard_map/ppermute | solution.py:68
  89.3 10.9 %copy-start.13 = (s32[4]{0:T(128)S(1)}, s32[4]{0:T(128)}, u32[]{:S(2)}) copy-start(s32[4]{0:T(128)} %constant.38.clone) | copy-start | bytes 52
  89.3 7.0 %collective-permute-start.28 = (f32[3,2048]{1,0:T(4,128)S(1)}, f32[3,2048]{1,0:T(4,128)S(1)}, u32[]{:S(2)}, u32[]{:S(2)}) collective-permute-start(f32[3,2048]{1,0:T(4,128)S(1)} %pad_maximum_fusion.2), channel_id=1, source_target_pairs={{0,8},{2,10},{4,12},{6,14},{8,0},{10,2},{12,4},{14,6},{16,24},{18,... | collective-permute-start | bytes 73736 | tf_op jit(solution)/shard_map/ppermute | solution.py:68
  89.4 8.7 %collective-permute-start.24 = (bf16[24,2048]{1,0:T(8,128)(2,1)S(1)}, bf16[24,2048]{1,0:T(8,128)(2,1)S(1)}, u32[]{:S(2)}, u32[]{:S(2)}) collective-permute-start(bf16[24,2048]{1,0:T(8,128)(2,1)S(1)} %add_convert_fusion.1), channel_id=1, source_target_pairs={{0,24},{2,26},{4,28},{6,30},{8,16},{10,18},{12,20},{14,22},{16,8},... | collective-permute-start | bytes 294920 | tf_op jit(solution)/shard_map/ppermute | solution.py:68
  96.3 5.2 %collective-permute-start.29 = (f32[3,2048]{1,0:T(4,128)S(1)}, f32[3,2048]{1,0:T(4,128)S(1)}, u32[]{:S(2)}, u32[]{:S(2)}) collective-permute-start(f32[3,2048]{1,0:T(4,128)S(1)} %add.125), channel_id=1, source_target_pairs={{0,16},{2,18},{4,20},{6,22},{8,24},{10,26},{12,28},{14,30},{16,0},... | collective-permute-start | bytes 73736 | tf_op jit(solution)/shard_map/ppermute | solution.py:68
  98.1 11.4 %collective-permute-start.26 = (bf16[96,2048]{1,0:T(8,128)(2,1)S(1)}, bf16[96,2048]{1,0:T(8,128)(2,1)S(1)}, u32[]{:S(2)}, u32[]{:S(2)}) collective-permute-start(bf16[96,2048]{1,0:T(8,128)(2,1)S(1)} %constant_dynamic-update-slice_fusion.18.refs_0_), channel_id=1, source_target_pairs={{0,4},{1,3},{2,6},{3,1},{4,0},{5,7},{6,2},{7,5},{8,12},{9,11},{10,... | collective-permute-start | bytes 1179656 | tf_op jit(solution)/shard_map/ppermute | solution.py:75
  98.8 10.8 %collective-permute-start.25 = (bf16[96,2048]{1,0:T(8,128)(2,1)S(1)}, bf16[96,2048]{1,0:T(8,128)(2,1)S(1)}, u32[]{:S(2)}, u32[]{:S(2)}) collective-permute-start(bf16[96,2048]{1,0:T(8,128)(2,1)S(1)} %constant_dynamic-update-slice_fusion.18.refs_0_), channel_id=1, source_target_pairs={{0,2},{1,5},{2,0},{3,7},{4,6},{5,1},{6,4},{7,3},{8,10},{9,13},{10,... | collective-permute-start | bytes 1179656 | tf_op jit(solution)/shard_map/ppermute | solution.py:75
  101.5 6.8 %collective-permute-start.30 = (f32[3,2048]{1,0:T(4,128)S(1)}, f32[3,2048]{1,0:T(4,128)S(1)}, u32[]{:S(2)}, u32[]{:S(2)}) collective-permute-start(f32[3,2048]{1,0:T(4,128)S(1)} %add.126), channel_id=1, source_target_pairs={{0,2},{1,5},{2,0},{3,7},{4,6},{5,1},{6,4},{7,3},{8,10},{9,13},{10,... | collective-permute-start | bytes 73736 | tf_op jit(solution)/shard_map/ppermute | solution.py:75
  109.6 3.9 %collective-permute-start.31 = (f32[3,2048]{1,0:T(4,128)S(1)}, f32[3,2048]{1,0:T(4,128)S(1)}, u32[]{:S(2)}, u32[]{:S(2)}) collective-permute-start(f32[3,2048]{1,0:T(4,128)S(1)} %add.127), channel_id=1, source_target_pairs={{0,4},{1,3},{2,6},{3,1},{4,0},{5,7},{6,2},{7,5},{8,12},{9,11},{10,... | collective-permute-start | bytes 73736 | tf_op jit(solution)/shard_map/ppermute | solution.py:75
  110.1 7.8 %collective-permute-start.27 = (bf16[96,2048]{1,0:T(8,128)(2,1)S(1)}, bf16[96,2048]{1,0:T(8,128)(2,1)S(1)}, u32[]{:S(2)}, u32[]{:S(2)}) collective-permute-start(bf16[96,2048]{1,0:T(8,128)(2,1)S(1)} %collective-permute-done.25.refs_1_), channel_id=1, source_target_pairs={{0,4},{1,3},{2,6},{3,1},{4,0},{5,7},{6,2},{7,5},{8,12},{9,11},{10,... | collective-permute-start | bytes 1179656 | tf_op jit(solution)/shard_map/ppermute | solution.py:75

commit v4 on v3

--- a/solution.py
+++ b/solution.py
@@ -154,9 +154,8 @@
         d_down = lax.dot_general(
             activation, grad_panel, contract_rows, preferred_element_type=F32
         ).astype(BF16)
-        back, d_down = lax.optimization_barrier((back, d_down))
-        grad_panel, _ = lax.optimization_barrier((grad_panel, back))
         d_downbias = jnp.sum(grad_panel.astype(F32), axis=0)
+        back, d_down, d_downbias = lax.optimization_barrier((back, d_down, d_downbias))
         column = own.astype(F32) + near.astype(F32) + back.astype(F32)
         blocks = [column[i * rows : (i + 1) * rows] for i in range(outer)]
         blocks[1:] = [block.astype(BF16) for block in blocks[1:]]

time: 121 us -> 120 us (level)
  transfers between devices with their start and end apart: 32 -> 32, of which waited for: 19 -> 19; matrix products, arithmetic and copies ran while one was open for 17% -> 18% of each run, Pallas kernels for 0% -> 0%
where the time goes in v4:
time: 120 us
  waiting for transfers between devices  46.2 us (38%)
  starting transfers between devices  43.2 us (36%)
  matrix products  18.4 us (15%)
  other arithmetic  5.22 us (4%)
  local copies, waits for them, and re-layouts  3.03 us (3%)
  Pallas kernels  2.6 us (2%)
    ppermute x14, waiting for transfers between devices, turn(): return lax.ppermute(x, ('wide', 'narrow'), pairs)  30.3 us
    ppermute x14, starting transfers between devices, flip(): return lax.ppermute(x, 'wide', [(i, i ^ bits) for i in range(wide)])  25.2 us
    ppermute x14, starting transfers between devices, turn(): return lax.ppermute(x, ('wide', 'narrow'), pairs)  17.8 us
    ppermute x14, waiting for transfers between devices, flip(): return lax.ppermute(x, 'wide', [(i, i ^ bits) for i in range(wide)])  12.4 us
    dot_general x1, matrix products, on_device(): lax.dot_general(hidden_panel, d_hidden, contract_rows, preferred_element_...  4.42 us
    dot_general x1, matrix products, on_device(): lax.dot_general(activation, grad_panel, contract_rows, preferred_element_...  4.41 us
    ppermute x4, waiting for transfers between devices, other_core(): return lax.ppermute(x, 'narrow', [(0, 1), (1, 0)])  3.47 us
    dot_general x2, matrix products, norm_grads(): lax.dot_general(d_hidden, w_up, (((1,), (1,)), ((), ())), preferred_eleme...  2.83 us
  transfers between devices with their start and end apart: 32, of which 19 were waited for; matrix products, arithmetic and copies ran while one was open for 18% of the time, Pallas kernels for 0%

profile of v4, /device:TPU:0, one launch (start us, length us, event | category | flops | bytes accessed | tf_op | source)
XLA Modules:
  0.0 119.7 jit_solution(3957926953931016316)
XLA Ops:
  0.7 4.1 %collective-permute-start.1 = (bf16[24,2048]{1,0:T(8,128)(2,1)}, bf16[24,2048]{1,0:T(8,128)(2,1)S(1)}, u32[]{:S(2)}, u32[]{:S(2)}) collective-permute-start(bf16[24,2048]{1,0:T(8,128)(2,1)} %param.19), channel_id=1, source_target_pairs={{0,16},{2,18},{4,20},{6,22},{8,24},{10,26},{12,28},{14,30},{16,0},... | collective-permute-start | bytes 294920 | tf_op jit(solution)/shard_map/ppermute | solution.py:68
  4.8 1.6 %collective-permute-start = (bf16[24,2048]{1,0:T(8,128)(2,1)}, bf16[24,2048]{1,0:T(8,128)(2,1)S(1)}, u32[]{:S(2)}, u32[]{:S(2)}) collective-permute-start(bf16[24,2048]{1,0:T(8,128)(2,1)} %param.19), channel_id=1, source_target_pairs={{0,8},{2,10},{4,12},{6,14},{8,0},{10,2},{12,4},{14,6},{16,24},{18,... | collective-permute-start | bytes 294920 | tf_op jit(solution)/shard_map/ppermute | solution.py:68
  6.4 1.3 %fusion.18 = (f32[24]{0:T(128)S(1)}, f32[24]{0:T(128)S(1)}, f32[24,2048]{1,0:T(8,128)S(1)}) fusion(bf16[256,2048]{1,0:T(8,128)(2,1)S(1)} %copy-done, s32[24]{0:T(128)} %param.12, bf16[24,2048]{1,0:T(8,128)(2,1)} %param.11), kind=kOutput, calls=%fused_computation.82 | convolution fusion | flops 25429968 | bytes 1343776 | tf_op jit(solution)/shard_map/dot_general | solution.py:120
  8.4 0.9 constant_dynamic-update-slice_fusion.3
  9.5 1.4 %collective-permute-start.9 = (bf16[24,2048]{1,0:T(8,128)(2,1)S(1)}, bf16[24,2048]{1,0:T(8,128)(2,1)S(1)}, u32[]{:S(2)}, u32[]{:S(2)}) collective-permute-start(bf16[24,2048]{1,0:T(8,128)(2,1)S(1)} %get-tuple-element.66), channel_id=1, source_target_pairs={{0,16},{2,18},{4,20},{6,22},{8,24},{10,26},{12,28},{14,30},{16,0},... | collective-permute-start | bytes 294920 | tf_op jit(solution)/shard_map/ppermute | solution.py:68
  10.9 2.5 %collective-permute-start.8 = (bf16[24,2048]{1,0:T(8,128)(2,1)S(1)}, bf16[24,2048]{1,0:T(8,128)(2,1)S(1)}, u32[]{:S(2)}, u32[]{:S(2)}) collective-permute-start(bf16[24,2048]{1,0:T(8,128)(2,1)S(1)} %get-tuple-element.66), channel_id=1, source_target_pairs={{0,8},{2,10},{4,12},{6,14},{8,0},{10,2},{12,4},{14,6},{16,24},{18,... | collective-permute-start | bytes 294920 | tf_op jit(solution)/shard_map/ppermute | solution.py:68
  14.0 1.5 %collective-permute-done.2 = bf16[24,2048]{1,0:T(8,128)(2,1)S(1)} collective-permute-done((bf16[24,2048]{1,0:T(8,128)(2,1)}, bf16[24,2048]{1,0:T(8,128)(2,1)S(1)}, u32[]{:S(2)}, u32[]{:S(2)}) %collective-permute-start.2) | collective-permute-done | bytes 98336 | tf_op jit(solution)/shard_map/ppermute | solution.py:68
  15.5 1.6 %collective-permute-start.4 = (bf16[96,2048]{1,0:T(8,128)(2,1)S(1)}, bf16[96,2048]{1,0:T(8,128)(2,1)S(1)}, u32[]{:S(2)}, u32[]{:S(2)}) collective-permute-start(bf16[96,2048]{1,0:T(8,128)(2,1)S(1)} %get-tuple-element.80), channel_id=1, source_target_pairs={{0,4},{1,3},{2,6},{3,1},{4,0},{5,7},{6,2},{7,5},{8,12},{9,11},{10,... | collective-permute-start | bytes 1179656 | tf_op jit(solution)/shard_map/ppermute | solution.py:75
  17.1 1.5 %collective-permute-start.3 = (bf16[96,2048]{1,0:T(8,128)(2,1)S(1)}, bf16[96,2048]{1,0:T(8,128)(2,1)S(1)}, u32[]{:S(2)}, u32[]{:S(2)}) collective-permute-start(bf16[96,2048]{1,0:T(8,128)(2,1)S(1)} %get-tuple-element.80), channel_id=1, source_target_pairs={{0,2},{1,5},{2,0},{3,7},{4,6},{5,1},{6,4},{7,3},{8,10},{9,13},{10,... | collective-permute-start | bytes 1179656 | tf_op jit(solution)/shard_map/ppermute | solution.py:75
  18.6 2.8 %collective-permute-done.10 = bf16[24,2048]{1,0:T(8,128)(2,1)S(1)} collective-permute-done((bf16[24,2048]{1,0:T(8,128)(2,1)S(1)}, bf16[24,2048]{1,0:T(8,128)(2,1)S(1)}, u32[]{:S(2)}, u32[]{:S(2)}) %collective-permute-start.10) | collective-permute-done | bytes 98336 | tf_op jit(solution)/shard_map/ppermute | solution.py:68
  21.6 1.6 %collective-permute-start.12 = (bf16[96,2048]{1,0:T(8,128)(2,1)S(1)}, bf16[96,2048]{1,0:T(8,128)(2,1)S(1)}, u32[]{:S(2)}, u32[]{:S(2)}) collective-permute-start(bf16[96,2048]{1,0:T(8,128)(2,1)S(1)} %pad_maximum_fusion.1), channel_id=1, source_target_pairs={{0,4},{1,3},{2,6},{3,1},{4,0},{5,7},{6,2},{7,5},{8,12},{9,11},{10,... | collective-permute-start | bytes 1179656 | tf_op jit(solution)/shard_map/ppermute | solution.py:75
  23.1 1.5 %collective-permute-start.11 = (bf16[96,2048]{1,0:T(8,128)(2,1)S(1)}, bf16[96,2048]{1,0:T(8,128)(2,1)S(1)}, u32[]{:S(2)}, u32[]{:S(2)}) collective-permute-start(bf16[96,2048]{1,0:T(8,128)(2,1)S(1)} %pad_maximum_fusion.1), channel_id=1, source_target_pairs={{0,2},{1,5},{2,0},{3,7},{4,6},{5,1},{6,4},{7,3},{8,10},{9,13},{10,... | collective-permute-start | bytes 1179656 | tf_op jit(solution)/shard_map/ppermute | solution.py:75
  24.7 2.9 %collective-permute-done.4 = bf16[96,2048]{1,0:T(8,128)(2,1)S(1)} collective-permute-done((bf16[96,2048]{1,0:T(8,128)(2,1)S(1)}, bf16[96,2048]{1,0:T(8,128)(2,1)S(1)}, u32[]{:S(2)}, u32[]{:S(2)}) %collective-permute-start.4) | collective-permute-done | bytes 393248 | tf_op jit(solution)/shard_map/ppermute | solution.py:75
  27.6 1.5 %collective-permute-start.5 = (bf16[96,2048]{1,0:T(8,128)(2,1)S(1)}, bf16[96,2048]{1,0:T(8,128)(2,1)S(1)}, u32[]{:S(2)}, u32[]{:S(2)}) collective-permute-start(bf16[96,2048]{1,0:T(8,128)(2,1)S(1)} %collective-permute-done.3), channel_id=1, source_target_pairs={{0,4},{1,3},{2,6},{3,1},{4,0},{5,7},{6,2},{7,5},{8,12},{9,11},{10,... | collective-permute-start | bytes 1179656 | tf_op jit(solution)/shard_map/ppermute | solution.py:75
  29.1 6.3 %collective-permute-done.12 = bf16[96,2048]{1,0:T(8,128)(2,1)S(1)} collective-permute-done((bf16[96,2048]{1,0:T(8,128)(2,1)S(1)}, bf16[96,2048]{1,0:T(8,128)(2,1)S(1)}, u32[]{:S(2)}, u32[]{:S(2)}) %collective-permute-start.12) | collective-permute-done | bytes 393248 | tf_op jit(solution)/shard_map/ppermute | solution.py:75
  35.7 1.5 %collective-permute-start.13 = (bf16[96,2048]{1,0:T(8,128)(2,1)S(1)}, bf16[96,2048]{1,0:T(8,128)(2,1)S(1)}, u32[]{:S(2)}, u32[]{:S(2)}) collective-permute-start(bf16[96,2048]{1,0:T(8,128)(2,1)S(1)} %collective-permute-done.11), channel_id=1, source_target_pairs={{0,4},{1,3},{2,6},{3,1},{4,0},{5,7},{6,2},{7,5},{8,12},{9,11},{10,... | collective-permute-start | bytes 1179656 | tf_op jit(solution)/shard_map/ppermute | solution.py:75
  37.2 2.4 %collective-permute-done.5 = bf16[96,2048]{1,0:T(8,128)(2,1)S(1)} collective-permute-done((bf16[96,2048]{1,0:T(8,128)(2,1)S(1)}, bf16[96,2048]{1,0:T(8,128)(2,1)S(1)}, u32[]{:S(2)}, u32[]{:S(2)}) %collective-permute-start.5) | collective-permute-done | bytes 393248 | tf_op jit(solution)/shard_map/ppermute | solution.py:75
  39.7 2.7 %convolution_convert_fusion.5 = bf16[384,1024]{1,0:T(8,128)(2,1)} fusion(bf16[384,2048]{1,0:T(8,128)(2,1)S(1)} %constant_dynamic-update-slice_fusion.4, bf16[1024,2048]{1,0:T(8,128)(2,1)S(1)} %copy-done.14), kind=kOutput, calls=%fused_computation.19 | convolution fusion | flops 1611005952 | bytes 6553600 | tf_op jit(solution)/shard_map/dot_general | solution.py:131
  42.4 1.4 %collective-permute-done.13 = bf16[96,2048]{1,0:T(8,128)(2,1)S(1)} collective-permute-done((bf16[96,2048]{1,0:T(8,128)(2,1)S(1)}, bf16[96,2048]{1,0:T(8,128)(2,1)S(1)}, u32[]{:S(2)}, u32[]{:S(2)}) %collective-permute-start.13) | collective-permute-done | bytes 393248 | tf_op jit(solution)/shard_map/ppermute | solution.py:75
  43.9 2.7 %convolution_convert_fusion.4 = bf16[384,1024]{1,0:T(8,128)(2,1)} fusion(bf16[384,2048]{1,0:T(8,128)(2,1)S(1)} %constant_dynamic-update-slice_fusion.11, bf16[2048,1024]{1,0:T(8,128)(2,1)S(1)} %copy-done.1), kind=kOutput, calls=%fused_computation.18 | convolution fusion | flops 1611005952 | bytes 6553600 | tf_op jit(solution)/shard_map/dot_general | solution.py:134
  46.7 2.4 %collective-permute-done.14 = bf16[384,1024]{1,0:T(8,128)(2,1)S(1)} collective-permute-done((bf16[384,1024]{1,0:T(8,128)(2,1)}, bf16[384,1024]{1,0:T(8,128)(2,1)S(1)}, u32[]{:S(2)}, u32[]{:S(2)}) %collective-permute-start.14) | collective-permute-done | bytes 786464 | tf_op jit(solution)/shard_map/ppermute | solution.py:78
  49.2 2.6 %multiply_convert_fusion = (bf16[384,1024]{1,0:T(8,128)(2,1)S(1)}, bf16[384,1024]{1,0:T(8,128)(2,1)S(1)}) fusion(bf16[384,1024]{1,0:T(8,128)(2,1)} %convolution_convert_fusion.4, f32[1024]{0:T(1024)S(1)} %copy-done.11, bf16[96,1024]{1,0:T(8,128)(2,1)S(1)} %get-tuple-element.70, bf16[96,1024]{1,0:T(8,128)(2,1)S(1)} %get-tuple-element.71, ...), kind=kLoop, calls=%fused_computation.15 | loop fusion | flops 12976128 | bytes 4722688 | tf_op jit(solution)/shard_map/convert_element_type | solution.py:138
  51.8 1.4 %convolution_convert_fusion.3 = bf16[96,2048]{1,0:T(8,128)(2,1)S(1)} fusion(bf16[2048,1024]{1,0:T(8,128)(2,1)S(1)} %copy-done.2, bf16[384,1024]{1,0:T(8,128)(2,1)S(1)} %get-tuple-element.44), kind=kOutput, calls=%fused_computation.6 | convolution fusion | flops 402849792 | bytes 4784128 | tf_op jit(solution)/shard_map/dot_general | solution.py:142
  53.2 1.6 %collective-permute-start.16 = (bf16[96,2048]{1,0:T(8,128)(2,1)S(1)}, bf16[96,2048]{1,0:T(8,128)(2,1)S(1)}, u32[]{:S(2)}, u32[]{:S(2)}) collective-permute-start(bf16[96,2048]{1,0:T(8,128)(2,1)S(1)} %convolution_convert_fusion.3), channel_id=1, source_target_pairs={{0,4},{1,3},{2,6},{3,1},{4,0},{5,7},{6,2},{7,5},{8,12},{9,11},{10,... | collective-permute-start | bytes 1179656 | tf_op jit(solution)/shard_map/ppermute | solution.py:75
  54.8 1.4 %convolution_convert_fusion.2 = bf16[288,2048]{1,0:T(8,128)(2,1)S(1)} fusion(bf16[2048,1024]{1,0:T(8,128)(2,1)S(1)} %copy-done.2, bf16[384,1024]{1,0:T(8,128)(2,1)S(1)} %get-tuple-element.44), kind=kOutput, calls=%fused_computation.4 | convolution fusion | flops 1208549376 | bytes 5963776 | tf_op jit(solution)/shard_map/dot_general | solution.py:142
  56.9 4.2 %collective-permute-done.16 = bf16[96,2048]{1,0:T(8,128)(2,1)S(1)} collective-permute-done((bf16[96,2048]{1,0:T(8,128)(2,1)S(1)}, bf16[96,2048]{1,0:T(8,128)(2,1)S(1)}, u32[]{:S(2)}, u32[]{:S(2)}) %collective-permute-start.16) | collective-permute-done | bytes 393248 | tf_op jit(solution)/shard_map/ppermute | solution.py:75
  61.2 1.1 collective-permute-start.17
  62.3 0.9 convert_reduce_fusion
  63.2 4.4 %convolution_convert_fusion.1 = bf16[1024,2048]{1,0:T(8,128)(2,1)} fusion(bf16[384,1024]{1,0:T(8,128)(2,1)S(1)} %get-tuple-element.37, bf16[384,2048]{1,0:T(8,128)(2,1)S(1)} %copy-done.4), kind=kOutput, calls=%fused_computation.2 | convolution fusion | flops 1612709888 | bytes 6553600 | tf_op jit(solution)/shard_map/dot_general | solution.py:154
  67.6 1.4 %collective-permute-done.17 = bf16[96,2048]{1,0:T(8,128)(2,1)S(1)} collective-permute-done((bf16[96,2048]{1,0:T(8,128)(2,1)S(1)}, bf16[96,2048]{1,0:T(8,128)(2,1)S(1)}, u32[]{:S(2)}, u32[]{:S(2)}) %collective-permute-start.17) | collective-permute-done | bytes 393248 | tf_op jit(solution)/shard_map/ppermute | solution.py:75
  69.2 6.0 %collective-permute-start.19 = (bf16[24,2048]{1,0:T(8,128)(2,1)S(1)}, bf16[24,2048]{1,0:T(8,128)(2,1)S(1)}, u32[]{:S(2)}, u32[]{:S(2)}) collective-permute-start(bf16[24,2048]{1,0:T(8,128)(2,1)S(1)} %get-tuple-element.78), channel_id=1, source_target_pairs={{0,16},{2,18},{4,20},{6,22},{8,24},{10,26},{12,28},{14,30},{16,0},... | collective-permute-start | bytes 294920 | tf_op jit(solution)/shard_map/ppermute | solution.py:68
  75.2 1.5 %collective-permute-start.20 = (bf16[24,2048]{1,0:T(8,128)(2,1)S(1)}, bf16[24,2048]{1,0:T(8,128)(2,1)S(1)}, u32[]{:S(2)}, u32[]{:S(2)}) collective-permute-start(bf16[24,2048]{1,0:T(8,128)(2,1)S(1)} %get-tuple-element.41), channel_id=1, source_target_pairs={{0,24},{2,26},{4,28},{6,30},{8,16},{10,18},{12,20},{14,22},{16,8},... | collective-permute-start | bytes 294920 | tf_op jit(solution)/shard_map/ppermute | solution.py:68
  76.9 5.0 %collective-permute-done.20 = bf16[24,2048]{1,0:T(8,128)(2,1)S(1)} collective-permute-done((bf16[24,2048]{1,0:T(8,128)(2,1)S(1)}, bf16[24,2048]{1,0:T(8,128)(2,1)S(1)}, u32[]{:S(2)}, u32[]{:S(2)}) %collective-permute-start.20) | collective-permute-done | bytes 98336 | tf_op jit(solution)/shard_map/ppermute | solution.py:68
  82.0 1.6 %collective-permute-done.18 = bf16[24,2048]{1,0:T(8,128)(2,1)S(1)} collective-permute-done((bf16[24,2048]{1,0:T(8,128)(2,1)S(1)}, bf16[24,2048]{1,0:T(8,128)(2,1)S(1)}, u32[]{:S(2)}, u32[]{:S(2)}) %collective-permute-start.18) | collective-permute-done | bytes 98336 | tf_op jit(solution)/shard_map/ppermute | solution.py:68
  84.0 1.1 collective-permute-done.21
  85.5 3.0 %collective-permute-start.22 = (bf16[24,2048]{1,0:T(8,128)(2,1)S(1)}, bf16[24,2048]{1,0:T(8,128)(2,1)S(1)}, u32[]{:S(2)}, u32[]{:S(2)}) collective-permute-start(bf16[24,2048]{1,0:T(8,128)(2,1)S(1)} %add_convert_fusion.1), channel_id=1, source_target_pairs={{0,8},{2,10},{4,12},{6,14},{8,0},{10,2},{12,4},{14,6},{16,24},{18,... | collective-permute-start | bytes 294920 | tf_op jit(solution)/shard_map/ppermute | solution.py:68
  88.6 1.8 %collective-permute-start.24 = (bf16[24,2048]{1,0:T(8,128)(2,1)S(1)}, bf16[24,2048]{1,0:T(8,128)(2,1)S(1)}, u32[]{:S(2)}, u32[]{:S(2)}) collective-permute-start(bf16[24,2048]{1,0:T(8,128)(2,1)S(1)} %add_convert_fusion.1), channel_id=1, source_target_pairs={{0,24},{2,26},{4,28},{6,30},{8,16},{10,18},{12,20},{14,22},{16,8},... | collective-permute-start | bytes 294920 | tf_op jit(solution)/shard_map/ppermute | solution.py:68
  90.3 4.4 %convolution_convert_fusion = bf16[2048,1024]{1,0:T(8,128)(2,1)} fusion(bf16[384,2048]{1,0:T(8,128)(2,1)S(1)} %copy-done.10, bf16[384,1024]{1,0:T(8,128)(2,1)S(1)} %get-tuple-element.44), kind=kOutput, calls=%fused_computation.1 | convolution fusion | flops 1612709888 | bytes 6553600 | tf_op jit(solution)/shard_map/dot_general | solution.py:182
  95.5 1.8 %collective-permute-start.29 = (f32[3,2048]{1,0:T(4,128)S(1)}, f32[3,2048]{1,0:T(4,128)S(1)}, u32[]{:S(2)}, u32[]{:S(2)}) collective-permute-start(f32[3,2048]{1,0:T(4,128)S(1)} %add.125), channel_id=1, source_target_pairs={{0,16},{2,18},{4,20},{6,22},{8,24},{10,26},{12,28},{14,30},{16,0},... | collective-permute-start | bytes 73736 | tf_op jit(solution)/shard_map/ppermute | solution.py:68
  98.0 1.4 %collective-permute-start.25 = (bf16[96,2048]{1,0:T(8,128)(2,1)S(1)}, bf16[96,2048]{1,0:T(8,128)(2,1)S(1)}, u32[]{:S(2)}, u32[]{:S(2)}) collective-permute-start(bf16[96,2048]{1,0:T(8,128)(2,1)S(1)} %constant_dynamic-update-slice_fusion.18.refs_0_), channel_id=1, source_target_pairs={{0,2},{1,5},{2,0},{3,7},{4,6},{5,1},{6,4},{7,3},{8,10},{9,13},{10,... | collective-permute-start | bytes 1179656 | tf_op jit(solution)/shard_map/ppermute | solution.py:75
  99.4 1.3 %collective-permute-done.29 = f32[3,2048]{1,0:T(4,128)S(1)} collective-permute-done((f32[3,2048]{1,0:T(4,128)S(1)}, f32[3,2048]{1,0:T(4,128)S(1)}, u32[]{:S(2)}, u32[]{:S(2)}) %collective-permute-start.29) | collective-permute-done | bytes 24608 | tf_op jit(solution)/shard_map/ppermute | solution.py:68
  100.7 1.3 %collective-permute-start.30 = (f32[3,2048]{1,0:T(4,128)S(1)}, f32[3,2048]{1,0:T(4,128)S(1)}, u32[]{:S(2)}, u32[]{:S(2)}) collective-permute-start(f32[3,2048]{1,0:T(4,128)S(1)} %add.126), channel_id=1, source_target_pairs={{0,2},{1,5},{2,0},{3,7},{4,6},{5,1},{6,4},{7,3},{8,10},{9,13},{10,... | collective-permute-start | bytes 73736 | tf_op jit(solution)/shard_map/ppermute | solution.py:75
  102.2 5.4 %collective-permute-done.30 = f32[3,2048]{1,0:T(4,128)S(1)} collective-permute-done((f32[3,2048]{1,0:T(4,128)S(1)}, f32[3,2048]{1,0:T(4,128)S(1)}, u32[]{:S(2)}, u32[]{:S(2)}) %collective-permute-start.30) | collective-permute-done | bytes 24608 | tf_op jit(solution)/shard_map/ppermute | solution.py:75
  107.6 1.2 collective-permute-done.26.refs_2_
  109.3 1.5 %collective-permute-start.27 = (bf16[96,2048]{1,0:T(8,128)(2,1)S(1)}, bf16[96,2048]{1,0:T(8,128)(2,1)S(1)}, u32[]{:S(2)}, u32[]{:S(2)}) collective-permute-start(bf16[96,2048]{1,0:T(8,128)(2,1)S(1)} %collective-permute-done.25.refs_1_), channel_id=1, source_target_pairs={{0,4},{1,3},{2,6},{3,1},{4,0},{5,7},{6,2},{7,5},{8,12},{9,11},{10,... | collective-permute-start | bytes 1179656 | tf_op jit(solution)/shard_map/ppermute | solution.py:75
  110.8 1.9 %collective-permute-done.31 = f32[3,2048]{1,0:T(4,128)S(1)} collective-permute-done((f32[3,2048]{1,0:T(4,128)S(1)}, f32[3,2048]{1,0:T(4,128)S(1)}, u32[]{:S(2)}, u32[]{:S(2)}) %collective-permute-start.31) | collective-permute-done | bytes 24608 | tf_op jit(solution)/shard_map/ppermute | solution.py:75
  114.1 3.0 %collective-permute-done.27.refs_3_ = bf16[96,2048]{1,0:T(8,128)(2,1)S(1)} collective-permute-done((bf16[96,2048]{1,0:T(8,128)(2,1)S(1)}, bf16[96,2048]{1,0:T(8,128)(2,1)S(1)}, u32[]{:S(2)}, u32[]{:S(2)}) %collective-permute-start.27) | collective-permute-done | bytes 393248 | tf_op jit(solution)/shard_map/ppermute | solution.py:75
  117.1 2.6 %place.1 = f32[256,2048]{1,0:T(8,128)} custom-call(bf16[96,2048]{1,0:T(8,128)(2,1)S(1)} %constant_dynamic-update-slice_fusion.18.refs_0_, bf16[96,2048]{1,0:T(8,128)(2,1)S(1)} %collective-permute-done.25.refs_1_, bf16[96,2048]{1,0:T(8,128)(2,1)S(1)} %collective-permute-done.26.refs_2_, bf16[96,2048]{1,0:T(8,128)(2,1)S(1)} %collective-permute-done.27.refs_3_, ...), custom_call_target="tpu_custom_call" | custom-call | flops 402653184 | bytes 1572864 | tf_op jit(solution)/shard_map/place/pallas_call | solution.py:52
  (110 shorter events, 7.7 us)
Async XLA Ops:
  0.6 5.7 %copy-start = (bf16[256,2048]{1,0:T(8,128)(2,1)S(1)}, bf16[256,2048]{1,0:T(8,128)(2,1)}, u32[]{:S(2)}) copy-start(bf16[256,2048]{1,0:T(8,128)(2,1)} %param.13) | copy-start | bytes 3145732
  0.6 8.7 %copy-start.7 = (f32[2048]{0:T(1024)S(1)}, f32[2048]{0:T(1024)}, u32[]{:S(2)}) copy-start(f32[2048]{0:T(1024)} %param.14) | copy-start | bytes 24580
  0.7 8.7 %copy-start.8 = (f32[2048]{0:T(1024)S(1)}, f32[2048]{0:T(1024)}, u32[]{:S(2)}) copy-start(f32[2048]{0:T(1024)} %param.15) | copy-start | bytes 24580
  0.7 13.3 %collective-permute-start.1 = (bf16[24,2048]{1,0:T(8,128)(2,1)}, bf16[24,2048]{1,0:T(8,128)(2,1)S(1)}, u32[]{:S(2)}, u32[]{:S(2)}) collective-permute-start(bf16[24,2048]{1,0:T(8,128)(2,1)} %param.19), channel_id=1, source_target_pairs={{0,16},{2,18},{4,20},{6,22},{8,24},{10,26},{12,28},{14,30},{16,0},... | collective-permute-start | bytes 294920 | tf_op jit(solution)/shard_map/ppermute | solution.py:68
  4.8 8.6 %collective-permute-start = (bf16[24,2048]{1,0:T(8,128)(2,1)}, bf16[24,2048]{1,0:T(8,128)(2,1)S(1)}, u32[]{:S(2)}, u32[]{:S(2)}) collective-permute-start(bf16[24,2048]{1,0:T(8,128)(2,1)} %param.19), channel_id=1, source_target_pairs={{0,8},{2,10},{4,12},{6,14},{8,0},{10,2},{12,4},{14,6},{16,24},{18,... | collective-permute-start | bytes 294920 | tf_op jit(solution)/shard_map/ppermute | solution.py:68
  7.7 1.7 %collective-permute-start.7 = (f32[2,24]{1,0:T(2,128)S(1)}, f32[2,24]{1,0:T(2,128)S(1)}, u32[]{:S(2)}, u32[]{:S(2)}) collective-permute-start(f32[2,24]{1,0:T(2,128)S(1)} %pad_maximum_fusion.3), channel_id=1, source_target_pairs={{0,1},{1,0},{2,3},{3,2},{4,5},{5,4},{6,7},{7,6},{8,9},{9,8},{10,11... | collective-permute-start | bytes 584 | tf_op jit(solution)/shard_map/ppermute | solution.py:78
  7.8 7.8 %collective-permute-start.2 = (bf16[24,2048]{1,0:T(8,128)(2,1)}, bf16[24,2048]{1,0:T(8,128)(2,1)S(1)}, u32[]{:S(2)}, u32[]{:S(2)}) collective-permute-start(bf16[24,2048]{1,0:T(8,128)(2,1)} %param.19), channel_id=1, source_target_pairs={{0,24},{2,26},{4,28},{6,30},{8,16},{10,18},{12,20},{14,22},{16,8},... | collective-permute-start | bytes 294920 | tf_op jit(solution)/shard_map/ppermute | solution.py:68
  9.5 12.0 %collective-permute-start.9 = (bf16[24,2048]{1,0:T(8,128)(2,1)S(1)}, bf16[24,2048]{1,0:T(8,128)(2,1)S(1)}, u32[]{:S(2)}, u32[]{:S(2)}) collective-permute-start(bf16[24,2048]{1,0:T(8,128)(2,1)S(1)} %get-tuple-element.66), channel_id=1, source_target_pairs={{0,16},{2,18},{4,20},{6,22},{8,24},{10,26},{12,28},{14,30},{16,0},... | collective-permute-start | bytes 294920 | tf_op jit(solution)/shard_map/ppermute | solution.py:68
  10.9 10.6 %collective-permute-start.8 = (bf16[24,2048]{1,0:T(8,128)(2,1)S(1)}, bf16[24,2048]{1,0:T(8,128)(2,1)S(1)}, u32[]{:S(2)}, u32[]{:S(2)}) collective-permute-start(bf16[24,2048]{1,0:T(8,128)(2,1)S(1)} %get-tuple-element.66), channel_id=1, source_target_pairs={{0,8},{2,10},{4,12},{6,14},{8,0},{10,2},{12,4},{14,6},{16,24},{18,... | collective-permute-start | bytes 294920 | tf_op jit(solution)/shard_map/ppermute | solution.py:68
  13.4 8.0 %collective-permute-start.10 = (bf16[24,2048]{1,0:T(8,128)(2,1)S(1)}, bf16[24,2048]{1,0:T(8,128)(2,1)S(1)}, u32[]{:S(2)}, u32[]{:S(2)}) collective-permute-start(bf16[24,2048]{1,0:T(8,128)(2,1)S(1)} %get-tuple-element.66), channel_id=1, source_target_pairs={{0,24},{2,26},{4,28},{6,30},{8,16},{10,18},{12,20},{14,22},{16,8},... | collective-permute-start | bytes 294920 | tf_op jit(solution)/shard_map/ppermute | solution.py:68
  15.5 12.0 %collective-permute-start.4 = (bf16[96,2048]{1,0:T(8,128)(2,1)S(1)}, bf16[96,2048]{1,0:T(8,128)(2,1)S(1)}, u32[]{:S(2)}, u32[]{:S(2)}) collective-permute-start(bf16[96,2048]{1,0:T(8,128)(2,1)S(1)} %get-tuple-element.80), channel_id=1, source_target_pairs={{0,4},{1,3},{2,6},{3,1},{4,0},{5,7},{6,2},{7,5},{8,12},{9,11},{10,... | collective-permute-start | bytes 1179656 | tf_op jit(solution)/shard_map/ppermute | solution.py:75
  17.1 10.4 %collective-permute-start.3 = (bf16[96,2048]{1,0:T(8,128)(2,1)S(1)}, bf16[96,2048]{1,0:T(8,128)(2,1)S(1)}, u32[]{:S(2)}, u32[]{:S(2)}) collective-permute-start(bf16[96,2048]{1,0:T(8,128)(2,1)S(1)} %get-tuple-element.80), channel_id=1, source_target_pairs={{0,2},{1,5},{2,0},{3,7},{4,6},{5,1},{6,4},{7,3},{8,10},{9,13},{10,... | collective-permute-start | bytes 1179656 | tf_op jit(solution)/shard_map/ppermute | solution.py:75
  21.6 13.9 %collective-permute-start.12 = (bf16[96,2048]{1,0:T(8,128)(2,1)S(1)}, bf16[96,2048]{1,0:T(8,128)(2,1)S(1)}, u32[]{:S(2)}, u32[]{:S(2)}) collective-permute-start(bf16[96,2048]{1,0:T(8,128)(2,1)S(1)} %pad_maximum_fusion.1), channel_id=1, source_target_pairs={{0,4},{1,3},{2,6},{3,1},{4,0},{5,7},{6,2},{7,5},{8,12},{9,11},{10,... | collective-permute-start | bytes 1179656 | tf_op jit(solution)/shard_map/ppermute | solution.py:75
  23.1 12.5 %collective-permute-start.11 = (bf16[96,2048]{1,0:T(8,128)(2,1)S(1)}, bf16[96,2048]{1,0:T(8,128)(2,1)S(1)}, u32[]{:S(2)}, u32[]{:S(2)}) collective-permute-start(bf16[96,2048]{1,0:T(8,128)(2,1)S(1)} %pad_maximum_fusion.1), channel_id=1, source_target_pairs={{0,2},{1,5},{2,0},{3,7},{4,6},{5,1},{6,4},{7,3},{8,10},{9,13},{10,... | collective-permute-start | bytes 1179656 | tf_op jit(solution)/shard_map/ppermute | solution.py:75
  24.6 15.0 %copy-start.14 = (bf16[1024,2048]{1,0:T(8,128)(2,1)S(1)}, bf16[1024,2048]{1,0:T(8,128)(2,1)}, u32[]{:S(2)}) copy-start(bf16[1024,2048]{1,0:T(8,128)(2,1)} %param.18) | copy-start | bytes 12582916
  27.6 12.1 %collective-permute-start.5 = (bf16[96,2048]{1,0:T(8,128)(2,1)S(1)}, bf16[96,2048]{1,0:T(8,128)(2,1)S(1)}, u32[]{:S(2)}, u32[]{:S(2)}) collective-permute-start(bf16[96,2048]{1,0:T(8,128)(2,1)S(1)} %collective-permute-done.3), channel_id=1, source_target_pairs={{0,4},{1,3},{2,6},{3,1},{4,0},{5,7},{6,2},{7,5},{8,12},{9,11},{10,... | collective-permute-start | bytes 1179656 | tf_op jit(solution)/shard_map/ppermute | solution.py:75
  35.7 8.2 %collective-permute-start.13 = (bf16[96,2048]{1,0:T(8,128)(2,1)S(1)}, bf16[96,2048]{1,0:T(8,128)(2,1)S(1)}, u32[]{:S(2)}, u32[]{:S(2)}) collective-permute-start(bf16[96,2048]{1,0:T(8,128)(2,1)S(1)} %collective-permute-done.11), channel_id=1, source_target_pairs={{0,4},{1,3},{2,6},{3,1},{4,0},{5,7},{6,2},{7,5},{8,12},{9,11},{10,... | collective-permute-start | bytes 1179656 | tf_op jit(solution)/shard_map/ppermute | solution.py:75
  39.7 2.7 %copy-start.3 = (bf16[384,2048]{1,0:T(8,128)(2,1)}, bf16[384,2048]{1,0:T(8,128)(2,1)S(1)}, u32[]{:S(2)}) copy-start(bf16[384,2048]{1,0:T(8,128)(2,1)S(1)} %constant_dynamic-update-slice_fusion.4) | copy-start | bytes 4718596
  39.7 4.2 %copy-start.1 = (bf16[2048,1024]{1,0:T(8,128)(2,1)S(1)}, bf16[2048,1024]{1,0:T(8,128)(2,1)}, u32[]{:S(2)}) copy-start(bf16[2048,1024]{1,0:T(8,128)(2,1)} %param.16) | copy-start | bytes 12582916
  42.4 4.2 %collective-permute-start.6 = (bf16[384,1024]{1,0:T(8,128)(2,1)}, bf16[384,1024]{1,0:T(8,128)(2,1)S(1)}, u32[]{:S(2)}, u32[]{:S(2)}) collective-permute-start(bf16[384,1024]{1,0:T(8,128)(2,1)} %convolution_convert_fusion.5), channel_id=1, source_target_pairs={{0,1},{1,0},{2,3},{3,2},{4,5},{5,4},{6,7},{7,6},{8,9},{9,8},{10,11... | collective-permute-start | bytes 2359304 | tf_op jit(solution)/shard_map/ppermute | solution.py:78
  43.9 2.7 %copy-start.9 = (bf16[384,2048]{1,0:T(8,128)(2,1)}, bf16[384,2048]{1,0:T(8,128)(2,1)S(1)}, u32[]{:S(2)}) copy-start(bf16[384,2048]{1,0:T(8,128)(2,1)S(1)} %constant_dynamic-update-slice_fusion.11) | copy-start | bytes 4718596
  43.9 2.7 %copy-start.12 = (s32[24]{0:T(128)S(1)}, s32[24]{0:T(128)}, u32[]{:S(2)}) copy-start(s32[24]{0:T(128)} %param.12) | copy-start | bytes 292
  46.6 2.5 %collective-permute-start.14 = (bf16[384,1024]{1,0:T(8,128)(2,1)}, bf16[384,1024]{1,0:T(8,128)(2,1)S(1)}, u32[]{:S(2)}, u32[]{:S(2)}) collective-permute-start(bf16[384,1024]{1,0:T(8,128)(2,1)} %convolution_convert_fusion.4), channel_id=1, source_target_pairs={{0,1},{1,0},{2,3},{3,2},{4,5},{5,4},{6,7},{7,6},{8,9},{9,8},{10,11... | collective-permute-start | bytes 2359304 | tf_op jit(solution)/shard_map/ppermute | solution.py:78
  46.6 2.5 %copy-start.11 = (f32[1024]{0:T(1024)S(1)}, f32[1024]{0:T(1024)}, u32[]{:S(2)}) copy-start(f32[1024]{0:T(1024)} %param.17) | copy-start | bytes 12292
  49.2 2.7 %copy-start.2 = (bf16[2048,1024]{1,0:T(8,128)(2,1)S(1)}, bf16[2048,1024]{1,0:T(8,128)(2,1)}, u32[]{:S(2)}) copy-start(bf16[2048,1024]{1,0:T(8,128)(2,1)} %param.16) | copy-start | bytes 12582916
  53.2 7.8 %collective-permute-start.16 = (bf16[96,2048]{1,0:T(8,128)(2,1)S(1)}, bf16[96,2048]{1,0:T(8,128)(2,1)S(1)}, u32[]{:S(2)}, u32[]{:S(2)}) collective-permute-start(bf16[96,2048]{1,0:T(8,128)(2,1)S(1)} %convolution_convert_fusion.3), channel_id=1, source_target_pairs={{0,4},{1,3},{2,6},{3,1},{4,0},{5,7},{6,2},{7,5},{8,12},{9,11},{10,... | collective-permute-start | bytes 1179656 | tf_op jit(solution)/shard_map/ppermute | solution.py:75
  56.3 6.1 %copy-start.4 = (bf16[384,2048]{1,0:T(8,128)(2,1)S(1)}, bf16[384,2048]{1,0:T(8,128)(2,1)}, u32[]{:S(2)}) copy-start(bf16[384,2048]{1,0:T(8,128)(2,1)} %copy-done.3) | copy-start | bytes 4718596
  56.3 12.7 %collective-permute-start.15 = (bf16[96,2048]{1,0:T(8,128)(2,1)S(1)}, bf16[96,2048]{1,0:T(8,128)(2,1)S(1)}, u32[]{:S(2)}, u32[]{:S(2)}) collective-permute-start(bf16[96,2048]{1,0:T(8,128)(2,1)S(1)} %slice.98), channel_id=1, source_target_pairs={{0,4},{1,3},{2,6},{3,1},{4,0},{5,7},{6,2},{7,5},{8,12},{9,11},{10,... | collective-permute-start | bytes 1179656 | tf_op jit(solution)/shard_map/ppermute | solution.py:75
  61.2 7.8 %collective-permute-start.17 = (bf16[96,2048]{1,0:T(8,128)(2,1)S(1)}, bf16[96,2048]{1,0:T(8,128)(2,1)S(1)}, u32[]{:S(2)}, u32[]{:S(2)}) collective-permute-start(bf16[96,2048]{1,0:T(8,128)(2,1)S(1)} %add_convert_fusion), channel_id=1, source_target_pairs={{0,2},{1,5},{2,0},{3,7},{4,6},{5,1},{6,4},{7,3},{8,10},{9,13},{10,... | collective-permute-start | bytes 1179656 | tf_op jit(solution)/shard_map/ppermute | solution.py:75
  67.6 17.5 %copy-start.5 = (bf16[24,2048]{1,0:T(8,128)(2,1)S(1)}, bf16[24,2048]{1,0:T(8,128)(2,1)}, u32[]{:S(2)}) copy-start(bf16[24,2048]{1,0:T(8,128)(2,1)} %param.19) | copy-start | bytes 294916
  69.2 12.8 %collective-permute-start.19 = (bf16[24,2048]{1,0:T(8,128)(2,1)S(1)}, bf16[24,2048]{1,0:T(8,128)(2,1)S(1)}, u32[]{:S(2)}, u32[]{:S(2)}) collective-permute-start(bf16[24,2048]{1,0:T(8,128)(2,1)S(1)} %get-tuple-element.78), channel_id=1, source_target_pairs={{0,16},{2,18},{4,20},{6,22},{8,24},{10,26},{12,28},{14,30},{16,0},... | collective-permute-start | bytes 294920 | tf_op jit(solution)/shard_map/ppermute | solution.py:68
  75.2 8.4 %collective-permute-start.18 = (bf16[24,2048]{1,0:T(8,128)(2,1)S(1)}, bf16[24,2048]{1,0:T(8,128)(2,1)S(1)}, u32[]{:S(2)}, u32[]{:S(2)}) collective-permute-start(bf16[24,2048]{1,0:T(8,128)(2,1)S(1)} %get-tuple-element.79), channel_id=1, source_target_pairs={{0,8},{2,10},{4,12},{6,14},{8,0},{10,2},{12,4},{14,6},{16,24},{18,... | collective-permute-start | bytes 294920 | tf_op jit(solution)/shard_map/ppermute | solution.py:68
  75.2 6.8 %collective-permute-start.20 = (bf16[24,2048]{1,0:T(8,128)(2,1)S(1)}, bf16[24,2048]{1,0:T(8,128)(2,1)S(1)}, u32[]{:S(2)}, u32[]{:S(2)}) collective-permute-start(bf16[24,2048]{1,0:T(8,128)(2,1)S(1)} %get-tuple-element.41), channel_id=1, source_target_pairs={{0,24},{2,26},{4,28},{6,30},{8,16},{10,18},{12,20},{14,22},{16,8},... | collective-permute-start | bytes 294920 | tf_op jit(solution)/shard_map/ppermute | solution.py:68
  76.9 13.4 %copy-start.10 = (bf16[384,2048]{1,0:T(8,128)(2,1)S(1)}, bf16[384,2048]{1,0:T(8,128)(2,1)}, u32[]{:S(2)}) copy-start(bf16[384,2048]{1,0:T(8,128)(2,1)} %copy-done.9) | copy-start | bytes 4718596
  83.8 1.2 %collective-permute-start.21 = (f32[2,24]{1,0:T(2,128)S(1)}, f32[2,24]{1,0:T(2,128)S(1)}, u32[]{:S(2)}, u32[]{:S(2)}) collective-permute-start(f32[2,24]{1,0:T(2,128)S(1)} %pad_maximum_fusion.4), channel_id=1, source_target_pairs={{0,1},{1,0},{2,3},{3,2},{4,5},{5,4},{6,7},{7,6},{8,9},{9,8},{10,11... | collective-permute-start | bytes 584 | tf_op jit(solution)/shard_map/ppermute | solution.py:78
  85.2 9.6 %copy-start.6 = (bf16[24,2048]{1,0:T(8,128)(2,1)}, bf16[24,2048]{1,0:T(8,128)(2,1)S(1)}, u32[]{:S(2)}) copy-start(bf16[24,2048]{1,0:T(8,128)(2,1)S(1)} %add_convert_fusion.1) | copy-start | bytes 294916
  85.2 12.1 %collective-permute-start.23 = (bf16[24,2048]{1,0:T(8,128)(2,1)S(1)}, bf16[24,2048]{1,0:T(8,128)(2,1)S(1)}, u32[]{:S(2)}, u32[]{:S(2)}) collective-permute-start(bf16[24,2048]{1,0:T(8,128)(2,1)S(1)} %add_convert_fusion.1), channel_id=1, source_target_pairs={{0,16},{2,18},{4,20},{6,22},{8,24},{10,26},{12,28},{14,30},{16,0},... | collective-permute-start | bytes 294920 | tf_op jit(solution)/shard_map/ppermute | solution.py:68
  85.5 11.8 %collective-permute-start.22 = (bf16[24,2048]{1,0:T(8,128)(2,1)S(1)}, bf16[24,2048]{1,0:T(8,128)(2,1)S(1)}, u32[]{:S(2)}, u32[]{:S(2)}) collective-permute-start(bf16[24,2048]{1,0:T(8,128)(2,1)S(1)} %add_convert_fusion.1), channel_id=1, source_target_pairs={{0,8},{2,10},{4,12},{6,14},{8,0},{10,2},{12,4},{14,6},{16,24},{18,... | collective-permute-start | bytes 294920 | tf_op jit(solution)/shard_map/ppermute | solution.py:68
  88.5 10.9 %copy-start.13 = (s32[4]{0:T(128)S(1)}, s32[4]{0:T(128)}, u32[]{:S(2)}) copy-start(s32[4]{0:T(128)} %constant.38.clone) | copy-start | bytes 52
  88.5 7.0 %collective-permute-start.28 = (f32[3,2048]{1,0:T(4,128)S(1)}, f32[3,2048]{1,0:T(4,128)S(1)}, u32[]{:S(2)}, u32[]{:S(2)}) collective-permute-start(f32[3,2048]{1,0:T(4,128)S(1)} %pad_maximum_fusion.2), channel_id=1, source_target_pairs={{0,8},{2,10},{4,12},{6,14},{8,0},{10,2},{12,4},{14,6},{16,24},{18,... | collective-permute-start | bytes 73736 | tf_op jit(solution)/shard_map/ppermute | solution.py:68
  88.6 8.7 %collective-permute-start.24 = (bf16[24,2048]{1,0:T(8,128)(2,1)S(1)}, bf16[24,2048]{1,0:T(8,128)(2,1)S(1)}, u32[]{:S(2)}, u32[]{:S(2)}) collective-permute-start(bf16[24,2048]{1,0:T(8,128)(2,1)S(1)} %add_convert_fusion.1), channel_id=1, source_target_pairs={{0,24},{2,26},{4,28},{6,30},{8,16},{10,18},{12,20},{14,22},{16,8},... | collective-permute-start | bytes 294920 | tf_op jit(solution)/shard_map/ppermute | solution.py:68
  95.5 5.2 %collective-permute-start.29 = (f32[3,2048]{1,0:T(4,128)S(1)}, f32[3,2048]{1,0:T(4,128)S(1)}, u32[]{:S(2)}, u32[]{:S(2)}) collective-permute-start(f32[3,2048]{1,0:T(4,128)S(1)} %add.125), channel_id=1, source_target_pairs={{0,16},{2,18},{4,20},{6,22},{8,24},{10,26},{12,28},{14,30},{16,0},... | collective-permute-start | bytes 73736 | tf_op jit(solution)/shard_map/ppermute | solution.py:68
  97.4 11.4 %collective-permute-start.26 = (bf16[96,2048]{1,0:T(8,128)(2,1)S(1)}, bf16[96,2048]{1,0:T(8,128)(2,1)S(1)}, u32[]{:S(2)}, u32[]{:S(2)}) collective-permute-start(bf16[96,2048]{1,0:T(8,128)(2,1)S(1)} %constant_dynamic-update-slice_fusion.18.refs_0_), channel_id=1, source_target_pairs={{0,4},{1,3},{2,6},{3,1},{4,0},{5,7},{6,2},{7,5},{8,12},{9,11},{10,... | collective-permute-start | bytes 1179656 | tf_op jit(solution)/shard_map/ppermute | solution.py:75
  98.0 10.8 %collective-permute-start.25 = (bf16[96,2048]{1,0:T(8,128)(2,1)S(1)}, bf16[96,2048]{1,0:T(8,128)(2,1)S(1)}, u32[]{:S(2)}, u32[]{:S(2)}) collective-permute-start(bf16[96,2048]{1,0:T(8,128)(2,1)S(1)} %constant_dynamic-update-slice_fusion.18.refs_0_), channel_id=1, source_target_pairs={{0,2},{1,5},{2,0},{3,7},{4,6},{5,1},{6,4},{7,3},{8,10},{9,13},{10,... | collective-permute-start | bytes 1179656 | tf_op jit(solution)/shard_map/ppermute | solution.py:75
  100.7 6.8 %collective-permute-start.30 = (f32[3,2048]{1,0:T(4,128)S(1)}, f32[3,2048]{1,0:T(4,128)S(1)}, u32[]{:S(2)}, u32[]{:S(2)}) collective-permute-start(f32[3,2048]{1,0:T(4,128)S(1)} %add.126), channel_id=1, source_target_pairs={{0,2},{1,5},{2,0},{3,7},{4,6},{5,1},{6,4},{7,3},{8,10},{9,13},{10,... | collective-permute-start | bytes 73736 | tf_op jit(solution)/shard_map/ppermute | solution.py:75
  108.8 3.9 %collective-permute-start.31 = (f32[3,2048]{1,0:T(4,128)S(1)}, f32[3,2048]{1,0:T(4,128)S(1)}, u32[]{:S(2)}, u32[]{:S(2)}) collective-permute-start(f32[3,2048]{1,0:T(4,128)S(1)} %add.127), channel_id=1, source_target_pairs={{0,4},{1,3},{2,6},{3,1},{4,0},{5,7},{6,2},{7,5},{8,12},{9,11},{10,... | collective-permute-start | bytes 73736 | tf_op jit(solution)/shard_map/ppermute | solution.py:75
  109.3 7.8 %collective-permute-start.27 = (bf16[96,2048]{1,0:T(8,128)(2,1)S(1)}, bf16[96,2048]{1,0:T(8,128)(2,1)S(1)}, u32[]{:S(2)}, u32[]{:S(2)}) collective-permute-start(bf16[96,2048]{1,0:T(8,128)(2,1)S(1)} %collective-permute-done.25.refs_1_), channel_id=1, source_target_pairs={{0,4},{1,3},{2,6},{3,1},{4,0},{5,7},{6,2},{7,5},{8,12},{9,11},{10,... | collective-permute-start | bytes 1179656 | tf_op jit(solution)/shard_map/ppermute | solution.py:75

commit v5 on v4

--- a/solution.py
+++ b/solution.py
@@ -25,7 +25,7 @@
 
 
 def params():
-    return pltpu.CompilerParams(vmem_limit_bytes=6 << 20)
+    return pltpu.CompilerParams(vmem_limit_bytes=10 << 20)
 
 
 def cost(flops, read):
@@ -48,7 +48,7 @@
 
 def place(pieces, indices, places):
     size, cols = pieces[0].shape
-    tile = min(cols, 512)
+    tile = min(cols, 1024)
     return pl.pallas_call(
         place_kernel,
         grid=(cols // tile,),

time: 120 us -> 119 us (level)
  no operation moved by 1% of the time
where the time goes in v5:
time: 119 us
  waiting for transfers between devices  46.2 us (39%)
  starting transfers between devices  43.2 us (36%)
  matrix products  18.4 us (15%)
  other arithmetic  5.22 us (4%)
  local copies, waits for them, and re-layouts  3.03 us (3%)
  Pallas kernels  1.99 us (2%)
    ppermute x14, waiting for transfers between devices, turn(): return lax.ppermute(x, ('wide', 'narrow'), pairs)  30.3 us
    ppermute x14, starting transfers between devices, flip(): return lax.ppermute(x, 'wide', [(i, i ^ bits) for i in range(wide)])  25.2 us
    ppermute x14, starting transfers between devices, turn(): return lax.ppermute(x, ('wide', 'narrow'), pairs)  17.8 us
    ppermute x14, waiting for transfers between devices, flip(): return lax.ppermute(x, 'wide', [(i, i ^ bits) for i in range(wide)])  12.4 us
    dot_general x1, matrix products, on_device(): lax.dot_general(hidden_panel, d_hidden, contract_rows, preferred_element_...  4.42 us
    dot_general x1, matrix products, on_device(): lax.dot_general(activation, grad_panel, contract_rows, preferred_element_...  4.41 us
    ppermute x4, waiting for transfers between devices, other_core(): return lax.ppermute(x, 'narrow', [(0, 1), (1, 0)])  3.47 us
    dot_general x2, matrix products, norm_grads(): lax.dot_general(d_hidden, w_up, (((1,), (1,)), ((), ())), preferred_eleme...  2.83 us
  transfers between devices with their start and end apart: 32, of which 19 were waited for; matrix products, arithmetic and copies ran while one was open for 18% of the time, Pallas kernels for 0%

profile of v5, /device:TPU:0, one launch (start us, length us, event | category | flops | bytes accessed | tf_op | source)
XLA Modules:
  0.0 119.1 jit_solution(1711134944415726314)
XLA Ops:
  0.7 4.1 %collective-permute-start.1 = (bf16[24,2048]{1,0:T(8,128)(2,1)}, bf16[24,2048]{1,0:T(8,128)(2,1)S(1)}, u32[]{:S(2)}, u32[]{:S(2)}) collective-permute-start(bf16[24,2048]{1,0:T(8,128)(2,1)} %param.19), channel_id=1, source_target_pairs={{0,16},{2,18},{4,20},{6,22},{8,24},{10,26},{12,28},{14,30},{16,0},... | collective-permute-start | bytes 294920 | tf_op jit(solution)/shard_map/ppermute | solution.py:68
  4.8 1.6 %collective-permute-start = (bf16[24,2048]{1,0:T(8,128)(2,1)}, bf16[24,2048]{1,0:T(8,128)(2,1)S(1)}, u32[]{:S(2)}, u32[]{:S(2)}) collective-permute-start(bf16[24,2048]{1,0:T(8,128)(2,1)} %param.19), channel_id=1, source_target_pairs={{0,8},{2,10},{4,12},{6,14},{8,0},{10,2},{12,4},{14,6},{16,24},{18,... | collective-permute-start | bytes 294920 | tf_op jit(solution)/shard_map/ppermute | solution.py:68
  6.4 1.3 %fusion.18 = (f32[24]{0:T(128)S(1)}, f32[24]{0:T(128)S(1)}, f32[24,2048]{1,0:T(8,128)S(1)}) fusion(bf16[256,2048]{1,0:T(8,128)(2,1)S(1)} %copy-done, s32[24]{0:T(128)} %param.12, bf16[24,2048]{1,0:T(8,128)(2,1)} %param.11), kind=kOutput, calls=%fused_computation.82 | convolution fusion | flops 25429968 | bytes 1343776 | tf_op jit(solution)/shard_map/dot_general | solution.py:120
  8.4 0.9 constant_dynamic-update-slice_fusion.3
  9.5 1.4 %collective-permute-start.9 = (bf16[24,2048]{1,0:T(8,128)(2,1)S(1)}, bf16[24,2048]{1,0:T(8,128)(2,1)S(1)}, u32[]{:S(2)}, u32[]{:S(2)}) collective-permute-start(bf16[24,2048]{1,0:T(8,128)(2,1)S(1)} %get-tuple-element.66), channel_id=1, source_target_pairs={{0,16},{2,18},{4,20},{6,22},{8,24},{10,26},{12,28},{14,30},{16,0},... | collective-permute-start | bytes 294920 | tf_op jit(solution)/shard_map/ppermute | solution.py:68
  10.9 2.5 %collective-permute-start.8 = (bf16[24,2048]{1,0:T(8,128)(2,1)S(1)}, bf16[24,2048]{1,0:T(8,128)(2,1)S(1)}, u32[]{:S(2)}, u32[]{:S(2)}) collective-permute-start(bf16[24,2048]{1,0:T(8,128)(2,1)S(1)} %get-tuple-element.66), channel_id=1, source_target_pairs={{0,8},{2,10},{4,12},{6,14},{8,0},{10,2},{12,4},{14,6},{16,24},{18,... | collective-permute-start | bytes 294920 | tf_op jit(solution)/shard_map/ppermute | solution.py:68
  14.0 1.5 %collective-permute-done.2 = bf16[24,2048]{1,0:T(8,128)(2,1)S(1)} collective-permute-done((bf16[24,2048]{1,0:T(8,128)(2,1)}, bf16[24,2048]{1,0:T(8,128)(2,1)S(1)}, u32[]{:S(2)}, u32[]{:S(2)}) %collective-permute-start.2) | collective-permute-done | bytes 98336 | tf_op jit(solution)/shard_map/ppermute | solution.py:68
  15.5 1.6 %collective-permute-start.4 = (bf16[96,2048]{1,0:T(8,128)(2,1)S(1)}, bf16[96,2048]{1,0:T(8,128)(2,1)S(1)}, u32[]{:S(2)}, u32[]{:S(2)}) collective-permute-start(bf16[96,2048]{1,0:T(8,128)(2,1)S(1)} %get-tuple-element.80), channel_id=1, source_target_pairs={{0,4},{1,3},{2,6},{3,1},{4,0},{5,7},{6,2},{7,5},{8,12},{9,11},{10,... | collective-permute-start | bytes 1179656 | tf_op jit(solution)/shard_map/ppermute | solution.py:75
  17.1 1.5 %collective-permute-start.3 = (bf16[96,2048]{1,0:T(8,128)(2,1)S(1)}, bf16[96,2048]{1,0:T(8,128)(2,1)S(1)}, u32[]{:S(2)}, u32[]{:S(2)}) collective-permute-start(bf16[96,2048]{1,0:T(8,128)(2,1)S(1)} %get-tuple-element.80), channel_id=1, source_target_pairs={{0,2},{1,5},{2,0},{3,7},{4,6},{5,1},{6,4},{7,3},{8,10},{9,13},{10,... | collective-permute-start | bytes 1179656 | tf_op jit(solution)/shard_map/ppermute | solution.py:75
  18.6 2.8 %collective-permute-done.10 = bf16[24,2048]{1,0:T(8,128)(2,1)S(1)} collective-permute-done((bf16[24,2048]{1,0:T(8,128)(2,1)S(1)}, bf16[24,2048]{1,0:T(8,128)(2,1)S(1)}, u32[]{:S(2)}, u32[]{:S(2)}) %collective-permute-start.10) | collective-permute-done | bytes 98336 | tf_op jit(solution)/shard_map/ppermute | solution.py:68
  21.6 1.6 %collective-permute-start.12 = (bf16[96,2048]{1,0:T(8,128)(2,1)S(1)}, bf16[96,2048]{1,0:T(8,128)(2,1)S(1)}, u32[]{:S(2)}, u32[]{:S(2)}) collective-permute-start(bf16[96,2048]{1,0:T(8,128)(2,1)S(1)} %pad_maximum_fusion.1), channel_id=1, source_target_pairs={{0,4},{1,3},{2,6},{3,1},{4,0},{5,7},{6,2},{7,5},{8,12},{9,11},{10,... | collective-permute-start | bytes 1179656 | tf_op jit(solution)/shard_map/ppermute | solution.py:75
  23.1 1.5 %collective-permute-start.11 = (bf16[96,2048]{1,0:T(8,128)(2,1)S(1)}, bf16[96,2048]{1,0:T(8,128)(2,1)S(1)}, u32[]{:S(2)}, u32[]{:S(2)}) collective-permute-start(bf16[96,2048]{1,0:T(8,128)(2,1)S(1)} %pad_maximum_fusion.1), channel_id=1, source_target_pairs={{0,2},{1,5},{2,0},{3,7},{4,6},{5,1},{6,4},{7,3},{8,10},{9,13},{10,... | collective-permute-start | bytes 1179656 | tf_op jit(solution)/shard_map/ppermute | solution.py:75
  24.7 2.9 %collective-permute-done.4 = bf16[96,2048]{1,0:T(8,128)(2,1)S(1)} collective-permute-done((bf16[96,2048]{1,0:T(8,128)(2,1)S(1)}, bf16[96,2048]{1,0:T(8,128)(2,1)S(1)}, u32[]{:S(2)}, u32[]{:S(2)}) %collective-permute-start.4) | collective-permute-done | bytes 393248 | tf_op jit(solution)/shard_map/ppermute | solution.py:75
  27.6 1.5 %collective-permute-start.5 = (bf16[96,2048]{1,0:T(8,128)(2,1)S(1)}, bf16[96,2048]{1,0:T(8,128)(2,1)S(1)}, u32[]{:S(2)}, u32[]{:S(2)}) collective-permute-start(bf16[96,2048]{1,0:T(8,128)(2,1)S(1)} %collective-permute-done.3), channel_id=1, source_target_pairs={{0,4},{1,3},{2,6},{3,1},{4,0},{5,7},{6,2},{7,5},{8,12},{9,11},{10,... | collective-permute-start | bytes 1179656 | tf_op jit(solution)/shard_map/ppermute | solution.py:75
  29.1 6.3 %collective-permute-done.12 = bf16[96,2048]{1,0:T(8,128)(2,1)S(1)} collective-permute-done((bf16[96,2048]{1,0:T(8,128)(2,1)S(1)}, bf16[96,2048]{1,0:T(8,128)(2,1)S(1)}, u32[]{:S(2)}, u32[]{:S(2)}) %collective-permute-start.12) | collective-permute-done | bytes 393248 | tf_op jit(solution)/shard_map/ppermute | solution.py:75
  35.7 1.5 %collective-permute-start.13 = (bf16[96,2048]{1,0:T(8,128)(2,1)S(1)}, bf16[96,2048]{1,0:T(8,128)(2,1)S(1)}, u32[]{:S(2)}, u32[]{:S(2)}) collective-permute-start(bf16[96,2048]{1,0:T(8,128)(2,1)S(1)} %collective-permute-done.11), channel_id=1, source_target_pairs={{0,4},{1,3},{2,6},{3,1},{4,0},{5,7},{6,2},{7,5},{8,12},{9,11},{10,... | collective-permute-start | bytes 1179656 | tf_op jit(solution)/shard_map/ppermute | solution.py:75
  37.2 2.4 %collective-permute-done.5 = bf16[96,2048]{1,0:T(8,128)(2,1)S(1)} collective-permute-done((bf16[96,2048]{1,0:T(8,128)(2,1)S(1)}, bf16[96,2048]{1,0:T(8,128)(2,1)S(1)}, u32[]{:S(2)}, u32[]{:S(2)}) %collective-permute-start.5) | collective-permute-done | bytes 393248 | tf_op jit(solution)/shard_map/ppermute | solution.py:75
  39.7 2.7 %convolution_convert_fusion.5 = bf16[384,1024]{1,0:T(8,128)(2,1)} fusion(bf16[384,2048]{1,0:T(8,128)(2,1)S(1)} %constant_dynamic-update-slice_fusion.4, bf16[1024,2048]{1,0:T(8,128)(2,1)S(1)} %copy-done.14), kind=kOutput, calls=%fused_computation.19 | convolution fusion | flops 1611005952 | bytes 6553600 | tf_op jit(solution)/shard_map/dot_general | solution.py:131
  42.4 1.4 %collective-permute-done.13 = bf16[96,2048]{1,0:T(8,128)(2,1)S(1)} collective-permute-done((bf16[96,2048]{1,0:T(8,128)(2,1)S(1)}, bf16[96,2048]{1,0:T(8,128)(2,1)S(1)}, u32[]{:S(2)}, u32[]{:S(2)}) %collective-permute-start.13) | collective-permute-done | bytes 393248 | tf_op jit(solution)/shard_map/ppermute | solution.py:75
  43.9 2.7 %convolution_convert_fusion.4 = bf16[384,1024]{1,0:T(8,128)(2,1)} fusion(bf16[384,2048]{1,0:T(8,128)(2,1)S(1)} %constant_dynamic-update-slice_fusion.11, bf16[2048,1024]{1,0:T(8,128)(2,1)S(1)} %copy-done.1), kind=kOutput, calls=%fused_computation.18 | convolution fusion | flops 1611005952 | bytes 6553600 | tf_op jit(solution)/shard_map/dot_general | solution.py:134
  46.7 2.4 %collective-permute-done.14 = bf16[384,1024]{1,0:T(8,128)(2,1)S(1)} collective-permute-done((bf16[384,1024]{1,0:T(8,128)(2,1)}, bf16[384,1024]{1,0:T(8,128)(2,1)S(1)}, u32[]{:S(2)}, u32[]{:S(2)}) %collective-permute-start.14) | collective-permute-done | bytes 786464 | tf_op jit(solution)/shard_map/ppermute | solution.py:78
  49.2 2.6 %multiply_convert_fusion = (bf16[384,1024]{1,0:T(8,128)(2,1)S(1)}, bf16[384,1024]{1,0:T(8,128)(2,1)S(1)}) fusion(bf16[384,1024]{1,0:T(8,128)(2,1)} %convolution_convert_fusion.4, f32[1024]{0:T(1024)S(1)} %copy-done.11, bf16[96,1024]{1,0:T(8,128)(2,1)S(1)} %get-tuple-element.70, bf16[96,1024]{1,0:T(8,128)(2,1)S(1)} %get-tuple-element.71, ...), kind=kLoop, calls=%fused_computation.15 | loop fusion | flops 12976128 | bytes 4722688 | tf_op jit(solution)/shard_map/convert_element_type | solution.py:138
  51.8 1.4 %convolution_convert_fusion.3 = bf16[96,2048]{1,0:T(8,128)(2,1)S(1)} fusion(bf16[2048,1024]{1,0:T(8,128)(2,1)S(1)} %copy-done.2, bf16[384,1024]{1,0:T(8,128)(2,1)S(1)} %get-tuple-element.44), kind=kOutput, calls=%fused_computation.6 | convolution fusion | flops 402849792 | bytes 4784128 | tf_op jit(solution)/shard_map/dot_general | solution.py:142
  53.2 1.6 %collective-permute-start.16 = (bf16[96,2048]{1,0:T(8,128)(2,1)S(1)}, bf16[96,2048]{1,0:T(8,128)(2,1)S(1)}, u32[]{:S(2)}, u32[]{:S(2)}) collective-permute-start(bf16[96,2048]{1,0:T(8,128)(2,1)S(1)} %convolution_convert_fusion.3), channel_id=1, source_target_pairs={{0,4},{1,3},{2,6},{3,1},{4,0},{5,7},{6,2},{7,5},{8,12},{9,11},{10,... | collective-permute-start | bytes 1179656 | tf_op jit(solution)/shard_map/ppermute | solution.py:75
  54.8 1.4 %convolution_convert_fusion.2 = bf16[288,2048]{1,0:T(8,128)(2,1)S(1)} fusion(bf16[2048,1024]{1,0:T(8,128)(2,1)S(1)} %copy-done.2, bf16[384,1024]{1,0:T(8,128)(2,1)S(1)} %get-tuple-element.44), kind=kOutput, calls=%fused_computation.4 | convolution fusion | flops 1208549376 | bytes 5963776 | tf_op jit(solution)/shard_map/dot_general | solution.py:142
  56.9 4.2 %collective-permute-done.16 = bf16[96,2048]{1,0:T(8,128)(2,1)S(1)} collective-permute-done((bf16[96,2048]{1,0:T(8,128)(2,1)S(1)}, bf16[96,2048]{1,0:T(8,128)(2,1)S(1)}, u32[]{:S(2)}, u32[]{:S(2)}) %collective-permute-start.16) | collective-permute-done | bytes 393248 | tf_op jit(solution)/shard_map/ppermute | solution.py:75
  61.2 1.1 collective-permute-start.17
  62.3 0.9 convert_reduce_fusion
  63.2 4.4 %convolution_convert_fusion.1 = bf16[1024,2048]{1,0:T(8,128)(2,1)} fusion(bf16[384,1024]{1,0:T(8,128)(2,1)S(1)} %get-tuple-element.37, bf16[384,2048]{1,0:T(8,128)(2,1)S(1)} %copy-done.4), kind=kOutput, calls=%fused_computation.2 | convolution fusion | flops 1612709888 | bytes 6553600 | tf_op jit(solution)/shard_map/dot_general | solution.py:154
  67.6 1.4 %collective-permute-done.17 = bf16[96,2048]{1,0:T(8,128)(2,1)S(1)} collective-permute-done((bf16[96,2048]{1,0:T(8,128)(2,1)S(1)}, bf16[96,2048]{1,0:T(8,128)(2,1)S(1)}, u32[]{:S(2)}, u32[]{:S(2)}) %collective-permute-start.17) | collective-permute-done | bytes 393248 | tf_op jit(solution)/shard_map/ppermute | solution.py:75
  69.2 6.0 %collective-permute-start.19 = (bf16[24,2048]{1,0:T(8,128)(2,1)S(1)}, bf16[24,2048]{1,0:T(8,128)(2,1)S(1)}, u32[]{:S(2)}, u32[]{:S(2)}) collective-permute-start(bf16[24,2048]{1,0:T(8,128)(2,1)S(1)} %get-tuple-element.78), channel_id=1, source_target_pairs={{0,16},{2,18},{4,20},{6,22},{8,24},{10,26},{12,28},{14,30},{16,0},... | collective-permute-start | bytes 294920 | tf_op jit(solution)/shard_map/ppermute | solution.py:68
  75.2 1.5 %collective-permute-start.20 = (bf16[24,2048]{1,0:T(8,128)(2,1)S(1)}, bf16[24,2048]{1,0:T(8,128)(2,1)S(1)}, u32[]{:S(2)}, u32[]{:S(2)}) collective-permute-start(bf16[24,2048]{1,0:T(8,128)(2,1)S(1)} %get-tuple-element.41), channel_id=1, source_target_pairs={{0,24},{2,26},{4,28},{6,30},{8,16},{10,18},{12,20},{14,22},{16,8},... | collective-permute-start | bytes 294920 | tf_op jit(solution)/shard_map/ppermute | solution.py:68
  76.9 5.0 %collective-permute-done.20 = bf16[24,2048]{1,0:T(8,128)(2,1)S(1)} collective-permute-done((bf16[24,2048]{1,0:T(8,128)(2,1)S(1)}, bf16[24,2048]{1,0:T(8,128)(2,1)S(1)}, u32[]{:S(2)}, u32[]{:S(2)}) %collective-permute-start.20) | collective-permute-done | bytes 98336 | tf_op jit(solution)/shard_map/ppermute | solution.py:68
  82.0 1.6 %collective-permute-done.18 = bf16[24,2048]{1,0:T(8,128)(2,1)S(1)} collective-permute-done((bf16[24,2048]{1,0:T(8,128)(2,1)S(1)}, bf16[24,2048]{1,0:T(8,128)(2,1)S(1)}, u32[]{:S(2)}, u32[]{:S(2)}) %collective-permute-start.18) | collective-permute-done | bytes 98336 | tf_op jit(solution)/shard_map/ppermute | solution.py:68
  84.0 1.1 collective-permute-done.21
  85.5 3.0 %collective-permute-start.22 = (bf16[24,2048]{1,0:T(8,128)(2,1)S(1)}, bf16[24,2048]{1,0:T(8,128)(2,1)S(1)}, u32[]{:S(2)}, u32[]{:S(2)}) collective-permute-start(bf16[24,2048]{1,0:T(8,128)(2,1)S(1)} %add_convert_fusion.1), channel_id=1, source_target_pairs={{0,8},{2,10},{4,12},{6,14},{8,0},{10,2},{12,4},{14,6},{16,24},{18,... | collective-permute-start | bytes 294920 | tf_op jit(solution)/shard_map/ppermute | solution.py:68
  88.6 1.8 %collective-permute-start.24 = (bf16[24,2048]{1,0:T(8,128)(2,1)S(1)}, bf16[24,2048]{1,0:T(8,128)(2,1)S(1)}, u32[]{:S(2)}, u32[]{:S(2)}) collective-permute-start(bf16[24,2048]{1,0:T(8,128)(2,1)S(1)} %add_convert_fusion.1), channel_id=1, source_target_pairs={{0,24},{2,26},{4,28},{6,30},{8,16},{10,18},{12,20},{14,22},{16,8},... | collective-permute-start | bytes 294920 | tf_op jit(solution)/shard_map/ppermute | solution.py:68
  90.3 4.4 %convolution_convert_fusion = bf16[2048,1024]{1,0:T(8,128)(2,1)} fusion(bf16[384,2048]{1,0:T(8,128)(2,1)S(1)} %copy-done.10, bf16[384,1024]{1,0:T(8,128)(2,1)S(1)} %get-tuple-element.44), kind=kOutput, calls=%fused_computation.1 | convolution fusion | flops 1612709888 | bytes 6553600 | tf_op jit(solution)/shard_map/dot_general | solution.py:182
  95.5 1.8 %collective-permute-start.29 = (f32[3,2048]{1,0:T(4,128)S(1)}, f32[3,2048]{1,0:T(4,128)S(1)}, u32[]{:S(2)}, u32[]{:S(2)}) collective-permute-start(f32[3,2048]{1,0:T(4,128)S(1)} %add.125), channel_id=1, source_target_pairs={{0,16},{2,18},{4,20},{6,22},{8,24},{10,26},{12,28},{14,30},{16,0},... | collective-permute-start | bytes 73736 | tf_op jit(solution)/shard_map/ppermute | solution.py:68
  98.0 1.4 %collective-permute-start.25 = (bf16[96,2048]{1,0:T(8,128)(2,1)S(1)}, bf16[96,2048]{1,0:T(8,128)(2,1)S(1)}, u32[]{:S(2)}, u32[]{:S(2)}) collective-permute-start(bf16[96,2048]{1,0:T(8,128)(2,1)S(1)} %constant_dynamic-update-slice_fusion.18.refs_0_), channel_id=1, source_target_pairs={{0,2},{1,5},{2,0},{3,7},{4,6},{5,1},{6,4},{7,3},{8,10},{9,13},{10,... | collective-permute-start | bytes 1179656 | tf_op jit(solution)/shard_map/ppermute | solution.py:75
  99.4 1.3 %collective-permute-done.29 = f32[3,2048]{1,0:T(4,128)S(1)} collective-permute-done((f32[3,2048]{1,0:T(4,128)S(1)}, f32[3,2048]{1,0:T(4,128)S(1)}, u32[]{:S(2)}, u32[]{:S(2)}) %collective-permute-start.29) | collective-permute-done | bytes 24608 | tf_op jit(solution)/shard_map/ppermute | solution.py:68
  100.7 1.3 %collective-permute-start.30 = (f32[3,2048]{1,0:T(4,128)S(1)}, f32[3,2048]{1,0:T(4,128)S(1)}, u32[]{:S(2)}, u32[]{:S(2)}) collective-permute-start(f32[3,2048]{1,0:T(4,128)S(1)} %add.126), channel_id=1, source_target_pairs={{0,2},{1,5},{2,0},{3,7},{4,6},{5,1},{6,4},{7,3},{8,10},{9,13},{10,... | collective-permute-start | bytes 73736 | tf_op jit(solution)/shard_map/ppermute | solution.py:75
  102.2 5.4 %collective-permute-done.30 = f32[3,2048]{1,0:T(4,128)S(1)} collective-permute-done((f32[3,2048]{1,0:T(4,128)S(1)}, f32[3,2048]{1,0:T(4,128)S(1)}, u32[]{:S(2)}, u32[]{:S(2)}) %collective-permute-start.30) | collective-permute-done | bytes 24608 | tf_op jit(solution)/shard_map/ppermute | solution.py:75
  107.6 1.2 %collective-permute-done.26.refs_2_ = bf16[96,2048]{1,0:T(8,128)(2,1)S(1)} collective-permute-done((bf16[96,2048]{1,0:T(8,128)(2,1)S(1)}, bf16[96,2048]{1,0:T(8,128)(2,1)S(1)}, u32[]{:S(2)}, u32[]{:S(2)}) %collective-permute-start.26) | collective-permute-done | bytes 393248 | tf_op jit(solution)/shard_map/ppermute | solution.py:75
  109.3 1.5 %collective-permute-start.27 = (bf16[96,2048]{1,0:T(8,128)(2,1)S(1)}, bf16[96,2048]{1,0:T(8,128)(2,1)S(1)}, u32[]{:S(2)}, u32[]{:S(2)}) collective-permute-start(bf16[96,2048]{1,0:T(8,128)(2,1)S(1)} %collective-permute-done.25.refs_1_), channel_id=1, source_target_pairs={{0,4},{1,3},{2,6},{3,1},{4,0},{5,7},{6,2},{7,5},{8,12},{9,11},{10,... | collective-permute-start | bytes 1179656 | tf_op jit(solution)/shard_map/ppermute | solution.py:75
  110.8 1.9 %collective-permute-done.31 = f32[3,2048]{1,0:T(4,128)S(1)} collective-permute-done((f32[3,2048]{1,0:T(4,128)S(1)}, f32[3,2048]{1,0:T(4,128)S(1)}, u32[]{:S(2)}, u32[]{:S(2)}) %collective-permute-start.31) | collective-permute-done | bytes 24608 | tf_op jit(solution)/shard_map/ppermute | solution.py:75
  114.1 3.0 %collective-permute-done.27.refs_3_ = bf16[96,2048]{1,0:T(8,128)(2,1)S(1)} collective-permute-done((bf16[96,2048]{1,0:T(8,128)(2,1)S(1)}, bf16[96,2048]{1,0:T(8,128)(2,1)S(1)}, u32[]{:S(2)}, u32[]{:S(2)}) %collective-permute-start.27) | collective-permute-done | bytes 393248 | tf_op jit(solution)/shard_map/ppermute | solution.py:75
  117.1 2.0 %place.1 = f32[256,2048]{1,0:T(8,128)} custom-call(bf16[96,2048]{1,0:T(8,128)(2,1)S(1)} %constant_dynamic-update-slice_fusion.18.refs_0_, bf16[96,2048]{1,0:T(8,128)(2,1)S(1)} %collective-permute-done.25.refs_1_, bf16[96,2048]{1,0:T(8,128)(2,1)S(1)} %collective-permute-done.26.refs_2_, bf16[96,2048]{1,0:T(8,128)(2,1)S(1)} %collective-permute-done.27.refs_3_, ...), custom_call_target="tpu_custom_call" | custom-call | flops 402653184 | bytes 1572864 | tf_op jit(solution)/shard_map/place/pallas_call | solution.py:52
  (110 shorter events, 7.7 us)
Async XLA Ops:
  0.6 5.7 %copy-start = (bf16[256,2048]{1,0:T(8,128)(2,1)S(1)}, bf16[256,2048]{1,0:T(8,128)(2,1)}, u32[]{:S(2)}) copy-start(bf16[256,2048]{1,0:T(8,128)(2,1)} %param.13) | copy-start | bytes 3145732
  0.6 8.7 %copy-start.7 = (f32[2048]{0:T(1024)S(1)}, f32[2048]{0:T(1024)}, u32[]{:S(2)}) copy-start(f32[2048]{0:T(1024)} %param.14) | copy-start | bytes 24580
  0.7 8.7 %copy-start.8 = (f32[2048]{0:T(1024)S(1)}, f32[2048]{0:T(1024)}, u32[]{:S(2)}) copy-start(f32[2048]{0:T(1024)} %param.15) | copy-start | bytes 24580
  0.7 13.3 %collective-permute-start.1 = (bf16[24,2048]{1,0:T(8,128)(2,1)}, bf16[24,2048]{1,0:T(8,128)(2,1)S(1)}, u32[]{:S(2)}, u32[]{:S(2)}) collective-permute-start(bf16[24,2048]{1,0:T(8,128)(2,1)} %param.19), channel_id=1, source_target_pairs={{0,16},{2,18},{4,20},{6,22},{8,24},{10,26},{12,28},{14,30},{16,0},... | collective-permute-start | bytes 294920 | tf_op jit(solution)/shard_map/ppermute | solution.py:68
  4.8 8.6 %collective-permute-start = (bf16[24,2048]{1,0:T(8,128)(2,1)}, bf16[24,2048]{1,0:T(8,128)(2,1)S(1)}, u32[]{:S(2)}, u32[]{:S(2)}) collective-permute-start(bf16[24,2048]{1,0:T(8,128)(2,1)} %param.19), channel_id=1, source_target_pairs={{0,8},{2,10},{4,12},{6,14},{8,0},{10,2},{12,4},{14,6},{16,24},{18,... | collective-permute-start | bytes 294920 | tf_op jit(solution)/shard_map/ppermute | solution.py:68
  7.7 1.7 %collective-permute-start.7 = (f32[2,24]{1,0:T(2,128)S(1)}, f32[2,24]{1,0:T(2,128)S(1)}, u32[]{:S(2)}, u32[]{:S(2)}) collective-permute-start(f32[2,24]{1,0:T(2,128)S(1)} %pad_maximum_fusion.3), channel_id=1, source_target_pairs={{0,1},{1,0},{2,3},{3,2},{4,5},{5,4},{6,7},{7,6},{8,9},{9,8},{10,11... | collective-permute-start | bytes 584 | tf_op jit(solution)/shard_map/ppermute | solution.py:78
  7.8 7.8 %collective-permute-start.2 = (bf16[24,2048]{1,0:T(8,128)(2,1)}, bf16[24,2048]{1,0:T(8,128)(2,1)S(1)}, u32[]{:S(2)}, u32[]{:S(2)}) collective-permute-start(bf16[24,2048]{1,0:T(8,128)(2,1)} %param.19), channel_id=1, source_target_pairs={{0,24},{2,26},{4,28},{6,30},{8,16},{10,18},{12,20},{14,22},{16,8},... | collective-permute-start | bytes 294920 | tf_op jit(solution)/shard_map/ppermute | solution.py:68
  9.5 12.0 %collective-permute-start.9 = (bf16[24,2048]{1,0:T(8,128)(2,1)S(1)}, bf16[24,2048]{1,0:T(8,128)(2,1)S(1)}, u32[]{:S(2)}, u32[]{:S(2)}) collective-permute-start(bf16[24,2048]{1,0:T(8,128)(2,1)S(1)} %get-tuple-element.66), channel_id=1, source_target_pairs={{0,16},{2,18},{4,20},{6,22},{8,24},{10,26},{12,28},{14,30},{16,0},... | collective-permute-start | bytes 294920 | tf_op jit(solution)/shard_map/ppermute | solution.py:68
  10.9 10.6 %collective-permute-start.8 = (bf16[24,2048]{1,0:T(8,128)(2,1)S(1)}, bf16[24,2048]{1,0:T(8,128)(2,1)S(1)}, u32[]{:S(2)}, u32[]{:S(2)}) collective-permute-start(bf16[24,2048]{1,0:T(8,128)(2,1)S(1)} %get-tuple-element.66), channel_id=1, source_target_pairs={{0,8},{2,10},{4,12},{6,14},{8,0},{10,2},{12,4},{14,6},{16,24},{18,... | collective-permute-start | bytes 294920 | tf_op jit(solution)/shard_map/ppermute | solution.py:68
  13.4 8.0 %collective-permute-start.10 = (bf16[24,2048]{1,0:T(8,128)(2,1)S(1)}, bf16[24,2048]{1,0:T(8,128)(2,1)S(1)}, u32[]{:S(2)}, u32[]{:S(2)}) collective-permute-start(bf16[24,2048]{1,0:T(8,128)(2,1)S(1)} %get-tuple-element.66), channel_id=1, source_target_pairs={{0,24},{2,26},{4,28},{6,30},{8,16},{10,18},{12,20},{14,22},{16,8},... | collective-permute-start | bytes 294920 | tf_op jit(solution)/shard_map/ppermute | solution.py:68
  15.5 12.0 %collective-permute-start.4 = (bf16[96,2048]{1,0:T(8,128)(2,1)S(1)}, bf16[96,2048]{1,0:T(8,128)(2,1)S(1)}, u32[]{:S(2)}, u32[]{:S(2)}) collective-permute-start(bf16[96,2048]{1,0:T(8,128)(2,1)S(1)} %get-tuple-element.80), channel_id=1, source_target_pairs={{0,4},{1,3},{2,6},{3,1},{4,0},{5,7},{6,2},{7,5},{8,12},{9,11},{10,... | collective-permute-start | bytes 1179656 | tf_op jit(solution)/shard_map/ppermute | solution.py:75
  17.1 10.4 %collective-permute-start.3 = (bf16[96,2048]{1,0:T(8,128)(2,1)S(1)}, bf16[96,2048]{1,0:T(8,128)(2,1)S(1)}, u32[]{:S(2)}, u32[]{:S(2)}) collective-permute-start(bf16[96,2048]{1,0:T(8,128)(2,1)S(1)} %get-tuple-element.80), channel_id=1, source_target_pairs={{0,2},{1,5},{2,0},{3,7},{4,6},{5,1},{6,4},{7,3},{8,10},{9,13},{10,... | collective-permute-start | bytes 1179656 | tf_op jit(solution)/shard_map/ppermute | solution.py:75
  21.6 13.9 %collective-permute-start.12 = (bf16[96,2048]{1,0:T(8,128)(2,1)S(1)}, bf16[96,2048]{1,0:T(8,128)(2,1)S(1)}, u32[]{:S(2)}, u32[]{:S(2)}) collective-permute-start(bf16[96,2048]{1,0:T(8,128)(2,1)S(1)} %pad_maximum_fusion.1), channel_id=1, source_target_pairs={{0,4},{1,3},{2,6},{3,1},{4,0},{5,7},{6,2},{7,5},{8,12},{9,11},{10,... | collective-permute-start | bytes 1179656 | tf_op jit(solution)/shard_map/ppermute | solution.py:75
  23.1 12.5 %collective-permute-start.11 = (bf16[96,2048]{1,0:T(8,128)(2,1)S(1)}, bf16[96,2048]{1,0:T(8,128)(2,1)S(1)}, u32[]{:S(2)}, u32[]{:S(2)}) collective-permute-start(bf16[96,2048]{1,0:T(8,128)(2,1)S(1)} %pad_maximum_fusion.1), channel_id=1, source_target_pairs={{0,2},{1,5},{2,0},{3,7},{4,6},{5,1},{6,4},{7,3},{8,10},{9,13},{10,... | collective-permute-start | bytes 1179656 | tf_op jit(solution)/shard_map/ppermute | solution.py:75
  24.6 15.0 %copy-start.14 = (bf16[1024,2048]{1,0:T(8,128)(2,1)S(1)}, bf16[1024,2048]{1,0:T(8,128)(2,1)}, u32[]{:S(2)}) copy-start(bf16[1024,2048]{1,0:T(8,128)(2,1)} %param.18) | copy-start | bytes 12582916
  27.6 12.1 %collective-permute-start.5 = (bf16[96,2048]{1,0:T(8,128)(2,1)S(1)}, bf16[96,2048]{1,0:T(8,128)(2,1)S(1)}, u32[]{:S(2)}, u32[]{:S(2)}) collective-permute-start(bf16[96,2048]{1,0:T(8,128)(2,1)S(1)} %collective-permute-done.3), channel_id=1, source_target_pairs={{0,4},{1,3},{2,6},{3,1},{4,0},{5,7},{6,2},{7,5},{8,12},{9,11},{10,... | collective-permute-start | bytes 1179656 | tf_op jit(solution)/shard_map/ppermute | solution.py:75
  35.7 8.2 %collective-permute-start.13 = (bf16[96,2048]{1,0:T(8,128)(2,1)S(1)}, bf16[96,2048]{1,0:T(8,128)(2,1)S(1)}, u32[]{:S(2)}, u32[]{:S(2)}) collective-permute-start(bf16[96,2048]{1,0:T(8,128)(2,1)S(1)} %collective-permute-done.11), channel_id=1, source_target_pairs={{0,4},{1,3},{2,6},{3,1},{4,0},{5,7},{6,2},{7,5},{8,12},{9,11},{10,... | collective-permute-start | bytes 1179656 | tf_op jit(solution)/shard_map/ppermute | solution.py:75
  39.7 2.7 %copy-start.3 = (bf16[384,2048]{1,0:T(8,128)(2,1)}, bf16[384,2048]{1,0:T(8,128)(2,1)S(1)}, u32[]{:S(2)}) copy-start(bf16[384,2048]{1,0:T(8,128)(2,1)S(1)} %constant_dynamic-update-slice_fusion.4) | copy-start | bytes 4718596
  39.7 4.2 %copy-start.1 = (bf16[2048,1024]{1,0:T(8,128)(2,1)S(1)}, bf16[2048,1024]{1,0:T(8,128)(2,1)}, u32[]{:S(2)}) copy-start(bf16[2048,1024]{1,0:T(8,128)(2,1)} %param.16) | copy-start | bytes 12582916
  42.4 4.2 %collective-permute-start.6 = (bf16[384,1024]{1,0:T(8,128)(2,1)}, bf16[384,1024]{1,0:T(8,128)(2,1)S(1)}, u32[]{:S(2)}, u32[]{:S(2)}) collective-permute-start(bf16[384,1024]{1,0:T(8,128)(2,1)} %convolution_convert_fusion.5), channel_id=1, source_target_pairs={{0,1},{1,0},{2,3},{3,2},{4,5},{5,4},{6,7},{7,6},{8,9},{9,8},{10,11... | collective-permute-start | bytes 2359304 | tf_op jit(solution)/shard_map/ppermute | solution.py:78
  43.9 2.7 %copy-start.9 = (bf16[384,2048]{1,0:T(8,128)(2,1)}, bf16[384,2048]{1,0:T(8,128)(2,1)S(1)}, u32[]{:S(2)}) copy-start(bf16[384,2048]{1,0:T(8,128)(2,1)S(1)} %constant_dynamic-update-slice_fusion.11) | copy-start | bytes 4718596
  43.9 2.7 %copy-start.12 = (s32[24]{0:T(128)S(1)}, s32[24]{0:T(128)}, u32[]{:S(2)}) copy-start(s32[24]{0:T(128)} %param.12) | copy-start | bytes 292
  46.6 2.5 %collective-permute-start.14 = (bf16[384,1024]{1,0:T(8,128)(2,1)}, bf16[384,1024]{1,0:T(8,128)(2,1)S(1)}, u32[]{:S(2)}, u32[]{:S(2)}) collective-permute-start(bf16[384,1024]{1,0:T(8,128)(2,1)} %convolution_convert_fusion.4), channel_id=1, source_target_pairs={{0,1},{1,0},{2,3},{3,2},{4,5},{5,4},{6,7},{7,6},{8,9},{9,8},{10,11... | collective-permute-start | bytes 2359304 | tf_op jit(solution)/shard_map/ppermute | solution.py:78
  46.6 2.5 %copy-start.11 = (f32[1024]{0:T(1024)S(1)}, f32[1024]{0:T(1024)}, u32[]{:S(2)}) copy-start(f32[1024]{0:T(1024)} %param.17) | copy-start | bytes 12292
  49.2 2.7 %copy-start.2 = (bf16[2048,1024]{1,0:T(8,128)(2,1)S(1)}, bf16[2048,1024]{1,0:T(8,128)(2,1)}, u32[]{:S(2)}) copy-start(bf16[2048,1024]{1,0:T(8,128)(2,1)} %param.16) | copy-start | bytes 12582916
  53.2 7.8 %collective-permute-start.16 = (bf16[96,2048]{1,0:T(8,128)(2,1)S(1)}, bf16[96,2048]{1,0:T(8,128)(2,1)S(1)}, u32[]{:S(2)}, u32[]{:S(2)}) collective-permute-start(bf16[96,2048]{1,0:T(8,128)(2,1)S(1)} %convolution_convert_fusion.3), channel_id=1, source_target_pairs={{0,4},{1,3},{2,6},{3,1},{4,0},{5,7},{6,2},{7,5},{8,12},{9,11},{10,... | collective-permute-start | bytes 1179656 | tf_op jit(solution)/shard_map/ppermute | solution.py:75
  56.3 6.1 %copy-start.4 = (bf16[384,2048]{1,0:T(8,128)(2,1)S(1)}, bf16[384,2048]{1,0:T(8,128)(2,1)}, u32[]{:S(2)}) copy-start(bf16[384,2048]{1,0:T(8,128)(2,1)} %copy-done.3) | copy-start | bytes 4718596
  56.3 12.7 %collective-permute-start.15 = (bf16[96,2048]{1,0:T(8,128)(2,1)S(1)}, bf16[96,2048]{1,0:T(8,128)(2,1)S(1)}, u32[]{:S(2)}, u32[]{:S(2)}) collective-permute-start(bf16[96,2048]{1,0:T(8,128)(2,1)S(1)} %slice.98), channel_id=1, source_target_pairs={{0,4},{1,3},{2,6},{3,1},{4,0},{5,7},{6,2},{7,5},{8,12},{9,11},{10,... | collective-permute-start | bytes 1179656 | tf_op jit(solution)/shard_map/ppermute | solution.py:75
  61.2 7.8 %collective-permute-start.17 = (bf16[96,2048]{1,0:T(8,128)(2,1)S(1)}, bf16[96,2048]{1,0:T(8,128)(2,1)S(1)}, u32[]{:S(2)}, u32[]{:S(2)}) collective-permute-start(bf16[96,2048]{1,0:T(8,128)(2,1)S(1)} %add_convert_fusion), channel_id=1, source_target_pairs={{0,2},{1,5},{2,0},{3,7},{4,6},{5,1},{6,4},{7,3},{8,10},{9,13},{10,... | collective-permute-start | bytes 1179656 | tf_op jit(solution)/shard_map/ppermute | solution.py:75
  67.6 17.5 %copy-start.5 = (bf16[24,2048]{1,0:T(8,128)(2,1)S(1)}, bf16[24,2048]{1,0:T(8,128)(2,1)}, u32[]{:S(2)}) copy-start(bf16[24,2048]{1,0:T(8,128)(2,1)} %param.19) | copy-start | bytes 294916
  69.2 12.8 %collective-permute-start.19 = (bf16[24,2048]{1,0:T(8,128)(2,1)S(1)}, bf16[24,2048]{1,0:T(8,128)(2,1)S(1)}, u32[]{:S(2)}, u32[]{:S(2)}) collective-permute-start(bf16[24,2048]{1,0:T(8,128)(2,1)S(1)} %get-tuple-element.78), channel_id=1, source_target_pairs={{0,16},{2,18},{4,20},{6,22},{8,24},{10,26},{12,28},{14,30},{16,0},... | collective-permute-start | bytes 294920 | tf_op jit(solution)/shard_map/ppermute | solution.py:68
  75.2 8.4 %collective-permute-start.18 = (bf16[24,2048]{1,0:T(8,128)(2,1)S(1)}, bf16[24,2048]{1,0:T(8,128)(2,1)S(1)}, u32[]{:S(2)}, u32[]{:S(2)}) collective-permute-start(bf16[24,2048]{1,0:T(8,128)(2,1)S(1)} %get-tuple-element.79), channel_id=1, source_target_pairs={{0,8},{2,10},{4,12},{6,14},{8,0},{10,2},{12,4},{14,6},{16,24},{18,... | collective-permute-start | bytes 294920 | tf_op jit(solution)/shard_map/ppermute | solution.py:68
  75.2 6.8 %collective-permute-start.20 = (bf16[24,2048]{1,0:T(8,128)(2,1)S(1)}, bf16[24,2048]{1,0:T(8,128)(2,1)S(1)}, u32[]{:S(2)}, u32[]{:S(2)}) collective-permute-start(bf16[24,2048]{1,0:T(8,128)(2,1)S(1)} %get-tuple-element.41), channel_id=1, source_target_pairs={{0,24},{2,26},{4,28},{6,30},{8,16},{10,18},{12,20},{14,22},{16,8},... | collective-permute-start | bytes 294920 | tf_op jit(solution)/shard_map/ppermute | solution.py:68
  76.9 13.4 %copy-start.10 = (bf16[384,2048]{1,0:T(8,128)(2,1)S(1)}, bf16[384,2048]{1,0:T(8,128)(2,1)}, u32[]{:S(2)}) copy-start(bf16[384,2048]{1,0:T(8,128)(2,1)} %copy-done.9) | copy-start | bytes 4718596
  83.8 1.2 %collective-permute-start.21 = (f32[2,24]{1,0:T(2,128)S(1)}, f32[2,24]{1,0:T(2,128)S(1)}, u32[]{:S(2)}, u32[]{:S(2)}) collective-permute-start(f32[2,24]{1,0:T(2,128)S(1)} %pad_maximum_fusion.4), channel_id=1, source_target_pairs={{0,1},{1,0},{2,3},{3,2},{4,5},{5,4},{6,7},{7,6},{8,9},{9,8},{10,11... | collective-permute-start | bytes 584 | tf_op jit(solution)/shard_map/ppermute | solution.py:78
  85.2 9.6 %copy-start.6 = (bf16[24,2048]{1,0:T(8,128)(2,1)}, bf16[24,2048]{1,0:T(8,128)(2,1)S(1)}, u32[]{:S(2)}) copy-start(bf16[24,2048]{1,0:T(8,128)(2,1)S(1)} %add_convert_fusion.1) | copy-start | bytes 294916
  85.2 12.1 %collective-permute-start.23 = (bf16[24,2048]{1,0:T(8,128)(2,1)S(1)}, bf16[24,2048]{1,0:T(8,128)(2,1)S(1)}, u32[]{:S(2)}, u32[]{:S(2)}) collective-permute-start(bf16[24,2048]{1,0:T(8,128)(2,1)S(1)} %add_convert_fusion.1), channel_id=1, source_target_pairs={{0,16},{2,18},{4,20},{6,22},{8,24},{10,26},{12,28},{14,30},{16,0},... | collective-permute-start | bytes 294920 | tf_op jit(solution)/shard_map/ppermute | solution.py:68
  85.5 11.8 %collective-permute-start.22 = (bf16[24,2048]{1,0:T(8,128)(2,1)S(1)}, bf16[24,2048]{1,0:T(8,128)(2,1)S(1)}, u32[]{:S(2)}, u32[]{:S(2)}) collective-permute-start(bf16[24,2048]{1,0:T(8,128)(2,1)S(1)} %add_convert_fusion.1), channel_id=1, source_target_pairs={{0,8},{2,10},{4,12},{6,14},{8,0},{10,2},{12,4},{14,6},{16,24},{18,... | collective-permute-start | bytes 294920 | tf_op jit(solution)/shard_map/ppermute | solution.py:68
  88.5 10.9 %copy-start.13 = (s32[4]{0:T(128)S(1)}, s32[4]{0:T(128)}, u32[]{:S(2)}) copy-start(s32[4]{0:T(128)} %constant.38.clone) | copy-start | bytes 52
  88.5 7.0 %collective-permute-start.28 = (f32[3,2048]{1,0:T(4,128)S(1)}, f32[3,2048]{1,0:T(4,128)S(1)}, u32[]{:S(2)}, u32[]{:S(2)}) collective-permute-start(f32[3,2048]{1,0:T(4,128)S(1)} %pad_maximum_fusion.2), channel_id=1, source_target_pairs={{0,8},{2,10},{4,12},{6,14},{8,0},{10,2},{12,4},{14,6},{16,24},{18,... | collective-permute-start | bytes 73736 | tf_op jit(solution)/shard_map/ppermute | solution.py:68
  88.6 8.7 %collective-permute-start.24 = (bf16[24,2048]{1,0:T(8,128)(2,1)S(1)}, bf16[24,2048]{1,0:T(8,128)(2,1)S(1)}, u32[]{:S(2)}, u32[]{:S(2)}) collective-permute-start(bf16[24,2048]{1,0:T(8,128)(2,1)S(1)} %add_convert_fusion.1), channel_id=1, source_target_pairs={{0,24},{2,26},{4,28},{6,30},{8,16},{10,18},{12,20},{14,22},{16,8},... | collective-permute-start | bytes 294920 | tf_op jit(solution)/shard_map/ppermute | solution.py:68
  95.5 5.2 %collective-permute-start.29 = (f32[3,2048]{1,0:T(4,128)S(1)}, f32[3,2048]{1,0:T(4,128)S(1)}, u32[]{:S(2)}, u32[]{:S(2)}) collective-permute-start(f32[3,2048]{1,0:T(4,128)S(1)} %add.125), channel_id=1, source_target_pairs={{0,16},{2,18},{4,20},{6,22},{8,24},{10,26},{12,28},{14,30},{16,0},... | collective-permute-start | bytes 73736 | tf_op jit(solution)/shard_map/ppermute | solution.py:68
  97.4 11.4 %collective-permute-start.26 = (bf16[96,2048]{1,0:T(8,128)(2,1)S(1)}, bf16[96,2048]{1,0:T(8,128)(2,1)S(1)}, u32[]{:S(2)}, u32[]{:S(2)}) collective-permute-start(bf16[96,2048]{1,0:T(8,128)(2,1)S(1)} %constant_dynamic-update-slice_fusion.18.refs_0_), channel_id=1, source_target_pairs={{0,4},{1,3},{2,6},{3,1},{4,0},{5,7},{6,2},{7,5},{8,12},{9,11},{10,... | collective-permute-start | bytes 1179656 | tf_op jit(solution)/shard_map/ppermute | solution.py:75
  98.0 10.8 %collective-permute-start.25 = (bf16[96,2048]{1,0:T(8,128)(2,1)S(1)}, bf16[96,2048]{1,0:T(8,128)(2,1)S(1)}, u32[]{:S(2)}, u32[]{:S(2)}) collective-permute-start(bf16[96,2048]{1,0:T(8,128)(2,1)S(1)} %constant_dynamic-update-slice_fusion.18.refs_0_), channel_id=1, source_target_pairs={{0,2},{1,5},{2,0},{3,7},{4,6},{5,1},{6,4},{7,3},{8,10},{9,13},{10,... | collective-permute-start | bytes 1179656 | tf_op jit(solution)/shard_map/ppermute | solution.py:75
  100.7 6.8 %collective-permute-start.30 = (f32[3,2048]{1,0:T(4,128)S(1)}, f32[3,2048]{1,0:T(4,128)S(1)}, u32[]{:S(2)}, u32[]{:S(2)}) collective-permute-start(f32[3,2048]{1,0:T(4,128)S(1)} %add.126), channel_id=1, source_target_pairs={{0,2},{1,5},{2,0},{3,7},{4,6},{5,1},{6,4},{7,3},{8,10},{9,13},{10,... | collective-permute-start | bytes 73736 | tf_op jit(solution)/shard_map/ppermute | solution.py:75
  108.8 3.9 %collective-permute-start.31 = (f32[3,2048]{1,0:T(4,128)S(1)}, f32[3,2048]{1,0:T(4,128)S(1)}, u32[]{:S(2)}, u32[]{:S(2)}) collective-permute-start(f32[3,2048]{1,0:T(4,128)S(1)} %add.127), channel_id=1, source_target_pairs={{0,4},{1,3},{2,6},{3,1},{4,0},{5,7},{6,2},{7,5},{8,12},{9,11},{10,... | collective-permute-start | bytes 73736 | tf_op jit(solution)/shard_map/ppermute | solution.py:75
  109.3 7.8 %collective-permute-start.27 = (bf16[96,2048]{1,0:T(8,128)(2,1)S(1)}, bf16[96,2048]{1,0:T(8,128)(2,1)S(1)}, u32[]{:S(2)}, u32[]{:S(2)}) collective-permute-start(bf16[96,2048]{1,0:T(8,128)(2,1)S(1)} %collective-permute-done.25.refs_1_), channel_id=1, source_target_pairs={{0,4},{1,3},{2,6},{3,1},{4,0},{5,7},{6,2},{7,5},{8,12},{9,11},{10,... | collective-permute-start | bytes 1179656 | tf_op jit(solution)/shard_map/ppermute | solution.py:75
